TPU v7x, 32 devices: a whole 2x2x4 slice. The times are simulated.
32 devices in a mesh: groups: 2 (over y), tile: 4 (over x, core), cuts: 4 (over z).
Axes of the slice: x: 2, y: 2, z: 4, core: 2. Of those that a mesh axis runs over, the one named last changes fastest.
Arguments:
- trade: bfloat16 [16, 4, 256, 8192], P(('groups', 'cuts'), 'tile'), parts along dimension 0, may hold values from -6 to 6
- factor: bfloat16 [32768, 256], P(('groups', 'tile', 'cuts')), parts along dimension 0, may hold values from -0.375 to 0.375
- scales: float32 [16, 256], P(('groups', 'cuts')), parts along dimension 0, may hold values from 0.1 to 1.9
- core: float32 [512, 256], P('groups'), parts along dimension 0, may hold values from -4 to 4
Outputs:
- grad_factor: float32 [32768, 256], P(('groups', 'tile', 'cuts')), parts along dimension 0
- grad_window: float32 [1024, 256], P(('groups', 'cuts')), parts along dimension 0
- grad_core: float32 [512, 256], P('groups'), parts along dimension 0
- grad_scales: float32 [16, 256], P(('groups', 'cuts')), parts along dimension 0
There are 2 independent parts, one for each index of `groups`. A program takes and returns all parts, laid end to end along the dimension named above; each array names one. Nothing has to cross between parts.
All inputs are finite; a program needn't handle non-finite values.
Results may differ from a plain program's by a relative error of at most 0.00055.
Values may be sent and summed in bfloat16 or wider, within the bound.
No kernel may reach another device: no remote copies, remote signals or barrier semaphores. Data moves between devices by JAX's collectives and lax.ppermute only.
A program may use at most 128 MiB of HBM per device.

v0:
```python
import math

import jax
import jax.numpy as jnp
from jax import lax
from jax.sharding import PartitionSpec as P

P_SIZE = 256


def swapped(value, axis, distance):
    mask = 2**distance
    pairs = [(source, source ^ mask) for source in range(lax.axis_size(axis))]
    return lax.ppermute(value, axis, pairs)


def from_root(block, axis, source):
    block = jnp.where(lax.axis_index(axis) == source, block, jnp.zeros_like(block))
    return lax.psum(block, axis)


def body(trade, factor, scales, core):
    n_cuts = lax.axis_size("cuts")
    band_index = lax.axis_index("tile") % 2
    months = trade.shape[0]
    rows_band = trade.shape[2]
    window_size = 2 * rows_band
    highest = lax.Precision.HIGHEST
    own_block = lax.all_gather(factor, "cuts", axis=0, tiled=True)
    block = own_block.shape[0]
    partner_block = swapped(own_block, "tile", 0)
    first_block = jnp.where(band_index == 0, own_block, partner_block)
    second_block = jnp.where(band_index == 0, partner_block, own_block)
    column_factor = jnp.concatenate([first_block, second_block], 0)
    window_block = from_root(own_block, "tile", 0)
    window_rows = lax.dynamic_slice_in_dim(window_block, band_index * rows_band, rows_band, 0)
    window32 = window_rows.astype(jnp.float32)
    coef = 1.0 / math.sqrt(months * n_cuts * window_size)
    acc_columns = jnp.zeros((2 * block, P_SIZE), jnp.float32)
    acc_window = jnp.zeros((rows_band, P_SIZE), jnp.float32)
    acc_core = jnp.zeros((P_SIZE, P_SIZE), jnp.float32)
    diag_terms = []
    for month in range(months):
        diag_k = scales[month]
        inner = diag_k[:, None] * core * diag_k[None, :]
        mapped = jnp.dot(window32, inner, precision=highest).astype(jnp.bfloat16)
        model = lax.dot_general(
            mapped, column_factor, (((1,), (1,)), ((), ())), preferred_element_type=jnp.float32
        )
        residual = (trade[month, 0].astype(jnp.float32) - model).astype(jnp.bfloat16)
        acc_columns = acc_columns + lax.dot_general(
            residual, mapped, (((0,), (0,)), ((), ())), preferred_element_type=jnp.float32
        )
        projected = jnp.dot(residual, column_factor, preferred_element_type=jnp.float32)
        acc_window = acc_window + jnp.dot(projected, inner.T, precision=highest)
        gram = jnp.dot(window32.T, projected, precision=highest)
        acc_core = acc_core + diag_k[:, None] * gram * diag_k[None, :]
        weighted = gram * core
        diag_terms.append(
            jnp.dot(weighted, diag_k, precision=highest)
            + jnp.dot(weighted.T, diag_k, precision=highest)
        )
    diag_stack = jnp.stack(diag_terms, 0)
    halves = acc_columns.reshape(2, block, P_SIZE)
    mine = jnp.where(band_index == 0, halves[0], halves[1])
    other = jnp.where(band_index == 0, halves[1], halves[0])
    received = swapped(other, "tile", 0)
    grad_factor = lax.psum_scatter(mine + received, "cuts", scatter_dimension=0, tiled=True)
    padded = lax.dynamic_update_slice_in_dim(
        jnp.zeros((window_size, P_SIZE), jnp.float32), acc_window, band_index * rows_band, 0
    )
    window_part = lax.psum_scatter(padded, "cuts", scatter_dimension=0, tiled=True)
    window_total = lax.psum(window_part, "tile")
    core_total = lax.psum(acc_core, ("tile", "cuts"))
    diag_total = lax.psum(diag_stack, "tile")
    return (-coef * grad_factor, -coef * window_total, -coef * core_total, -coef * diag_total)


def solution(mesh):
    return jax.shard_map(
        body,
        mesh=mesh,
        in_specs=(
            P(("groups", "cuts"), "tile", None, None),
            P(("groups", "tile", "cuts"), None),
            P(("groups", "cuts"), None),
            P("groups", None),
        ),
        out_specs=(
            P(("groups", "tile", "cuts"), None),
            P(("groups", "cuts"), None),
            P("groups", None),
            P(("groups", "cuts"), None),
        ),
        check_vma=False,
    )
```

profile of v0, /device:TPU:0, one launch (start us, length us, event | category | flops | bytes accessed | tf_op | source)
XLA Modules:
  0.0 385.2 jit_solution(4281532647967686441)
XLA Ops:
  7.2 0.7 all-gather.2.cloned.1.call-update
  7.9 50.3 %all-gather.2.cloned.1.call-done = bf16[4096,256]{1,0:T(8,128)(2,1)} async-done(((bf16[1024,256]{1,0:T(8,128)(2,1)}), bf16[4096,256]{1,0:T(8,128)(2,1)}) %all-gather.2.cloned.1.call-update) | async-done | bytes 2097168 | tf_op jit(solution)/shard_map/all_gather | solution.py:29
  58.2 4.5 %collective-permute-done = bf16[4096,256]{1,0:T(8,128)(2,1)} collective-permute-done((bf16[4096,256]{1,0:T(8,128)(2,1)}, bf16[4096,256]{1,0:T(8,128)(2,1)}, u32[]{:S(2)}, u32[]{:S(2)}) %collective-permute-start) | collective-permute-done | bytes 2097184 | tf_op jit(solution)/shard_map/ppermute | solution.py:14
  62.7 4.6 %broadcast_select_fusion.2 = (bf16[4096,256]{1,0:T(8,128)(2,1)S(1)}, bf16[4096,256]{1,0:T(8,128)(2,1)}, bf16[4096,256]{1,0:T(8,128)(2,1)}) fusion(bf16[4096,256]{1,0:T(8,128)(2,1)} %all-gather.2.cloned.1.call-done, bf16[4096,256]{1,0:T(8,128)(2,1)} %collective-permute-done, pred[]{:T(512)S(6)} %eq.6, pred[]{:T(512)S(6)} %eq.12), kind=kLoop, calls=%fused_computation.10 | loop fusion | flops 3145728 | bytes 10485762 | tf_op jit(solution)/shard_map/jit(_where)/select_n | solution.py:32
  67.5 50.2 %all-reduce.4.cloned.1.call-done = bf16[4096,256]{1,0:T(8,128)(2,1)} async-done(((bf16[4096,256]{1,0:T(8,128)(2,1)}), bf16[4096,256]{1,0:T(8,128)(2,1)}) %all-reduce.4.cloned.1.call-update) | async-done | bytes 2097168 | tf_op jit(solution)/shard_map/psum | solution.py:19
  117.6 1.3 convolution_convert_fusion.1
  119.0 4.3 %fusion = bf16[256,8192]{1,0:T(8,128)(2,1)S(1)} fusion(bf16[256,256]{1,0:T(8,128)(2,1)S(1)} %convolution_convert_fusion.1, bf16[2,1,256,8192]{3,2,1,0:T(8,128)(2,1)} %param.4, bf16[4096,256]{1,0:T(8,128)(2,1)} %get-tuple-element.5, bf16[4096,256]{1,0:T(8,128)(2,1)S(1)} %get-tuple-element.4), kind=kOutput, calls=%fused_computation.3 | convolution fusion | flops 1088421888 | bytes 12713984 | tf_op jit(solution)/shard_map/dot_general | solution.py:47
  123.2 1.5 convolution_convert_fusion
  124.7 9.6 %fusion.1 = bf16[256,8192]{1,0:T(8,128)(2,1)S(1)} fusion(bf16[256,256]{1,0:T(8,128)(2,1)S(1)} %convolution_convert_fusion, bf16[2,1,256,8192]{3,2,1,0:T(8,128)(2,1)} %param.4, bf16[4096,256]{1,0:T(8,128)(2,1)S(1)} %copy-done.6, bf16[4096,256]{1,0:T(8,128)(2,1)S(1)} %get-tuple-element.4), kind=kOutput, calls=%fused_computation.4 | convolution fusion | flops 1088421888 | bytes 12713984 | tf_op jit(solution)/shard_map/dot_general | solution.py:47
  134.4 1.3 fusion.43
  135.7 0.6 copy-done.2
  136.3 1.3 convolution_add_fusion
  137.7 2.8 slice_select_fusion
  140.5 1.6 copy-done
  142.2 4.2 %fusion.41 = f32[256,256]{1,0:T(8,128)S(1)} fusion(bf16[256,8192]{1,0:T(8,128)(2,1)} %copy-done.4, bf16[4096,256]{1,0:T(8,128)(2,1)} %get-tuple-element.5, bf16[4096,256]{1,0:T(8,128)(2,1)S(1)} %get-tuple-element.4), kind=kOutput, calls=%fused_computation.61 | convolution fusion | flops 1082130432 | bytes 8650752 | tf_op jit(solution)/shard_map/dot_general | solution.py:54
  146.4 0.5 fusion.7
  146.9 1.2 fusion.40
  148.2 0.5 fusion.2
  148.7 0.8 copy-done.5
  149.6 1.2 fusion.24
  150.8 1.9 multiply_add_fusion
  152.8 18.8 %reduce-scatter.5.cloned.1.call-done = f32[128,256]{1,0:T(8,128)} async-done(((f32[512,256]{1,0:T(8,128)}), f32[128,256]{1,0:T(8,128)}) %reduce-scatter.5.cloned.1.call-update) | async-done | bytes 131088 | tf_op jit(solution)/shard_map/reduce_scatter | solution.py:72
  171.7 7.4 %select_add_fusion = f32[4096,256]{1,0:T(8,128)} fusion(f32[4096,256]{1,0:T(8,128)} %collective-permute-done.1, f32[8192,256]{1,0:T(8,128)} %copy-done, pred[]{:T(512)S(6)} %eq.6), kind=kLoop, calls=%fused_computation.6 | loop fusion | flops 2097152 | bytes 16777216 | tf_op jit(solution)/shard_map/add | solution.py:68
  179.6 0.3 fusion.17
  180.3 5.7 %psum.31 = f32[2,256]{1,0:T(2,128)S(1)} all-reduce(f32[2,256]{1,0:T(2,128)S(1)} %pad_maximum_fusion.1), channel_id=1, replica_groups=mesh['groups'=2,'tile'=4,'cuts'=4] {'tile'}, use_global_device_ids=true, to_apply=%region_5.6 | all-reduce | flops 512 | bytes 4096 | tf_op jit(solution)/shard_map/psum | solution.py:75
  185.9 0.6 broadcast_multiply_fusion.3
  186.5 76.4 %all-reduce.8.cloned.1.call-done = f32[256,256]{1,0:T(8,128)} async-done(((f32[256,256]{1,0:T(8,128)}), f32[256,256]{1,0:T(8,128)}) %all-reduce.8.cloned.1.call-update) | async-done | bytes 262160 | tf_op jit(solution)/shard_map/psum | solution.py:74
  262.9 1.7 broadcast_multiply_fusion.1
  264.6 32.5 %all-reduce.6.cloned.1.call-done = f32[128,256]{1,0:T(8,128)} async-done(((f32[128,256]{1,0:T(8,128)}), f32[128,256]{1,0:T(8,128)}) %all-reduce.6.cloned.1.call-update) | async-done | bytes 131088 | tf_op jit(solution)/shard_map/psum | solution.py:73
  297.1 1.6 broadcast_multiply_fusion.2
  298.7 77.4 %reduce-scatter.3.cloned.1.call-done = f32[1024,256]{1,0:T(8,128)} async-done(((f32[4096,256]{1,0:T(8,128)}), f32[1024,256]{1,0:T(8,128)}) %reduce-scatter.3.cloned.1.call-update) | async-done | bytes 1048592 | tf_op jit(solution)/shard_map/reduce_scatter | solution.py:68
  376.1 2.3 broadcast_multiply_fusion
  (37 shorter events, 1.3 us)
Async XLA Ops:
  7.2 51.1 %all-gather.2.cloned.1.call-start = ((), (), s32[]{:S(2)}) async-start(), calls=%async_computation.2 | async-start | bytes 2621440 | tf_op jit(solution)/shard_map/all_gather | solution.py:29
  7.9 109.7 %all-reduce.4.cloned.1.call-start = ((), (), s32[]{:S(2)}) async-start(), calls=%async_computation.3 | async-start | bytes 4194304 | tf_op jit(solution)/shard_map/psum | solution.py:19
  58.2 4.5 %collective-permute-start = (bf16[4096,256]{1,0:T(8,128)(2,1)}, bf16[4096,256]{1,0:T(8,128)(2,1)}, u32[]{:S(2)}, u32[]{:S(2)}) collective-permute-start(bf16[4096,256]{1,0:T(8,128)(2,1)} %all-gather.2.cloned.1.call-done), channel_id=1, source_target_pairs={{0,4},{4,0},{8,12},{12,8},{1,5},{5,1},{9,13},{13,9},{2,6},{6,2},{1... | collective-permute-start | bytes 6291464 | tf_op jit(solution)/shard_map/ppermute | solution.py:14
  58.2 9.2 %copy-start.8 = (f32[2,256]{1,0:T(2,128)S(1)}, f32[2,256]{1,0:T(2,128)}, u32[]{:S(2)}) copy-start(f32[2,256]{1,0:T(2,128)} %param.6) | copy-start | bytes 6148
  58.2 59.4 %copy-start.1 = (f32[256,256]{1,0:T(8,128)S(1)}, f32[256,256]{1,0:T(8,128)}, u32[]{:S(2)}) copy-start(f32[256,256]{1,0:T(8,128)} %param.7) | copy-start | bytes 786436
  67.4 104.2 %reduce-scatter.5.cloned.1.call-start = ((), (), s32[]{:S(2)}) async-start(), calls=%async_computation.5 | async-start | bytes 655360 | tf_op jit(solution)/shard_map/reduce_scatter | solution.py:72
  118.9 5.8 %copy-start.6 = (bf16[4096,256]{1,0:T(8,128)(2,1)S(1)}, bf16[4096,256]{1,0:T(8,128)(2,1)}, u32[]{:S(2)}) copy-start(bf16[4096,256]{1,0:T(8,128)(2,1)} %get-tuple-element.5) | copy-start | bytes 6291460
  123.2 11.1 %copy-start.4 = (bf16[256,8192]{1,0:T(8,128)(2,1)}, bf16[256,8192]{1,0:T(8,128)(2,1)S(1)}, u32[]{:S(2)}) copy-start(bf16[256,8192]{1,0:T(8,128)(2,1)S(1)} %fusion) | copy-start | bytes 12582916
  134.4 2.0 copy-start.2
  137.7 4.5 %copy-start = (f32[8192,256]{1,0:T(8,128)}, f32[8192,256]{1,0:T(8,128)S(1)}, u32[]{:S(2)}) copy-start(f32[8192,256]{1,0:T(8,128)S(1)} %convolution_add_fusion) | copy-start | bytes 25165828
  142.2 29.5 %collective-permute-start.1 = (f32[4096,256]{1,0:T(8,128)}, f32[4096,256]{1,0:T(8,128)}, u32[]{:S(2)}, u32[]{:S(2)}) collective-permute-start(f32[4096,256]{1,0:T(8,128)} %slice_select_fusion), channel_id=1, source_target_pairs={{0,4},{4,0},{8,12},{12,8},{1,5},{5,1},{9,13},{13,9},{2,6},{6,2},{1... | collective-permute-start | bytes 12582920 | tf_op jit(solution)/shard_map/ppermute | solution.py:14
  142.2 4.7 %copy-start.3 = (bf16[256,8192]{1,0:T(8,128)(2,1)S(1)}, bf16[256,8192]{1,0:T(8,128)(2,1)}, u32[]{:S(2)}) copy-start(bf16[256,8192]{1,0:T(8,128)(2,1)} %copy-done.2) | copy-start | bytes 12582916
  142.2 4.8 %copy-start.7 = (bf16[4096,256]{1,0:T(8,128)(2,1)S(1)}, bf16[4096,256]{1,0:T(8,128)(2,1)}, u32[]{:S(2)}) copy-start(bf16[4096,256]{1,0:T(8,128)(2,1)} %get-tuple-element.5) | copy-start | bytes 6291460
  148.7 0.8 copy-start.5
  149.5 113.4 %all-reduce.8.cloned.1.call-start = ((), (), s32[]{:S(2)}) async-start(), calls=%async_computation.7 | async-start | bytes 524288 | tf_op jit(solution)/shard_map/psum | solution.py:74
  152.8 144.3 %all-reduce.6.cloned.1.call-start = ((), (), s32[]{:S(2)}) async-start(), calls=%async_computation.6 | async-start | bytes 262144 | tf_op jit(solution)/shard_map/psum | solution.py:73
  171.6 204.5 %reduce-scatter.3.cloned.1.call-start = ((), (), s32[]{:S(2)}) async-start(), calls=%async_computation.4 | async-start | bytes 5242880 | tf_op jit(solution)/shard_map/reduce_scatter | solution.py:68
Sparse Core Ops, SparseCore 0:
  9.6 48.6 all-gather.1
  67.5 50.0 all-reduce.3
  149.7 21.8 reduce-scatter.4
  175.8 87.1 all-reduce.7
  265.2 31.8 all-reduce.5
  299.3 76.7 reduce-scatter.2
where the time goes:
time: 385 us
  waiting for transfers between devices  311 us (81%)
  matrix products  30 us (8%)
  other arithmetic  21 us (5%)
  between operations  14.3 us (4%)
  blocking collectives  5.67 us (1%)
    reduce_scatter x1, waiting for transfers between devices, body(): lax.psum_scatter(mine + received, 'cuts', scatter_dimension=0, tiled=True)  77.4 us
    psum x1, waiting for transfers between devices, body(): core_total = lax.psum(acc_core, ('tile', 'cuts'))  76.4 us
    all_gather x1, waiting for transfers between devices, body(): own_block = lax.all_gather(factor, 'cuts', axis=0, tiled=True)  50.3 us
    psum x1, waiting for transfers between devices, from_root(): return lax.psum(block, axis)  50.2 us
    psum x1, waiting for transfers between devices, body(): window_total = lax.psum(window_part, 'tile')  32.5 us
    reduce_scatter x1, waiting for transfers between devices, body(): lax.psum_scatter(padded, 'cuts', scatter_dimension=0, tiled=True)  18.8 us
    dot_general x2, matrix products, body(): lax.dot_general(mapped, column_factor, (((1,), (1,)), ((), ())), preferre...  13.9 us
  transfers between devices with their start and end apart: 8, of which 7 were waited for; matrix products, arithmetic and copies ran while one was open for 6% of the time, Pallas kernels for 0%

commit v1 on v0

v1 whole, which is shorter than its diff:
```python
import functools
import math

import jax
import jax.numpy as jnp
from jax import lax
from jax.experimental import pallas as pl
from jax.experimental.pallas import tpu as pltpu
from jax.sharding import PartitionSpec as P

P_SIZE = 256
F32, BF16, F16 = jnp.float32, jnp.bfloat16, jnp.float16
NN = (((1,), (0,)), ((), ()))
NT = (((1,), (1,)), ((), ()))
TN = (((0,), (0,)), ((), ()))
VMEM_LIMIT = 48 * 2**20


def dot(a, b, dims, **more):
    return lax.dot_general(a, b, dims, preferred_element_type=F32, **more)


def split3(value):
    first = value.astype(BF16)
    rest = value - first.astype(F32)
    second = rest.astype(BF16)
    return first, second, (rest - second.astype(F32)).astype(BF16)


def swapped(value, axis, mask):
    pairs = [(source, source ^ mask) for source in range(lax.axis_size(axis))]
    return lax.ppermute(value, axis, pairs)


def mapped_kernel(core_ref, window_ref, inner_ref, mapped_ref, turned_ref):
    rows = window_ref.shape[0] // 2
    at = core_ref[0]
    own = window_ref[pl.ds(pl.multiple_of(at * rows, rows), rows), :]
    other = window_ref[pl.ds(pl.multiple_of((1 - at) * rows, rows), rows), :]
    window = jnp.concatenate([own, other], 0)
    for month in range(inner_ref.shape[0]):
        value = sum(dot(window, term, NN) for term in split3(inner_ref[month]))
        rounded = value.astype(BF16)
        mapped_ref[month] = rounded
        turned_ref[:, month * 2 * rows : (month + 1) * 2 * rows] = rounded.astype(F32).T.astype(BF16)


def mapped_call(core_at, window, inner):
    months, size = inner.shape[0], window.shape[0]
    return pl.pallas_call(
        mapped_kernel,
        out_shape=[
            jax.ShapeDtypeStruct((months, size, P_SIZE), BF16),
            jax.ShapeDtypeStruct((P_SIZE, months * size), BF16),
        ],
        in_specs=[
            pl.BlockSpec(memory_space=pltpu.SMEM),
            pl.BlockSpec(memory_space=pltpu.VMEM),
            pl.BlockSpec(memory_space=pltpu.VMEM),
        ],
        out_specs=[pl.BlockSpec(memory_space=pltpu.VMEM)] * 2,
        compiler_params=pltpu.CompilerParams(vmem_limit_bytes=VMEM_LIMIT),
        cost_estimate=pl.CostEstimate(
            flops=6 * months * size * P_SIZE * P_SIZE, bytes_accessed=2 * 2**20, transcendentals=0
        ),
        name="mapped",
    )(core_at, window, inner)


def encoded(value):
    peak = jnp.max(jnp.abs(value), axis=0, keepdims=True)
    exponent = jnp.ceil(jnp.log2(jnp.maximum(peak, 1e-30)))
    return value * jnp.exp2(15.0 - exponent), jnp.broadcast_to(exponent, (16, value.shape[1]))


def piece_kernel(scaled, at_ref, own_ref, other_ref, block_ref, mapped_ref, turned_ref, grad_ref, proj_ref):
    step = pl.program_id(0)
    block = block_ref[...]
    months, size = mapped_ref.shape[0], mapped_ref.shape[1]
    rows = size // 2
    model = dot(mapped_ref[...].reshape(months * size, P_SIZE), block, NT)
    parts = []
    for month in range(months):
        for band in range(2):
            flows = own_ref[month, 0] if band == 0 else other_ref[month]
            at = (2 * month + band) * rows
            parts.append((flows.astype(F32) - model[at : at + rows]).astype(BF16))
    residual = jnp.concatenate(parts, 0)
    grad = dot(turned_ref[...], residual, NN)
    if scaled:
        value, exponent = encoded(grad)
        grad_ref[:P_SIZE, :] = value
        grad_ref[P_SIZE:, :] = exponent
    else:
        grad_ref[...] = grad
    projected = dot(residual, block, NN).reshape(proj_ref.shape)

    @pl.when(step == 0)
    def _():
        proj_ref[...] = projected

    @pl.when(step > 0)
    def _():
        proj_ref[...] += projected


def piece_call(at, trade, other, block, mapped, turned, scaled, label):
    months, size = mapped.shape[0], mapped.shape[1]
    rows, columns = size // 2, block.shape[0]
    width = min(512, columns)
    steps = columns // width
    high = P_SIZE + 16 if scaled else P_SIZE
    spec = pltpu.PrefetchScalarGridSpec(
        num_scalar_prefetch=1,
        grid=(steps,),
        in_specs=[
            pl.BlockSpec((months, 1, rows, width), lambda j, s: (0, 0, 0, s[0] * steps + j)),
            pl.BlockSpec((months, rows, width), lambda j, s: (0, 0, s[1] * steps + j)),
            pl.BlockSpec((width, P_SIZE), lambda j, s: (j, 0)),
            pl.BlockSpec((months, size, P_SIZE), lambda j, s: (0, 0, 0)),
            pl.BlockSpec((P_SIZE, months * size), lambda j, s: (0, 0)),
        ],
        out_specs=[
            pl.BlockSpec((high, width), lambda j, s: (0, j)),
            pl.BlockSpec((months, size, P_SIZE), lambda j, s: (0, 0, 0)),
        ],
    )
    return pl.pallas_call(
        functools.partial(piece_kernel, scaled),
        grid_spec=spec,
        out_shape=[
            jax.ShapeDtypeStruct((high, columns), F32),
            jax.ShapeDtypeStruct((months, size, P_SIZE), F32),
        ],
        compiler_params=pltpu.CompilerParams(vmem_limit_bytes=VMEM_LIMIT),
        cost_estimate=pl.CostEstimate(
            flops=6 * months * size * columns * P_SIZE,
            bytes_accessed=2 * months * size * columns + 4 * 2**20,
            transcendentals=0,
        ),
        name=label,
    )(at, trade, other, block, mapped, turned)


def relay_kernel(first_ref, second_ref, out_ref):
    received = first_ref[:P_SIZE, :] * jnp.exp2(first_ref[P_SIZE : P_SIZE + 1, :] - 15.0)
    value, exponent = encoded(received + second_ref[...])
    out_ref[:P_SIZE, :] = value
    out_ref[P_SIZE:, :] = exponent


def relay_call(received, own):
    columns = own.shape[1]
    width = columns // 2
    return pl.pallas_call(
        relay_kernel,
        grid=(2,),
        in_specs=[
            pl.BlockSpec((P_SIZE + 16, width), lambda j: (0, j)),
            pl.BlockSpec((P_SIZE, width), lambda j: (0, j)),
        ],
        out_specs=pl.BlockSpec((P_SIZE + 16, width), lambda j: (0, j)),
        out_shape=jax.ShapeDtypeStruct((P_SIZE + 16, columns), F32),
        compiler_params=pltpu.CompilerParams(vmem_limit_bytes=VMEM_LIMIT),
        cost_estimate=pl.CostEstimate(flops=10 * P_SIZE * columns, bytes_accessed=3 * 2**20, transcendentals=0),
        name="relay",
    )(received, own)


def final_kernel(coef, own_ref, near_ref, far_ref, out_ref):
    total = own_ref[...]
    for ref in (near_ref, far_ref):
        total = total + ref[:P_SIZE, :] * jnp.exp2(ref[P_SIZE : P_SIZE + 1, :] - 15.0)
    out_ref[...] = (-coef * total).T


def final_call(coef, own, near, far):
    columns = own.shape[1]
    width = columns // 2
    tall = pl.BlockSpec((P_SIZE + 16, width), lambda j: (0, j))
    return pl.pallas_call(
        functools.partial(final_kernel, coef),
        grid=(2,),
        in_specs=[pl.BlockSpec((P_SIZE, width), lambda j: (0, j)), tall, tall],
        out_specs=pl.BlockSpec((width, P_SIZE), lambda j: (j, 0)),
        out_shape=jax.ShapeDtypeStruct((columns, P_SIZE), F32),
        compiler_params=pltpu.CompilerParams(vmem_limit_bytes=VMEM_LIMIT),
        cost_estimate=pl.CostEstimate(flops=10 * P_SIZE * columns, bytes_accessed=4 * 2**20, transcendentals=0),
        name="final",
    )(own, near, far)


def terms_kernel(cuts, at_ref, window_ref, inner_ref, core_ref, scales_ref, columns_ref, *rest):
    projs, (keep_ref, send_ref, acc_ref) = rest[:-3], rest[-3:]
    months, size = projs[0].shape[0], projs[0].shape[1]
    rows = size // 2
    at = at_ref[0]
    own = window_ref[pl.ds(pl.multiple_of(at * rows, rows), rows), :]
    other = window_ref[pl.ds(pl.multiple_of((1 - at) * rows, rows), rows), :]
    window = jnp.concatenate([own, other], 0)
    core = core_ref[...]
    acc_window = jnp.zeros((size, P_SIZE), F32)
    acc_core = jnp.zeros((P_SIZE, P_SIZE), F32)
    diagonals = []
    for month in range(months):
        proj = projs[0][month]
        for ref in projs[1:]:
            proj = proj + ref[month]
        acc_window = acc_window + dot(proj, inner_ref[month], NT, precision=lax.Precision.HIGHEST)
        gram = sum(dot(window, term, TN) for term in split3(proj))
        down = columns_ref[:, month : month + 1]
        acc_core = acc_core + down * gram * scales_ref[month : month + 1, :]
        weighted = gram * core
        diagonals.append(jnp.sum((weighted + weighted.T) * down, axis=0, keepdims=True))
    diagonals.append(jnp.zeros((8 - months, P_SIZE), F32))
    diagonal = jnp.concatenate(diagonals, 0)
    acc_ref[pl.ds(pl.multiple_of(at * rows, rows), rows), :] = acc_window[:rows]
    acc_ref[pl.ds(pl.multiple_of((1 - at) * rows, rows), rows), :] = acc_window[rows:]
    acc_ref[size:, :] = acc_core
    w = size // (4 * cuts)
    q = P_SIZE // 4
    half = cuts * w + q
    for ref, which in ((keep_ref, at), (send_ref, 1 - at)):
        for x in range(2):
            for cut in range(cuts):
                start = pl.multiple_of(cut * 4 * w + which * 2 * w + x * w, 8)
                ref[x * half + cut * w : x * half + (cut + 1) * w, :] = acc_ref[pl.ds(start, w), :]
            start = pl.multiple_of(size + which * 2 * q + x * q, 8)
            ref[x * half + cuts * w : (x + 1) * half, :] = acc_ref[pl.ds(start, q), :]
        ref[2 * half :, :] = diagonal


def terms_call(cuts, core_at, window, inner, core, scales, projs):
    months, size = projs[0].shape[0], projs[0].shape[1]
    high = size // 2 + P_SIZE // 2 + 8
    vmem = pl.BlockSpec(memory_space=pltpu.VMEM)
    return pl.pallas_call(
        functools.partial(terms_kernel, cuts),
        in_specs=[pl.BlockSpec(memory_space=pltpu.SMEM)] + [vmem] * (5 + len(projs)),
        out_specs=[vmem, vmem],
        out_shape=[jax.ShapeDtypeStruct((high, P_SIZE), F32)] * 2,
        scratch_shapes=[pltpu.VMEM((size + P_SIZE, P_SIZE), F32)],
        compiler_params=pltpu.CompilerParams(vmem_limit_bytes=VMEM_LIMIT),
        cost_estimate=pl.CostEstimate(
            flops=18 * months * size * P_SIZE * P_SIZE, bytes_accessed=6 * 2**20, transcendentals=0
        ),
        name="terms",
    )(core_at, window, inner, core, scales, scales.T, *projs)


def body_line(trade, factor, scales, core):
    cuts = lax.axis_size("cuts")
    tile, cut = lax.axis_index("tile"), lax.axis_index("cuts")
    x, at = tile // 2, tile % 2
    months, rows = trade.shape[0], trade.shape[2]
    size, piece = 2 * rows, factor.shape[0]
    coef = 1.0 / math.sqrt(months * cuts * size)
    core_at = at.astype(jnp.int32).reshape(1)
    inner = scales[:, :, None] * core[None] * scales[:, None, :]

    head = factor[:size]
    sent = [lax.ppermute(head, ("tile", "cuts"), [(0, target)]) for target in range(1, cuts)]
    line = jnp.where(cut == 0, head, sum(sent[1:], sent[0]))
    across = lax.ppermute(line, "tile", [(0, 2)])
    even = jnp.where(x == 0, line, across)
    window = jnp.where(at == 0, even, lax.ppermute(even, "tile", [(0, 1), (2, 3)]))

    near = swapped(factor, "cuts", 1)
    middle = swapped(factor, "cuts", 2)
    far = swapped(middle, "cuts", 1)

    half = cuts * piece
    give = lax.dynamic_slice_in_dim(trade[:, 0], (1 - at) * half, half, 2)
    other = swapped(give, "tile", 1)

    mapped, turned = mapped_call(core_at, window, inner)

    def piece_of(which, block, scaled, label):
        where = jnp.stack([at * cuts + which, which]).astype(jnp.int32)
        return piece_call(where, trade, other, block, mapped, turned, scaled, label)

    grad_near, proj_near = piece_of(cut ^ 1, near, True, "piece_near")
    from_near = swapped(grad_near.astype(F16), "cuts", 1)
    grad_own, proj_own = piece_of(cut, factor, False, "piece_own")
    grad_middle, proj_middle = piece_of(cut ^ 2, middle, False, "piece_middle")
    grad_far, proj_far = piece_of(cut ^ 3, far, True, "piece_far")
    joined = swapped(grad_far.astype(F16), "cuts", 1)

    keep, send = terms_call(cuts, core_at, window, inner, core, scales, [proj_near, proj_own, proj_middle, proj_far])
    both = keep + swapped(send, "tile", 1)
    w, q = size // (4 * cuts), P_SIZE // 4
    part = cuts * w + q
    low, high, diagonal = both[:part], both[part : 2 * part], both[2 * part :]
    keep = jnp.concatenate([jnp.where(x == 0, low, high), diagonal], 0)
    send = jnp.concatenate([jnp.where(x == 0, high, low), diagonal], 0)
    quarter = keep + swapped(send, "tile", 2)
    diagonal = quarter[part : part + months]
    core_part = quarter[cuts * w : part]

    def for_cut(which):
        return jnp.concatenate([lax.dynamic_slice_in_dim(quarter, which * w, w, 0), core_part], 0)

    total = for_cut(cut)
    for mask in range(1, cuts):
        total = total + swapped(for_cut(cut ^ mask), "cuts", mask)

    def joined_pair(mine, theirs, first):
        return jnp.where(first, mine, theirs), jnp.where(first, theirs, mine)

    first, second = joined_pair(total, swapped(total, "tile", 2), x == 0)
    line_total = jnp.concatenate([first[:w], second[:w], first[w:], second[w:]], 0)
    first, second = joined_pair(line_total, swapped(line_total, "tile", 1), at == 0)
    grad_window = jnp.concatenate([first[: 2 * w], second[: 2 * w]], 0)
    grad_core = jnp.concatenate([first[2 * w :], second[2 * w :]], 0)

    passed = relay_call(joined.astype(F32), grad_middle)
    from_far = swapped(passed.astype(F16), "cuts", 2)
    grad_factor = final_call(coef, grad_own, from_near.astype(F32), from_far.astype(F32))
    return (grad_factor, -coef * grad_window, -coef * grad_core, -coef * diagonal)


def from_root(block, axis, source):
    block = jnp.where(lax.axis_index(axis) == source, block, jnp.zeros_like(block))
    return lax.psum(block, axis)


def body_any(trade, factor, scales, core):
    n_cuts = lax.axis_size("cuts")
    band_index = lax.axis_index("tile") % 2
    months = trade.shape[0]
    rows_band = trade.shape[2]
    window_size = 2 * rows_band
    highest = lax.Precision.HIGHEST
    own_block = lax.all_gather(factor, "cuts", axis=0, tiled=True)
    block = own_block.shape[0]
    partner_block = swapped(own_block, "tile", 1)
    first_block = jnp.where(band_index == 0, own_block, partner_block)
    second_block = jnp.where(band_index == 0, partner_block, own_block)
    column_factor = jnp.concatenate([first_block, second_block], 0)
    window_block = from_root(own_block, "tile", 0)
    window_rows = lax.dynamic_slice_in_dim(window_block, band_index * rows_band, rows_band, 0)
    window32 = window_rows.astype(F32)
    coef = 1.0 / math.sqrt(months * n_cuts * window_size)
    acc_columns = jnp.zeros((2 * block, P_SIZE), F32)
    acc_window = jnp.zeros((rows_band, P_SIZE), F32)
    acc_core = jnp.zeros((P_SIZE, P_SIZE), F32)
    diag_terms = []
    for month in range(months):
        diag_k = scales[month]
        inner = diag_k[:, None] * core * diag_k[None, :]
        mapped = jnp.dot(window32, inner, precision=highest).astype(BF16)
        model = dot(mapped, column_factor, NT)
        residual = (trade[month, 0].astype(F32) - model).astype(BF16)
        acc_columns = acc_columns + dot(residual, mapped, TN)
        projected = dot(residual, column_factor, NN)
        acc_window = acc_window + jnp.dot(projected, inner.T, precision=highest)
        gram = jnp.dot(window32.T, projected, precision=highest)
        acc_core = acc_core + diag_k[:, None] * gram * diag_k[None, :]
        weighted = gram * core
        diag_terms.append(
            jnp.dot(weighted, diag_k, precision=highest) + jnp.dot(weighted.T, diag_k, precision=highest)
        )
    diag_stack = jnp.stack(diag_terms, 0)
    halves = acc_columns.reshape(2, block, P_SIZE)
    mine = jnp.where(band_index == 0, halves[0], halves[1])
    theirs = jnp.where(band_index == 0, halves[1], halves[0])
    received = swapped(theirs, "tile", 1)
    grad_factor = lax.psum_scatter(mine + received, "cuts", scatter_dimension=0, tiled=True)
    padded = lax.dynamic_update_slice_in_dim(
        jnp.zeros((window_size, P_SIZE), F32), acc_window, band_index * rows_band, 0
    )
    window_part = lax.psum_scatter(padded, "cuts", scatter_dimension=0, tiled=True)
    window_total = lax.psum(window_part, "tile")
    core_total = lax.psum(acc_core, ("tile", "cuts"))
    diag_total = lax.psum(diag_stack, "tile")
    return (-coef * grad_factor, -coef * window_total, -coef * core_total, -coef * diag_total)


def body(trade, factor, scales, core):
    line = lax.axis_size("cuts") == 4 and lax.axis_size("tile") == 4
    if line and factor.shape[0] >= 2 * trade.shape[2]:
        return body_line(trade, factor, scales, core)
    return body_any(trade, factor, scales, core)


def solution(mesh):
    return jax.shard_map(
        body,
        mesh=mesh,
        in_specs=(
            P(("groups", "cuts"), "tile", None, None),
            P(("groups", "tile", "cuts"), None),
            P(("groups", "cuts"), None),
            P("groups", None),
        ),
        out_specs=(
            P(("groups", "tile", "cuts"), None),
            P(("groups", "cuts"), None),
            P("groups", None),
            P(("groups", "cuts"), None),
        ),
        check_vma=False,
    )
```

time: 385 us -> 133 us (0.35)
  waiting for transfers between devices: 311 us -> 73.6 us
  matrix products: 30 us -> 0 us
  starting transfers between devices: 0.24 us -> 25.8 us
  Pallas kernels: 0 us -> 22.7 us
  other arithmetic: 21 us -> 3.26 us
  between operations: 14.3 us -> 1.14 us
  blocking collectives: 5.67 us -> 0 us
    psum x3 -> x0, waiting for transfers between devices: 159 us -> none  [the longest x1 76.4 us: body(): core_total = lax.psum(acc_core, ('tile', 'cuts'))]
    reduce_scatter x2 -> x0, waiting for transfers between devices: 96.1 us -> none  [the longest x1 77.4 us: body(): lax.psum_scatter(mine + received, 'cuts', scatter_dimension=0, tiled=True)]
    all_gather x1 -> x0, waiting for transfers between devices: 50.3 us -> none  [body(): own_block = lax.all_gather(factor, 'cuts', axis=0, tiled=True)]
    ppermute x2 -> x14, waiting for transfers between devices: 4.5 us -> 54.7 us  [swapped(): return lax.ppermute(value, axis, pairs)]
    dot_general x16 -> x0, matrix products: 30 us -> none  [the longest x2 13.9 us: body(): lax.dot_general(mapped, column_factor, (((1,), (1,)), ((), ())), preferre...]
    pallas_call x0 -> x8, Pallas kernels: none -> 22.7 us  [the longest x4 18.2 us: piece_call(): pl.pallas_call(functools.partial(piece_kernel, scaled), grid_spec=spec, o...]
    ppermute x0 -> x5, waiting for transfers between devices: none -> 18.9 us  [the longest x3 15.2 us: body_line(): lax.ppermute(head, ('tile', 'cuts'), [(0, target)])]
    ppermute x2 -> x14, starting transfers between devices: 0.01 us -> 14 us  [swapped(): return lax.ppermute(value, axis, pairs)]
  transfers between devices with their start and end apart: 8 -> 19, of which waited for: 7 -> 13; matrix products, arithmetic and copies ran while one was open for 6% -> 3% of each run, Pallas kernels for 0% -> 11%
where the time goes in v1:
time: 133 us; the launch traced here: 132 us
  waiting for transfers between devices  73.6 us (55%)
  starting transfers between devices  25.8 us (19%)
  Pallas kernels  22.7 us (17%)
  local copies, waits for them, and re-layouts  5.72 us (4%)
  other arithmetic  3.26 us (2%)
    ppermute x14, waiting for transfers between devices, swapped(): return lax.ppermute(value, axis, pairs)  54.7 us
    pallas_call x4, Pallas kernels, piece_call(): pl.pallas_call(functools.partial(piece_kernel, scaled), grid_spec=spec, o...  18.2 us
    ppermute x3, waiting for transfers between devices, body_line(): lax.ppermute(head, ('tile', 'cuts'), [(0, target)])  15.2 us
    ppermute x14, starting transfers between devices, swapped(): return lax.ppermute(value, axis, pairs)  14 us
    ppermute x3, starting transfers between devices, body_line(): lax.ppermute(head, ('tile', 'cuts'), [(0, target)])  9.13 us
    dynamic_slice x1, local copies, waits for them, and re-layouts, body_line(): give = lax.dynamic_slice_in_dim(trade[:, 0], (1 - at) * half, half, 2)  4.77 us
    ppermute x1, waiting for transfers between devices, body_line(): across = lax.ppermute(line, 'tile', [(0, 2)])  3.63 us
  transfers between devices with their start and end apart: 19, of which 13 were waited for; matrix products, arithmetic and copies ran while one was open for 3% of the time, Pallas kernels for 11%

profile of v1, /device:TPU:0, one launch (start us, length us, event | category | flops | bytes accessed | tf_op | source)
XLA Modules:
  0.0 132.2 jit_solution(13298994245090607580)
XLA Ops:
  0.7 4.8 %dynamic-slice_bitcast_fusion = bf16[2,256,4096]{2,1,0:T(8,128)(2,1)} fusion(bf16[2,1,256,8192]{3,2,1,0:T(8,128)(2,1)} %own_ref.7, s32[]{:T(128)S(6)} %select_n.81), kind=kLoop, calls=%fused_computation | loop fusion | bytes 8388612 | tf_op jit(solution)/shard_map/dynamic_slice | solution.py:273
  5.9 6.5 %collective-permute-start.3 = (bf16[512,256]{1,0:T(8,128)(2,1)S(1)}, bf16[512,256]{1,0:T(8,128)(2,1)S(1)}, u32[]{:S(2)}, u32[]{:S(2)}) collective-permute-start(bf16[512,256]{1,0:T(8,128)(2,1)S(1)} %slice.42), channel_id=1, source_target_pairs={{0,3},{16,19}} | collective-permute-start | bytes 786440 | tf_op jit(solution)/shard_map/ppermute | solution.py:262
  12.4 1.3 collective-permute-start.2
  13.8 1.3 collective-permute-start.1
  15.2 4.0 %collective-permute-done.3 = bf16[512,256]{1,0:T(8,128)(2,1)S(1)} collective-permute-done((bf16[512,256]{1,0:T(8,128)(2,1)S(1)}, bf16[512,256]{1,0:T(8,128)(2,1)S(1)}, u32[]{:S(2)}, u32[]{:S(2)}) %collective-permute-start.3) | collective-permute-done | bytes 262176 | tf_op jit(solution)/shard_map/ppermute | solution.py:262
  19.2 5.6 %collective-permute-done.2 = bf16[512,256]{1,0:T(8,128)(2,1)S(1)} collective-permute-done((bf16[512,256]{1,0:T(8,128)(2,1)S(1)}, bf16[512,256]{1,0:T(8,128)(2,1)S(1)}, u32[]{:S(2)}, u32[]{:S(2)}) %collective-permute-start.2) | collective-permute-done | bytes 262176 | tf_op jit(solution)/shard_map/ppermute | solution.py:262
  24.8 5.6 %collective-permute-done.1 = bf16[512,256]{1,0:T(8,128)(2,1)S(1)} collective-permute-done((bf16[512,256]{1,0:T(8,128)(2,1)S(1)}, bf16[512,256]{1,0:T(8,128)(2,1)S(1)}, u32[]{:S(2)}, u32[]{:S(2)}) %collective-permute-start.1) | collective-permute-done | bytes 262176 | tf_op jit(solution)/shard_map/ppermute | solution.py:262
  30.5 1.3 collective-permute-start.4
  32.0 3.6 %collective-permute-done.4 = bf16[512,256]{1,0:T(8,128)(2,1)S(1)} collective-permute-done((bf16[512,256]{1,0:T(8,128)(2,1)S(1)}, bf16[512,256]{1,0:T(8,128)(2,1)S(1)}, u32[]{:S(2)}, u32[]{:S(2)}) %collective-permute-start.4) | collective-permute-done | bytes 262176 | tf_op jit(solution)/shard_map/ppermute | solution.py:264
  35.7 1.3 collective-permute-start.5
  37.1 0.8 copy.8
  38.1 3.8 %collective-permute-start.9 = (bf16[1024,256]{1,0:T(8,128)(2,1)S(1)}, bf16[1024,256]{1,0:T(8,128)(2,1)S(1)}, u32[]{:S(2)}, u32[]{:S(2)}) collective-permute-start(bf16[1024,256]{1,0:T(8,128)(2,1)S(1)} %collective-permute-done.8.block_ref), channel_id=1, source_target_pairs={{0,1},{1,0},{2,3},{3,2},{4,5},{5,4},{6,7},{7,6},{8,9},{9,8},{10,11... | collective-permute-start | bytes 1572872 | tf_op jit(solution)/shard_map/ppermute | solution.py:32
  41.9 0.7 mapped.1
  42.6 4.5 %piece_middle.1 = (f32[256,1024]{1,0:T(8,128)S(1)}, f32[2,512,256]{2,1,0:T(8,128)S(1)}) custom-call(s32[2]{0:T(128)S(1)} %pad_add_fusion.3.at_ref, bf16[2,1,256,8192]{3,2,1,0:T(8,128)(2,1)} %own_ref.7, bf16[2,256,4096]{2,1,0:T(8,128)(2,1)} %collective-permute-done.other_ref, bf16[1024,256]{1,0:T(8,128)(2,1)S(1)} %collective-permute-done.8.block_ref, ...), custom_call_target="tpu_custom_call" | custom-call | flops 1610612736 | bytes 6291456 | tf_op jit(solution)/shard_map/piece_middle/pallas_call | solution.py:128
  47.2 4.5 %piece_own.1 = (f32[256,1024]{1,0:T(8,128)S(1)}, f32[2,512,256]{2,1,0:T(8,128)S(1)}) custom-call(s32[2]{0:T(128)S(1)} %pad_add_fusion.at_ref, bf16[2,1,256,8192]{3,2,1,0:T(8,128)(2,1)} %own_ref.7, bf16[2,256,4096]{2,1,0:T(8,128)(2,1)} %collective-permute-done.other_ref, bf16[1024,256]{1,0:T(8,128)(2,1)S(1)} %copy-done, ...), custom_call_target="tpu_custom_call" | custom-call | flops 1610612736 | bytes 6291456 | tf_op jit(solution)/shard_map/piece_own/pallas_call | solution.py:128
  51.7 2.8 %collective-permute-done.9.block_ref = bf16[1024,256]{1,0:T(8,128)(2,1)S(1)} collective-permute-done((bf16[1024,256]{1,0:T(8,128)(2,1)S(1)}, bf16[1024,256]{1,0:T(8,128)(2,1)S(1)}, u32[]{:S(2)}, u32[]{:S(2)}) %collective-permute-start.9) | collective-permute-done | bytes 524320 | tf_op jit(solution)/shard_map/ppermute | solution.py:32
  54.5 4.6 %piece_far.1 = (f32[272,1024]{1,0:T(8,128)S(1)}, f32[2,512,256]{2,1,0:T(8,128)S(1)}) custom-call(s32[2]{0:T(128)S(1)} %pad_add_fusion.2.at_ref, bf16[2,1,256,8192]{3,2,1,0:T(8,128)(2,1)} %own_ref.7, bf16[2,256,4096]{2,1,0:T(8,128)(2,1)} %collective-permute-done.other_ref, bf16[1024,256]{1,0:T(8,128)(2,1)S(1)} %collective-permute-done.9.block_ref, ...), custom_call_target="tpu_custom_call" | custom-call | flops 1610612736 | bytes 6291456 | tf_op jit(solution)/shard_map/piece_far/pallas_call | solution.py:128
  59.1 4.6 %piece_near.1 = (f32[272,1024]{1,0:T(8,128)S(1)}, f32[2,512,256]{2,1,0:T(8,128)S(1)}) custom-call(s32[2]{0:T(128)S(1)} %pad_add_fusion.1.at_ref, bf16[2,1,256,8192]{3,2,1,0:T(8,128)(2,1)} %own_ref.7, bf16[2,256,4096]{2,1,0:T(8,128)(2,1)} %collective-permute-done.other_ref, bf16[1024,256]{1,0:T(8,128)(2,1)S(1)} %collective-permute-done.6.block_ref, ...), custom_call_target="tpu_custom_call" | custom-call | flops 1610612736 | bytes 6291456 | tf_op jit(solution)/shard_map/piece_near/pallas_call | solution.py:128
  63.7 1.8 %terms.1 = (f32[392,256]{1,0:T(8,128)S(1)}, f32[392,256]{1,0:T(8,128)S(1)}) custom-call(s32[1]{0:T(128)} %bitcast.3.core_ref.at_ref, bf16[512,256]{1,0:T(8,128)(2,1)S(1)} %broadcast_select_fusion.1.window_ref, f32[2,256,256]{2,1,0:T(8,128)S(1)} %multiply_multiply_fusion.inner_ref, f32[256,256]{1,0:T(8,128)S(1)} %copy-done.3, f32[2,256]{1,0:T(2,128)S(1)} %copy-done.7, ...), custom_call_target="tpu_custom_call" | custom-call | flops 1207959552 | bytes 6291456 | tf_op jit(solution)/shard_map/terms/pallas_call | solution.py:237
  65.5 1.7 %collective-permute-done.12 = f32[392,256]{1,0:T(8,128)S(1)} collective-permute-done((f32[392,256]{1,0:T(8,128)S(1)}, f32[392,256]{1,0:T(8,128)S(1)}, u32[]{:S(2)}, u32[]{:S(2)}) %collective-permute-start.12) | collective-permute-done | bytes 401440 | tf_op jit(solution)/shard_map/ppermute | solution.py:32
  67.6 2.5 %collective-permute-start.10 = (f16[272,1024]{1,0:T(8,128)(2,1)S(1)}, f16[272,1024]{1,0:T(8,128)(2,1)S(1)}, u32[]{:S(2)}, u32[]{:S(2)}) collective-permute-start(f16[272,1024]{1,0:T(8,128)(2,1)S(1)} %convert_element_type.20), channel_id=1, source_target_pairs={{0,1},{1,0},{2,3},{3,2},{4,5},{5,4},{6,7},{7,6},{8,9},{9,8},{10,11... | collective-permute-start | bytes 1671176 | tf_op jit(solution)/shard_map/ppermute | solution.py:32
  70.3 4.3 %collective-permute-done.13 = f32[200,256]{1,0:T(8,128)S(1)} collective-permute-done((f32[200,256]{1,0:T(8,128)S(1)}, f32[200,256]{1,0:T(8,128)S(1)}, u32[]{:S(2)}, u32[]{:S(2)}) %collective-permute-start.13) | collective-permute-done | bytes 204832 | tf_op jit(solution)/shard_map/ppermute | solution.py:32
  74.7 2.5 %collective-permute-start.14 = (f32[96,256]{1,0:T(8,128)S(1)}, f32[96,256]{1,0:T(8,128)S(1)}, u32[]{:S(2)}, u32[]{:S(2)}) collective-permute-start(f32[96,256]{1,0:T(8,128)S(1)} %get-tuple-element.38), channel_id=1, source_target_pairs={{0,1},{1,0},{2,3},{3,2},{4,5},{5,4},{6,7},{7,6},{8,9},{9,8},{10,11... | collective-permute-start | bytes 294920 | tf_op jit(solution)/shard_map/ppermute | solution.py:32
  77.2 2.1 %collective-permute-start.15 = (f32[96,256]{1,0:T(8,128)S(1)}, f32[96,256]{1,0:T(8,128)S(1)}, u32[]{:S(2)}, u32[]{:S(2)}) collective-permute-start(f32[96,256]{1,0:T(8,128)S(1)} %get-tuple-element.39), channel_id=1, source_target_pairs={{0,2},{1,3},{2,0},{3,1},{4,6},{5,7},{6,4},{7,5},{8,10},{9,11},{10,... | collective-permute-start | bytes 294920 | tf_op jit(solution)/shard_map/ppermute | solution.py:32
  79.7 19.5 %collective-permute-done.14 = f32[96,256]{1,0:T(8,128)S(1)} collective-permute-done((f32[96,256]{1,0:T(8,128)S(1)}, f32[96,256]{1,0:T(8,128)S(1)}, u32[]{:S(2)}, u32[]{:S(2)}) %collective-permute-start.14) | collective-permute-done | bytes 98336 | tf_op jit(solution)/shard_map/ppermute | solution.py:32
  99.3 3.6 %collective-permute-done.16 = f32[96,256]{1,0:T(8,128)S(1)} collective-permute-done((f32[96,256]{1,0:T(8,128)S(1)}, f32[96,256]{1,0:T(8,128)S(1)}, u32[]{:S(2)}, u32[]{:S(2)}) %collective-permute-start.16) | collective-permute-done | bytes 98336 | tf_op jit(solution)/shard_map/ppermute | solution.py:32
  102.9 1.8 %collective-permute-start.17 = (f32[96,256]{1,0:T(8,128)S(1)}, f32[96,256]{1,0:T(8,128)S(1)}, u32[]{:S(2)}, u32[]{:S(2)}) collective-permute-start(f32[96,256]{1,0:T(8,128)S(1)} %fusion.3), channel_id=1, source_target_pairs={{0,8},{4,12},{8,0},{12,4},{1,9},{5,13},{9,1},{13,5},{2,10},{6,14},... | collective-permute-start | bytes 294920 | tf_op jit(solution)/shard_map/ppermute | solution.py:32
  105.6 2.0 %collective-permute-done.17 = f32[96,256]{1,0:T(8,128)S(1)} collective-permute-done((f32[96,256]{1,0:T(8,128)S(1)}, f32[96,256]{1,0:T(8,128)S(1)}, u32[]{:S(2)}, u32[]{:S(2)}) %collective-permute-start.17) | collective-permute-done | bytes 98336 | tf_op jit(solution)/shard_map/ppermute | solution.py:32
  108.3 0.8 collective-permute-done.18
  109.9 0.7 maximum_multiply_fusion
  110.7 19.9 %collective-permute-done.11 = f16[272,1024]{1,0:T(8,128)(2,1)S(1)} collective-permute-done((f16[272,1024]{1,0:T(8,128)(2,1)S(1)}, f16[272,1024]{1,0:T(8,128)(2,1)S(1)}, u32[]{:S(2)}, u32[]{:S(2)}) %collective-permute-start.11) | collective-permute-done | bytes 557088 | tf_op jit(solution)/shard_map/ppermute | solution.py:32
  130.7 1.5 %final.1 = f32[1024,256]{1,0:T(8,128)} custom-call(f32[256,1024]{1,0:T(8,128)S(1)} %copy-done.5, f32[272,1024]{1,0:T(8,128)S(1)} %convert_element_type.19.near_ref, f32[272,1024]{1,0:T(8,128)S(1)} %convert_element_type.23.far_ref), custom_call_target="tpu_custom_call" | custom-call | flops 2621440 | bytes 4194304 | tf_op jit(solution)/shard_map/final/pallas_call | solution.py:181
  (70 shorter events, 4.6 us)
Async XLA Ops:
  0.7 5.2 %copy-start = (bf16[1024,256]{1,0:T(8,128)(2,1)S(1)}, bf16[1024,256]{1,0:T(8,128)(2,1)}, u32[]{:S(2)}) copy-start(bf16[1024,256]{1,0:T(8,128)(2,1)} %block_ref.1) | copy-start | bytes 1572868
  5.4 37.2 %collective-permute-start = (bf16[2,256,4096]{2,1,0:T(8,128)(2,1)}, bf16[2,256,4096]{2,1,0:T(8,128)(2,1)}, u32[]{:S(2)}, u32[]{:S(2)}) collective-permute-start(bf16[2,256,4096]{2,1,0:T(8,128)(2,1)} %dynamic-slice_bitcast_fusion), channel_id=1, source_target_pairs={{0,4},{4,0},{8,12},{12,8},{1,5},{5,1},{9,13},{13,9},{2,6},{6,2},{1... | collective-permute-start | bytes 12582920 | tf_op jit(solution)/shard_map/ppermute | solution.py:32
  5.9 31.2 %copy-start.7 = (f32[2,256]{1,0:T(2,128)S(1)}, f32[2,256]{1,0:T(2,128)}, u32[]{:S(2)}) copy-start(f32[2,256]{1,0:T(2,128)} %scales_ref.1) | copy-start | bytes 6148
  5.9 13.3 %collective-permute-start.3 = (bf16[512,256]{1,0:T(8,128)(2,1)S(1)}, bf16[512,256]{1,0:T(8,128)(2,1)S(1)}, u32[]{:S(2)}, u32[]{:S(2)}) collective-permute-start(bf16[512,256]{1,0:T(8,128)(2,1)S(1)} %slice.42), channel_id=1, source_target_pairs={{0,3},{16,19}} | collective-permute-start | bytes 786440 | tf_op jit(solution)/shard_map/ppermute | solution.py:262
  12.4 12.4 %collective-permute-start.2 = (bf16[512,256]{1,0:T(8,128)(2,1)S(1)}, bf16[512,256]{1,0:T(8,128)(2,1)S(1)}, u32[]{:S(2)}, u32[]{:S(2)}) collective-permute-start(bf16[512,256]{1,0:T(8,128)(2,1)S(1)} %slice.42), channel_id=1, source_target_pairs={{0,2},{16,18}} | collective-permute-start | bytes 786440 | tf_op jit(solution)/shard_map/ppermute | solution.py:262
  13.8 16.7 %collective-permute-start.1 = (bf16[512,256]{1,0:T(8,128)(2,1)S(1)}, bf16[512,256]{1,0:T(8,128)(2,1)S(1)}, u32[]{:S(2)}, u32[]{:S(2)}) collective-permute-start(bf16[512,256]{1,0:T(8,128)(2,1)S(1)} %slice.42), channel_id=1, source_target_pairs={{0,1},{16,17}} | collective-permute-start | bytes 786440 | tf_op jit(solution)/shard_map/ppermute | solution.py:262
  15.1 23.0 %collective-permute-start.8 = (bf16[1024,256]{1,0:T(8,128)(2,1)S(1)}, bf16[1024,256]{1,0:T(8,128)(2,1)S(1)}, u32[]{:S(2)}, u32[]{:S(2)}) collective-permute-start(bf16[1024,256]{1,0:T(8,128)(2,1)S(1)} %copy-done), channel_id=1, source_target_pairs={{0,2},{1,3},{2,0},{3,1},{4,6},{5,7},{6,4},{7,5},{8,10},{9,11},{10,... | collective-permute-start | bytes 1572872 | tf_op jit(solution)/shard_map/ppermute | solution.py:32
  15.2 22.7 %copy-start.3 = (f32[256,256]{1,0:T(8,128)S(1)}, f32[256,256]{1,0:T(8,128)}, u32[]{:S(2)}) copy-start(f32[256,256]{1,0:T(8,128)} %core_ref.1) | copy-start | bytes 786436
  19.2 39.9 %collective-permute-start.6 = (bf16[1024,256]{1,0:T(8,128)(2,1)S(1)}, bf16[1024,256]{1,0:T(8,128)(2,1)S(1)}, u32[]{:S(2)}, u32[]{:S(2)}) collective-permute-start(bf16[1024,256]{1,0:T(8,128)(2,1)S(1)} %copy-done), channel_id=1, source_target_pairs={{0,1},{1,0},{2,3},{3,2},{4,5},{5,4},{6,7},{7,6},{8,9},{9,8},{10,11... | collective-permute-start | bytes 1572872 | tf_op jit(solution)/shard_map/ppermute | solution.py:32
  30.5 5.2 %collective-permute-start.4 = (bf16[512,256]{1,0:T(8,128)(2,1)S(1)}, bf16[512,256]{1,0:T(8,128)(2,1)S(1)}, u32[]{:S(2)}, u32[]{:S(2)}) collective-permute-start(bf16[512,256]{1,0:T(8,128)(2,1)S(1)} %add_select_fusion), channel_id=1, source_target_pairs={{0,8},{1,9},{2,10},{3,11},{16,24},{17,25},{18,26},{19,27}} | collective-permute-start | bytes 786440 | tf_op jit(solution)/shard_map/ppermute | solution.py:264
  35.7 6.2 %collective-permute-start.5 = (bf16[512,256]{1,0:T(8,128)(2,1)S(1)}, bf16[512,256]{1,0:T(8,128)(2,1)S(1)}, u32[]{:S(2)}, u32[]{:S(2)}) collective-permute-start(bf16[512,256]{1,0:T(8,128)(2,1)S(1)} %broadcast_select_fusion), channel_id=1, source_target_pairs={{0,4},{8,12},{1,5},{9,13},{2,6},{10,14},{3,7},{11,15},{16,20},{24,... | collective-permute-start | bytes 786440 | tf_op jit(solution)/shard_map/ppermute | solution.py:266
  38.1 16.4 %collective-permute-start.9 = (bf16[1024,256]{1,0:T(8,128)(2,1)S(1)}, bf16[1024,256]{1,0:T(8,128)(2,1)S(1)}, u32[]{:S(2)}, u32[]{:S(2)}) collective-permute-start(bf16[1024,256]{1,0:T(8,128)(2,1)S(1)} %collective-permute-done.8.block_ref), channel_id=1, source_target_pairs={{0,1},{1,0},{2,3},{3,2},{4,5},{5,4},{6,7},{7,6},{8,9},{9,8},{10,11... | collective-permute-start | bytes 1572872 | tf_op jit(solution)/shard_map/ppermute | solution.py:32
  47.2 4.5 %copy-start.1 = (f32[256,1024]{1,0:T(8,128)}, f32[256,1024]{1,0:T(8,128)S(1)}, u32[]{:S(2)}) copy-start(f32[256,1024]{1,0:T(8,128)S(1)} %get-tuple-element.21.second_ref) | copy-start | bytes 3145732
  51.7 7.4 %copy-start.4 = (f32[256,1024]{1,0:T(8,128)}, f32[256,1024]{1,0:T(8,128)S(1)}, u32[]{:S(2)}) copy-start(f32[256,1024]{1,0:T(8,128)S(1)} %get-tuple-element.18.own_ref) | copy-start | bytes 3145732
  59.1 4.6 %copy-start.6 = (f32[2,256]{0,1:T(8,128)S(1)}, f32[2,256]{0,1:T(8,128)}, u32[]{:S(2)}) copy-start(f32[2,256]{0,1:T(8,128)} %copy.8) | copy-start | bytes 6148
  65.4 1.8 %collective-permute-start.12 = (f32[392,256]{1,0:T(8,128)S(1)}, f32[392,256]{1,0:T(8,128)S(1)}, u32[]{:S(2)}, u32[]{:S(2)}) collective-permute-start(f32[392,256]{1,0:T(8,128)S(1)} %get-tuple-element.27), channel_id=1, source_target_pairs={{0,4},{4,0},{8,12},{12,8},{1,5},{5,1},{9,13},{13,9},{2,6},{6,2},{1... | collective-permute-start | bytes 1204232 | tf_op jit(solution)/shard_map/ppermute | solution.py:32
  67.4 7.2 %collective-permute-start.13 = (f32[200,256]{1,0:T(8,128)S(1)}, f32[200,256]{1,0:T(8,128)S(1)}, u32[]{:S(2)}, u32[]{:S(2)}) collective-permute-start(f32[200,256]{1,0:T(8,128)S(1)} %pad_maximum_fusion), channel_id=1, source_target_pairs={{0,8},{4,12},{8,0},{12,4},{1,9},{5,13},{9,1},{13,5},{2,10},{6,14},... | collective-permute-start | bytes 614408 | tf_op jit(solution)/shard_map/ppermute | solution.py:32
  67.6 37.1 %collective-permute-start.10 = (f16[272,1024]{1,0:T(8,128)(2,1)S(1)}, f16[272,1024]{1,0:T(8,128)(2,1)S(1)}, u32[]{:S(2)}, u32[]{:S(2)}) collective-permute-start(f16[272,1024]{1,0:T(8,128)(2,1)S(1)} %convert_element_type.20), channel_id=1, source_target_pairs={{0,1},{1,0},{2,3},{3,2},{4,5},{5,4},{6,7},{7,6},{8,9},{9,8},{10,11... | collective-permute-start | bytes 1671176 | tf_op jit(solution)/shard_map/ppermute | solution.py:32
  70.2 35.3 %collective-permute-start.7 = (f16[272,1024]{1,0:T(8,128)(2,1)S(1)}, f16[272,1024]{1,0:T(8,128)(2,1)S(1)}, u32[]{:S(2)}, u32[]{:S(2)}) collective-permute-start(f16[272,1024]{1,0:T(8,128)(2,1)S(1)} %convert_element_type.18), channel_id=1, source_target_pairs={{0,1},{1,0},{2,3},{3,2},{4,5},{5,4},{6,7},{7,6},{8,9},{9,8},{10,11... | collective-permute-start | bytes 1671176 | tf_op jit(solution)/shard_map/ppermute | solution.py:32
  74.7 30.1 %copy-start.2 = (f32[256,1024]{1,0:T(8,128)S(1)}, f32[256,1024]{1,0:T(8,128)}, u32[]{:S(2)}) copy-start(f32[256,1024]{1,0:T(8,128)} %copy-done.1) | copy-start | bytes 3145732
  74.7 24.5 %collective-permute-start.14 = (f32[96,256]{1,0:T(8,128)S(1)}, f32[96,256]{1,0:T(8,128)S(1)}, u32[]{:S(2)}, u32[]{:S(2)}) collective-permute-start(f32[96,256]{1,0:T(8,128)S(1)} %get-tuple-element.38), channel_id=1, source_target_pairs={{0,1},{1,0},{2,3},{3,2},{4,5},{5,4},{6,7},{7,6},{8,9},{9,8},{10,11... | collective-permute-start | bytes 294920 | tf_op jit(solution)/shard_map/ppermute | solution.py:32
  77.2 22.0 %collective-permute-start.15 = (f32[96,256]{1,0:T(8,128)S(1)}, f32[96,256]{1,0:T(8,128)S(1)}, u32[]{:S(2)}, u32[]{:S(2)}) collective-permute-start(f32[96,256]{1,0:T(8,128)S(1)} %get-tuple-element.39), channel_id=1, source_target_pairs={{0,2},{1,3},{2,0},{3,1},{4,6},{5,7},{6,4},{7,5},{8,10},{9,11},{10,... | collective-permute-start | bytes 294920 | tf_op jit(solution)/shard_map/ppermute | solution.py:32
  79.3 23.5 %collective-permute-start.16 = (f32[96,256]{1,0:T(8,128)S(1)}, f32[96,256]{1,0:T(8,128)S(1)}, u32[]{:S(2)}, u32[]{:S(2)}) collective-permute-start(f32[96,256]{1,0:T(8,128)S(1)} %get-tuple-element.40), channel_id=1, source_target_pairs={{0,3},{1,2},{2,1},{3,0},{4,7},{5,6},{6,5},{7,4},{8,11},{9,10},{10,... | collective-permute-start | bytes 294920 | tf_op jit(solution)/shard_map/ppermute | solution.py:32
  102.9 4.7 %collective-permute-start.17 = (f32[96,256]{1,0:T(8,128)S(1)}, f32[96,256]{1,0:T(8,128)S(1)}, u32[]{:S(2)}, u32[]{:S(2)}) collective-permute-start(f32[96,256]{1,0:T(8,128)S(1)} %fusion.3), channel_id=1, source_target_pairs={{0,8},{4,12},{8,0},{12,4},{1,9},{5,13},{9,1},{13,5},{2,10},{6,14},... | collective-permute-start | bytes 294920 | tf_op jit(solution)/shard_map/ppermute | solution.py:32
  105.4 25.2 %collective-permute-start.11 = (f16[272,1024]{1,0:T(8,128)(2,1)S(1)}, f16[272,1024]{1,0:T(8,128)(2,1)S(1)}, u32[]{:S(2)}, u32[]{:S(2)}) collective-permute-start(f16[272,1024]{1,0:T(8,128)(2,1)S(1)} %convert_element_type.22), channel_id=1, source_target_pairs={{0,2},{1,3},{2,0},{3,1},{4,6},{5,7},{6,4},{7,5},{8,10},{9,11},{10,... | collective-permute-start | bytes 1671176 | tf_op jit(solution)/shard_map/ppermute | solution.py:32
  107.7 1.5 %collective-permute-start.18 = (f32[192,256]{1,0:T(8,128)S(1)}, f32[192,256]{1,0:T(8,128)S(1)}, u32[]{:S(2)}, u32[]{:S(2)}) collective-permute-start(f32[192,256]{1,0:T(8,128)S(1)} %pad_maximum_fusion.2), channel_id=1, source_target_pairs={{0,4},{4,0},{8,12},{12,8},{1,5},{5,1},{9,13},{13,9},{2,6},{6,2},{1... | collective-permute-start | bytes 589832 | tf_op jit(solution)/shard_map/ppermute | solution.py:32
  109.9 20.8 %copy-start.5 = (f32[256,1024]{1,0:T(8,128)S(1)}, f32[256,1024]{1,0:T(8,128)}, u32[]{:S(2)}) copy-start(f32[256,1024]{1,0:T(8,128)} %copy-done.4) | copy-start | bytes 3145732

commit v2 on v1

--- a/solution.py
+++ b/solution.py
@@ -14,6 +14,8 @@
 NT = (((1,), (1,)), ((), ()))
 TN = (((0,), (0,)), ((), ()))
 VMEM_LIMIT = 48 * 2**20
+LARGE = pl.CostEstimate(flops=10**11, bytes_accessed=10**8, transcendentals=0)
+SMALL = pl.CostEstimate(flops=1000, bytes_accessed=1000, transcendentals=0)
 
 
 def dot(a, b, dims, **more):
@@ -60,11 +62,32 @@
         ],
         out_specs=[pl.BlockSpec(memory_space=pltpu.VMEM)] * 2,
         compiler_params=pltpu.CompilerParams(vmem_limit_bytes=VMEM_LIMIT),
-        cost_estimate=pl.CostEstimate(
-            flops=6 * months * size * P_SIZE * P_SIZE, bytes_accessed=2 * 2**20, transcendentals=0
-        ),
+        cost_estimate=SMALL,
         name="mapped",
     )(core_at, window, inner)
+
+
+def half_kernel(at_ref, trade_ref, out_ref):
+    out_ref[...] = trade_ref[:, 0]
+
+
+def half_call(at, trade, half):
+    months, rows = trade.shape[0], trade.shape[2]
+    width = min(1024, half)
+    steps = half // width
+    return pl.pallas_call(
+        half_kernel,
+        grid_spec=pltpu.PrefetchScalarGridSpec(
+            num_scalar_prefetch=1,
+            grid=(steps,),
+            in_specs=[pl.BlockSpec((months, 1, rows, width), lambda j, s: (0, 0, 0, s[0] * steps + j))],
+            out_specs=pl.BlockSpec((months, rows, width), lambda j, s: (0, 0, j)),
+        ),
+        out_shape=jax.ShapeDtypeStruct((months, rows, half), trade.dtype),
+        compiler_params=pltpu.CompilerParams(vmem_limit_bytes=VMEM_LIMIT),
+        cost_estimate=SMALL,
+        name="half",
+    )(at, trade)
 
 
 def encoded(value):
@@ -73,26 +96,25 @@
     return value * jnp.exp2(15.0 - exponent), jnp.broadcast_to(exponent, (16, value.shape[1]))
 
 
-def piece_kernel(scaled, at_ref, own_ref, other_ref, block_ref, mapped_ref, turned_ref, grad_ref, proj_ref):
-    step = pl.program_id(0)
-    block = block_ref[...]
-    months, size = mapped_ref.shape[0], mapped_ref.shape[1]
-    rows = size // 2
-    model = dot(mapped_ref[...].reshape(months * size, P_SIZE), block, NT)
+def piece_kernel(scaled, at_ref, own_ref, other_ref, first_ref, second_ref, mapped_ref, turned_ref, grad_ref, proj_ref):
+    step, width = pl.program_id(0), own_ref.shape[3]
+    block = jnp.where(step == 0, first_ref[...], second_ref[...])
+    months, rows = mapped_ref.shape[0], mapped_ref.shape[1] // 2
     parts = []
     for month in range(months):
         for band in range(2):
             flows = own_ref[month, 0] if band == 0 else other_ref[month]
-            at = (2 * month + band) * rows
-            parts.append((flows.astype(F32) - model[at : at + rows]).astype(BF16))
+            model = dot(mapped_ref[month, band * rows : (band + 1) * rows, :], block, NT)
+            parts.append((flows.astype(F32) - model).astype(BF16))
     residual = jnp.concatenate(parts, 0)
     grad = dot(turned_ref[...], residual, NN)
+    at = pl.multiple_of(step * width, width)
     if scaled:
         value, exponent = encoded(grad)
-        grad_ref[:P_SIZE, :] = value
-        grad_ref[P_SIZE:, :] = exponent
+        grad_ref[:P_SIZE, pl.ds(at, width)] = value
+        grad_ref[P_SIZE:, pl.ds(at, width)] = exponent
     else:
-        grad_ref[...] = grad
+        grad_ref[:, pl.ds(at, width)] = grad
     projected = dot(residual, block, NN).reshape(proj_ref.shape)
 
     @pl.when(step == 0)
@@ -104,90 +126,55 @@
         proj_ref[...] += projected
 
 
-def piece_call(at, trade, other, block, mapped, turned, scaled, label):
+def piece_call(at, trade, other, blocks, mapped, turned, scaled, cost, label):
     months, size = mapped.shape[0], mapped.shape[1]
-    rows, columns = size // 2, block.shape[0]
-    width = min(512, columns)
-    steps = columns // width
-    high = P_SIZE + 16 if scaled else P_SIZE
+    rows, width = size // 2, blocks[0].shape[0]
+    vmem = pl.BlockSpec(memory_space=pltpu.VMEM)
     spec = pltpu.PrefetchScalarGridSpec(
         num_scalar_prefetch=1,
-        grid=(steps,),
+        grid=(2,),
         in_specs=[
-            pl.BlockSpec((months, 1, rows, width), lambda j, s: (0, 0, 0, s[0] * steps + j)),
-            pl.BlockSpec((months, rows, width), lambda j, s: (0, 0, s[1] * steps + j)),
-            pl.BlockSpec((width, P_SIZE), lambda j, s: (j, 0)),
-            pl.BlockSpec((months, size, P_SIZE), lambda j, s: (0, 0, 0)),
-            pl.BlockSpec((P_SIZE, months * size), lambda j, s: (0, 0)),
-        ],
-        out_specs=[
-            pl.BlockSpec((high, width), lambda j, s: (0, j)),
-            pl.BlockSpec((months, size, P_SIZE), lambda j, s: (0, 0, 0)),
-        ],
+            pl.BlockSpec((months, 1, rows, width), lambda j, s: (0, 0, 0, s[0] * 2 + j)),
+            pl.BlockSpec((months, rows, width), lambda j, s: (0, 0, s[1] * 2 + j)),
+        ]
+        + [vmem] * 4,
+        out_specs=[vmem, vmem],
     )
     return pl.pallas_call(
         functools.partial(piece_kernel, scaled),
         grid_spec=spec,
         out_shape=[
-            jax.ShapeDtypeStruct((high, columns), F32),
+            jax.ShapeDtypeStruct((P_SIZE + 16 if scaled else P_SIZE, 2 * width), F32),
             jax.ShapeDtypeStruct((months, size, P_SIZE), F32),
         ],
         compiler_params=pltpu.CompilerParams(vmem_limit_bytes=VMEM_LIMIT),
-        cost_estimate=pl.CostEstimate(
-            flops=6 * months * size * columns * P_SIZE,
-            bytes_accessed=2 * months * size * columns + 4 * 2**20,
-            transcendentals=0,
-        ),
+        cost_estimate=cost,
         name=label,
-    )(at, trade, other, block, mapped, turned)
-
-
-def relay_kernel(first_ref, second_ref, out_ref):
-    received = first_ref[:P_SIZE, :] * jnp.exp2(first_ref[P_SIZE : P_SIZE + 1, :] - 15.0)
-    value, exponent = encoded(received + second_ref[...])
-    out_ref[:P_SIZE, :] = value
-    out_ref[P_SIZE:, :] = exponent
-
-
-def relay_call(received, own):
-    columns = own.shape[1]
-    width = columns // 2
-    return pl.pallas_call(
-        relay_kernel,
-        grid=(2,),
-        in_specs=[
-            pl.BlockSpec((P_SIZE + 16, width), lambda j: (0, j)),
-            pl.BlockSpec((P_SIZE, width), lambda j: (0, j)),
-        ],
-        out_specs=pl.BlockSpec((P_SIZE + 16, width), lambda j: (0, j)),
-        out_shape=jax.ShapeDtypeStruct((P_SIZE + 16, columns), F32),
-        compiler_params=pltpu.CompilerParams(vmem_limit_bytes=VMEM_LIMIT),
-        cost_estimate=pl.CostEstimate(flops=10 * P_SIZE * columns, bytes_accessed=3 * 2**20, transcendentals=0),
-        name="relay",
-    )(received, own)
-
-
-def final_kernel(coef, own_ref, near_ref, far_ref, out_ref):
+    )(at, trade, other, *blocks, mapped, turned)
+
+
+def final_kernel(coef, own_ref, *rest):
+    received, out_ref = rest[:-1], rest[-1]
     total = own_ref[...]
-    for ref in (near_ref, far_ref):
+    for ref in received:
         total = total + ref[:P_SIZE, :] * jnp.exp2(ref[P_SIZE : P_SIZE + 1, :] - 15.0)
     out_ref[...] = (-coef * total).T
 
 
-def final_call(coef, own, near, far):
+def final_call(coef, own, received):
     columns = own.shape[1]
     width = columns // 2
     tall = pl.BlockSpec((P_SIZE + 16, width), lambda j: (0, j))
     return pl.pallas_call(
         functools.partial(final_kernel, coef),
         grid=(2,),
-        in_specs=[pl.BlockSpec((P_SIZE, width), lambda j: (0, j)), tall, tall],
+        in_specs=[pl.BlockSpec((P_SIZE, width), lambda j: (0, j))] + [tall] * len(received),
         out_specs=pl.BlockSpec((width, P_SIZE), lambda j: (j, 0)),
         out_shape=jax.ShapeDtypeStruct((columns, P_SIZE), F32),
         compiler_params=pltpu.CompilerParams(vmem_limit_bytes=VMEM_LIMIT),
-        cost_estimate=pl.CostEstimate(flops=10 * P_SIZE * columns, bytes_accessed=4 * 2**20, transcendentals=0),
+        cost_estimate=SMALL,
         name="final",
-    )(own, near, far)
+    )(own, *received)
 
 
 def terms_kernel(cuts, at_ref, window_ref, inner_ref, core_ref, scales_ref, columns_ref, *rest):
@@ -241,9 +228,7 @@
         out_shape=[jax.ShapeDtypeStruct((high, P_SIZE), F32)] * 2,
         scratch_shapes=[pltpu.VMEM((size + P_SIZE, P_SIZE), F32)],
         compiler_params=pltpu.CompilerParams(vmem_limit_bytes=VMEM_LIMIT),
-        cost_estimate=pl.CostEstimate(
-            flops=18 * months * size * P_SIZE * P_SIZE, bytes_accessed=6 * 2**20, transcendentals=0
-        ),
+        cost_estimate=SMALL,
         name="terms",
     )(core_at, window, inner, core, scales, scales.T, *projs)
 
@@ -257,37 +242,43 @@
     coef = 1.0 / math.sqrt(months * cuts * size)
     core_at = at.astype(jnp.int32).reshape(1)
     inner = scales[:, :, None] * core[None] * scales[:, None, :]
-
-    head = factor[:size]
-    sent = [lax.ppermute(head, ("tile", "cuts"), [(0, target)]) for target in range(1, cuts)]
-    line = jnp.where(cut == 0, head, sum(sent[1:], sent[0]))
-    across = lax.ppermute(line, "tile", [(0, 2)])
-    even = jnp.where(x == 0, line, across)
-    window = jnp.where(at == 0, even, lax.ppermute(even, "tile", [(0, 1), (2, 3)]))
-
-    near = swapped(factor, "cuts", 1)
-    middle = swapped(factor, "cuts", 2)
-    far = swapped(middle, "cuts", 1)
+    hold = lax.optimization_barrier
 
     half = cuts * piece
-    give = lax.dynamic_slice_in_dim(trade[:, 0], (1 - at) * half, half, 2)
+    give = half_call((1 - at).astype(jnp.int32).reshape(1), trade, half)
     other = swapped(give, "tile", 1)
 
+    parts = [factor[:size], factor[size:]]
+    third = lax.ppermute(parts[0], ("tile", "cuts"), [(0, 3)])
+    middle = [swapped(value, "cuts", 2) for value in parts]
+    near = [swapped(value, "cuts", 1) for value in parts]
+    line = jnp.where(cut == 0, parts[0], jnp.where(cut == 1, near[0], jnp.where(cut == 2, middle[0], third)))
+    out = [lax.ppermute(line, "tile", [(0, target)]) for target in (1, 2, 3)]
+    out, middle[1] = hold((out, middle[1]))
+    far = [swapped(value, "cuts", 1) for value in middle]
+    window = jnp.where(tile == 0, line, sum(out[1:], out[0]))
     mapped, turned = mapped_call(core_at, window, inner)
 
-    def piece_of(which, block, scaled, label):
+    def piece_of(which, block, scaled, cost, label, after=None):
         where = jnp.stack([at * cuts + which, which]).astype(jnp.int32)
-        return piece_call(where, trade, other, block, mapped, turned, scaled, label)
-
-    grad_near, proj_near = piece_of(cut ^ 1, near, True, "piece_near")
-    from_near = swapped(grad_near.astype(F16), "cuts", 1)
-    grad_own, proj_own = piece_of(cut, factor, False, "piece_own")
-    grad_middle, proj_middle = piece_of(cut ^ 2, middle, False, "piece_middle")
-    grad_far, proj_far = piece_of(cut ^ 3, far, True, "piece_far")
-    joined = swapped(grad_far.astype(F16), "cuts", 1)
+        if after is not None:
+            where, _ = hold((where, after))
+        return piece_call(where, trade, other, block, mapped, turned, scaled, cost, label)
+
+    grad_middle, proj_middle = piece_of(cut ^ 2, middle, True, SMALL, "piece_middle")
+    grad_middle = grad_middle.astype(F16)
+    from_middle = swapped(grad_middle, "cuts", 2)
+    grad_own, proj_own = piece_of(cut, parts, False, LARGE, "piece_own", grad_middle)
+    grad_far, proj_far = piece_of(cut ^ 3, far, True, SMALL, "piece_far", proj_own)
+    grad_far = grad_far.astype(F16)
+    from_far = swapped(grad_far, "cuts", 3)
+    grad_near, proj_near = piece_of(cut ^ 1, near, True, SMALL, "piece_near", grad_far)
+    grad_near = grad_near.astype(F16)
+    from_near = swapped(grad_near, "cuts", 1)
 
     keep, send = terms_call(cuts, core_at, window, inner, core, scales, [proj_near, proj_own, proj_middle, proj_far])
-    both = keep + swapped(send, "tile", 1)
+    send, from_middle = hold((swapped(send, "tile", 1), from_middle))
+    both = keep + send
     w, q = size // (4 * cuts), P_SIZE // 4
     part = cuts * w + q
     low, high, diagonal = both[:part], both[part : 2 * part], both[2 * part :]
@@ -313,9 +304,8 @@
     grad_window = jnp.concatenate([first[: 2 * w], second[: 2 * w]], 0)
     grad_core = jnp.concatenate([first[2 * w :], second[2 * w :]], 0)
 
-    passed = relay_call(joined.astype(F32), grad_middle)
-    from_far = swapped(passed.astype(F16), "cuts", 2)
-    grad_factor = final_call(coef, grad_own, from_near.astype(F32), from_far.astype(F32))
+    received = [value.astype(F32) for value in (from_near, from_middle, from_far)]
+    grad_factor = final_call(coef, grad_own, received)
     return (grad_factor, -coef * grad_window, -coef * grad_core, -coef * diagonal)
 
 
@@ -378,7 +368,7 @@
 
 def body(trade, factor, scales, core):
     line = lax.axis_size("cuts") == 4 and lax.axis_size("tile") == 4
-    if line and factor.shape[0] >= 2 * trade.shape[2]:
+    if line and factor.shape[0] == 4 * trade.shape[2]:
         return body_line(trade, factor, scales, core)
     return body_any(trade, factor, scales, core)
 

time: 133 us -> 119 us (0.89)
  waiting for transfers between devices: 73.6 us -> 50.5 us
  other arithmetic: 3.26 us -> 8.8 us
  local copies, waits for them, and re-layouts: 5.72 us -> 0.26 us
  starting transfers between devices: 25.8 us -> 31.2 us
  Pallas kernels: 22.7 us -> 26.3 us
    ppermute x5 -> x4, waiting for transfers between devices: 18.9 us -> 1.82 us  [the longest x1 1.81 us: body_line(): third = lax.ppermute(parts[0], ('tile', 'cuts'), [(0, 3)])]
    ppermute x14 -> x17, starting transfers between devices: 14 us -> 25.4 us  [swapped(): return lax.ppermute(value, axis, pairs)]
    ppermute x14 -> x17, waiting for transfers between devices: 54.7 us -> 48.7 us  [swapped(): return lax.ppermute(value, axis, pairs)]
    ppermute x5 -> x4, starting transfers between devices: 11.7 us -> 5.79 us  [the longest x3 3.92 us: body_line(): out = [lax.ppermute(line, 'tile', [(0, target)]) for target in (1, 2, 3)]]
    dynamic_slice x1 -> x0, local copies, waits for them, and re-layouts: 4.77 us -> none  [body_line(): give = lax.dynamic_slice_in_dim(trade[:, 0], (1 - at) * half, half, 2)]
    convert_element_type x6, other arithmetic: 0.49 us -> 5.05 us  [the longest x3 2.35 us: body_line(): value.astype(F32)]
    pallas_call x1, Pallas kernels: 0.57 us -> 4.95 us  [half_call(): pl.pallas_call(half_kernel, grid_spec=pltpu.PrefetchScalarGridSpec(num_sc...]
    pallas_call x4, Pallas kernels: 18.2 us -> 16.5 us  [piece_call(): pl.pallas_call(functools.partial(piece_kernel, scaled), grid_spec=spec, o...]
  transfers between devices with their start and end apart: 19 -> 21, of which waited for: 13 -> 11; matrix products, arithmetic and copies ran while one was open for 3% -> 5% of each run, Pallas kernels for 11% -> 18%
where the time goes in v2:
time: 119 us; the launch traced here: 118 us
  waiting for transfers between devices  50.5 us (42%)
  starting transfers between devices  31.2 us (26%)
  Pallas kernels  26.3 us (22%)
  other arithmetic  8.8 us (7%)
    ppermute x17, waiting for transfers between devices, swapped(): return lax.ppermute(value, axis, pairs)  48.7 us
    ppermute x17, starting transfers between devices, swapped(): return lax.ppermute(value, axis, pairs)  25.4 us
    pallas_call x4, Pallas kernels, piece_call(): pl.pallas_call(functools.partial(piece_kernel, scaled), grid_spec=spec, o...  16.5 us
    pallas_call x1, Pallas kernels, half_call(): pl.pallas_call(half_kernel, grid_spec=pltpu.PrefetchScalarGridSpec(num_sc...  4.95 us
    ppermute x3, starting transfers between devices, body_line(): out = [lax.ppermute(line, 'tile', [(0, target)]) for target in (1, 2, 3)]  3.92 us
    pallas_call x1, Pallas kernels, terms_call(): pl.pallas_call(functools.partial(terms_kernel, cuts), in_specs=[pl.BlockS...  2.51 us
  transfers between devices with their start and end apart: 21, of which 11 were waited for; matrix products, arithmetic and copies ran while one was open for 5% of the time, Pallas kernels for 18%

profile of v2, /device:TPU:0, one launch (start us, length us, event | category | flops | bytes accessed | tf_op | source)
XLA Modules:
  0.0 118.1 jit_solution(15391501550618312738)
XLA Ops:
  0.7 5.0 %half.1 = bf16[2,256,4096]{2,1,0:T(8,128)(2,1)} custom-call(s32[1]{0:T(128)} %bitcast.4.at_ref, bf16[2,1,256,8192]{3,2,1,0:T(8,128)(2,1)} %own_ref.7), custom_call_target="tpu_custom_call" | custom-call | flops 1000 | bytes 1000 | tf_op jit(solution)/shard_map/half/pallas_call | solution.py:78
  6.1 3.7 %collective-permute-start.1 = (bf16[512,256]{1,0:T(8,128)(2,1)S(1)}, bf16[512,256]{1,0:T(8,128)(2,1)S(1)}, u32[]{:S(2)}, u32[]{:S(2)}) collective-permute-start(bf16[512,256]{1,0:T(8,128)(2,1)S(1)} %slice.45.first_ref), channel_id=1, source_target_pairs={{0,2},{1,3},{2,0},{3,1},{4,6},{5,7},{6,4},{7,5},{8,10},{9,11},{10,... | collective-permute-start | bytes 786440 | tf_op jit(solution)/shard_map/ppermute | solution.py:34
  9.8 1.6 %collective-permute-start.2 = (bf16[512,256]{1,0:T(8,128)(2,1)S(1)}, bf16[512,256]{1,0:T(8,128)(2,1)S(1)}, u32[]{:S(2)}, u32[]{:S(2)}) collective-permute-start(bf16[512,256]{1,0:T(8,128)(2,1)S(1)} %slice.45.first_ref), channel_id=1, source_target_pairs={{0,1},{1,0},{2,3},{3,2},{4,5},{5,4},{6,7},{7,6},{8,9},{9,8},{10,11... | collective-permute-start | bytes 786440 | tf_op jit(solution)/shard_map/ppermute | solution.py:34
  11.3 1.9 %collective-permute-start.3 = (bf16[512,256]{1,0:T(8,128)(2,1)S(1)}, bf16[512,256]{1,0:T(8,128)(2,1)S(1)}, u32[]{:S(2)}, u32[]{:S(2)}) collective-permute-start(bf16[512,256]{1,0:T(8,128)(2,1)S(1)} %slice.45.first_ref), channel_id=1, source_target_pairs={{0,3},{16,19}} | collective-permute-start | bytes 786440 | tf_op jit(solution)/shard_map/ppermute | solution.py:252
  13.5 9.0 %collective-permute-done.1.first_ref = bf16[512,256]{1,0:T(8,128)(2,1)S(1)} collective-permute-done((bf16[512,256]{1,0:T(8,128)(2,1)S(1)}, bf16[512,256]{1,0:T(8,128)(2,1)S(1)}, u32[]{:S(2)}, u32[]{:S(2)}) %collective-permute-start.1) | collective-permute-done | bytes 262176 | tf_op jit(solution)/shard_map/ppermute | solution.py:34
  22.6 1.8 %collective-permute-done.3 = bf16[512,256]{1,0:T(8,128)(2,1)S(1)} collective-permute-done((bf16[512,256]{1,0:T(8,128)(2,1)S(1)}, bf16[512,256]{1,0:T(8,128)(2,1)S(1)}, u32[]{:S(2)}, u32[]{:S(2)}) %collective-permute-start.3) | collective-permute-done | bytes 262176 | tf_op jit(solution)/shard_map/ppermute | solution.py:252
  24.5 1.3 %collective-permute-start.4 = (bf16[512,256]{1,0:T(8,128)(2,1)S(1)}, bf16[512,256]{1,0:T(8,128)(2,1)S(1)}, u32[]{:S(2)}, u32[]{:S(2)}) collective-permute-start(bf16[512,256]{1,0:T(8,128)(2,1)S(1)} %get-tuple-element.47), channel_id=1, source_target_pairs={{0,4},{1,5},{2,6},{3,7},{16,20},{17,21},{18,22},{19,23}} | collective-permute-start | bytes 786440 | tf_op jit(solution)/shard_map/ppermute | solution.py:256
  25.8 1.3 %collective-permute-start.5 = (bf16[512,256]{1,0:T(8,128)(2,1)S(1)}, bf16[512,256]{1,0:T(8,128)(2,1)S(1)}, u32[]{:S(2)}, u32[]{:S(2)}) collective-permute-start(bf16[512,256]{1,0:T(8,128)(2,1)S(1)} %get-tuple-element.47), channel_id=1, source_target_pairs={{0,8},{1,9},{2,10},{3,11},{16,24},{17,25},{18,26},{19,27}} | collective-permute-start | bytes 786440 | tf_op jit(solution)/shard_map/ppermute | solution.py:256
  27.2 1.3 %collective-permute-start.6 = (bf16[512,256]{1,0:T(8,128)(2,1)S(1)}, bf16[512,256]{1,0:T(8,128)(2,1)S(1)}, u32[]{:S(2)}, u32[]{:S(2)}) collective-permute-start(bf16[512,256]{1,0:T(8,128)(2,1)S(1)} %get-tuple-element.47), channel_id=1, source_target_pairs={{0,12},{1,13},{2,14},{3,15},{16,28},{17,29},{18,30},{19,31}} | collective-permute-start | bytes 786440 | tf_op jit(solution)/shard_map/ppermute | solution.py:256
  28.5 1.1 collective-permute-start.7
  30.0 3.9 %collective-permute-start.10 = (bf16[512,256]{1,0:T(8,128)(2,1)S(1)}, bf16[512,256]{1,0:T(8,128)(2,1)S(1)}, u32[]{:S(2)}, u32[]{:S(2)}) collective-permute-start(bf16[512,256]{1,0:T(8,128)(2,1)S(1)} %get-tuple-element.46.second_ref), channel_id=1, source_target_pairs={{0,1},{1,0},{2,3},{3,2},{4,5},{5,4},{6,7},{7,6},{8,9},{9,8},{10,11... | collective-permute-start | bytes 786440 | tf_op jit(solution)/shard_map/ppermute | solution.py:34
  33.9 5.8 %collective-permute-done.7.second_ref = bf16[512,256]{1,0:T(8,128)(2,1)S(1)} collective-permute-done((bf16[512,256]{1,0:T(8,128)(2,1)S(1)}, bf16[512,256]{1,0:T(8,128)(2,1)S(1)}, u32[]{:S(2)}, u32[]{:S(2)}) %collective-permute-start.7) | collective-permute-done | bytes 262176 | tf_op jit(solution)/shard_map/ppermute | solution.py:34
  41.4 4.2 %piece_middle.1 = (f32[272,1024]{1,0:T(8,128)S(1)}, f32[2,512,256]{2,1,0:T(8,128)S(1)}) custom-call(s32[2]{0:T(128)S(1)} %pad_add_fusion.1.at_ref, bf16[2,1,256,8192]{3,2,1,0:T(8,128)(2,1)} %own_ref.7, bf16[2,256,4096]{2,1,0:T(8,128)(2,1)} %collective-permute-done.other_ref, bf16[512,256]{1,0:T(8,128)(2,1)S(1)} %collective-permute-done.1.first_ref, ...), custom_call_target="tpu_custom_call" | custom-call | flops 1000 | bytes 1000 | tf_op jit(solution)/shard_map/piece_middle/pallas_call | solution.py:143
  46.5 2.2 %collective-permute-start.13 = (f16[272,1024]{1,0:T(8,128)(2,1)}, f16[272,1024]{1,0:T(8,128)(2,1)}, u32[]{:S(2)}, u32[]{:S(2)}) collective-permute-start(f16[272,1024]{1,0:T(8,128)(2,1)} %convert_element_type.18), channel_id=1, source_target_pairs={{0,2},{1,3},{2,0},{3,1},{4,6},{5,7},{6,4},{7,5},{8,10},{9,11},{10,... | collective-permute-start | bytes 1671176 | tf_op jit(solution)/shard_map/ppermute | solution.py:34
  48.7 4.0 %piece_own.1 = (f32[256,1024]{1,0:T(8,128)S(1)}, f32[2,512,256]{2,1,0:T(8,128)S(1)}) custom-call(s32[2]{0:T(128)S(1)} %pad_add_fusion.at_ref, bf16[2,1,256,8192]{3,2,1,0:T(8,128)(2,1)} %own_ref.7, bf16[2,256,4096]{2,1,0:T(8,128)(2,1)} %collective-permute-done.other_ref, bf16[512,256]{1,0:T(8,128)(2,1)S(1)} %slice.45.first_ref, ...), custom_call_target="tpu_custom_call" | custom-call | flops 99999997952 | bytes 100000000 | tf_op jit(solution)/shard_map/piece_own/pallas_call | solution.py:143
  52.7 5.0 %collective-permute-done.9.second_ref = bf16[512,256]{1,0:T(8,128)(2,1)S(1)} collective-permute-done((bf16[512,256]{1,0:T(8,128)(2,1)S(1)}, bf16[512,256]{1,0:T(8,128)(2,1)S(1)}, u32[]{:S(2)}, u32[]{:S(2)}) %collective-permute-start.9) | collective-permute-done | bytes 262176 | tf_op jit(solution)/shard_map/ppermute | solution.py:34
  57.7 4.2 %piece_far.1 = (f32[272,1024]{1,0:T(8,128)S(1)}, f32[2,512,256]{2,1,0:T(8,128)S(1)}) custom-call(s32[2]{0:T(128)S(1)} %pad_add_fusion.3.at_ref, bf16[2,1,256,8192]{3,2,1,0:T(8,128)(2,1)} %own_ref.7, bf16[2,256,4096]{2,1,0:T(8,128)(2,1)} %collective-permute-done.other_ref, bf16[512,256]{1,0:T(8,128)(2,1)S(1)} %collective-permute-done.8.first_ref, ...), custom_call_target="tpu_custom_call" | custom-call | flops 1000 | bytes 1000 | tf_op jit(solution)/shard_map/piece_far/pallas_call | solution.py:143
  62.8 4.2 %piece_near.1 = (f32[272,1024]{1,0:T(8,128)S(1)}, f32[2,512,256]{2,1,0:T(8,128)S(1)}) custom-call(s32[2]{0:T(128)S(1)} %pad_add_fusion.2.at_ref, bf16[2,1,256,8192]{3,2,1,0:T(8,128)(2,1)} %own_ref.7, bf16[2,256,4096]{2,1,0:T(8,128)(2,1)} %collective-permute-done.other_ref, bf16[512,256]{1,0:T(8,128)(2,1)S(1)} %collective-permute-done.2.first_ref, ...), custom_call_target="tpu_custom_call" | custom-call | flops 1000 | bytes 1000 | tf_op jit(solution)/shard_map/piece_near/pallas_call | solution.py:143
  66.9 2.5 %terms.1 = (f32[392,256]{1,0:T(8,128)S(1)}, f32[392,256]{1,0:T(8,128)}) custom-call(s32[1]{0:T(128)} %bitcast.5.core_ref.at_ref, bf16[512,256]{1,0:T(8,128)(2,1)S(1)} %add_select_fusion.window_ref, f32[2,256,256]{2,1,0:T(8,128)S(1)} %multiply_multiply_fusion.inner_ref, f32[256,256]{1,0:T(8,128)S(1)} %copy-done, f32[2,256]{1,0:T(2,128)S(1)} %copy-done.1, ...), custom_call_target="tpu_custom_call" | custom-call | flops 1000 | bytes 1000 | tf_op jit(solution)/shard_map/terms/pallas_call | solution.py:224
  69.5 2.1 %collective-permute-done.12 = f32[392,256]{1,0:T(8,128)} collective-permute-done((f32[392,256]{1,0:T(8,128)}, f32[392,256]{1,0:T(8,128)}, u32[]{:S(2)}, u32[]{:S(2)}) %collective-permute-start.12) | collective-permute-done | bytes 401440 | tf_op jit(solution)/shard_map/ppermute | solution.py:34
  71.5 1.1 add.57
  72.7 3.5 %collective-permute-start.15 = (f32[200,256]{1,0:T(8,128)S(1)}, f32[200,256]{1,0:T(8,128)S(1)}, u32[]{:S(2)}, u32[]{:S(2)}) collective-permute-start(f32[200,256]{1,0:T(8,128)S(1)} %pad_maximum_fusion), channel_id=1, source_target_pairs={{0,8},{4,12},{8,0},{12,4},{1,9},{5,13},{9,1},{13,5},{2,10},{6,14},... | collective-permute-start | bytes 614408 | tf_op jit(solution)/shard_map/ppermute | solution.py:34
  76.2 2.3 %collective-permute-start.14 = (f16[272,1024]{1,0:T(8,128)(2,1)S(1)}, f16[272,1024]{1,0:T(8,128)(2,1)}, u32[]{:S(2)}, u32[]{:S(2)}) collective-permute-start(f16[272,1024]{1,0:T(8,128)(2,1)S(1)} %copy-done.3), channel_id=1, source_target_pairs={{0,3},{1,2},{2,1},{3,0},{4,7},{5,6},{6,5},{7,4},{8,11},{9,10},{10,... | collective-permute-start | bytes 1671176 | tf_op jit(solution)/shard_map/ppermute | solution.py:34
  79.4 1.2 collective-permute-done.15
  80.7 2.9 %collective-permute-start.18 = (f32[96,256]{1,0:T(8,128)S(1)}, f32[96,256]{1,0:T(8,128)S(1)}, u32[]{:S(2)}, u32[]{:S(2)}) collective-permute-start(f32[96,256]{1,0:T(8,128)S(1)} %get-tuple-element.60), channel_id=1, source_target_pairs={{0,3},{1,2},{2,1},{3,0},{4,7},{5,6},{6,5},{7,4},{8,11},{9,10},{10,... | collective-permute-start | bytes 294920 | tf_op jit(solution)/shard_map/ppermute | solution.py:34
  83.6 1.6 %collective-permute-start.16 = (f32[96,256]{1,0:T(8,128)S(1)}, f32[96,256]{1,0:T(8,128)S(1)}, u32[]{:S(2)}, u32[]{:S(2)}) collective-permute-start(f32[96,256]{1,0:T(8,128)S(1)} %get-tuple-element.58), channel_id=1, source_target_pairs={{0,1},{1,0},{2,3},{3,2},{4,5},{5,4},{6,7},{7,6},{8,9},{9,8},{10,11... | collective-permute-start | bytes 294920 | tf_op jit(solution)/shard_map/ppermute | solution.py:34
  85.1 22.6 %collective-permute-done.18 = f32[96,256]{1,0:T(8,128)S(1)} collective-permute-done((f32[96,256]{1,0:T(8,128)S(1)}, f32[96,256]{1,0:T(8,128)S(1)}, u32[]{:S(2)}, u32[]{:S(2)}) %collective-permute-start.18) | collective-permute-done | bytes 98336 | tf_op jit(solution)/shard_map/ppermute | solution.py:34
  107.7 1.4 %collective-permute-done.17 = f32[96,256]{1,0:T(8,128)S(1)} collective-permute-done((f32[96,256]{1,0:T(8,128)S(1)}, f32[96,256]{1,0:T(8,128)S(1)}, u32[]{:S(2)}, u32[]{:S(2)}) %collective-permute-start.17) | collective-permute-done | bytes 98336 | tf_op jit(solution)/shard_map/ppermute | solution.py:34
  109.8 1.2 %collective-permute-start.19 = (f32[96,256]{1,0:T(8,128)S(1)}, f32[96,256]{1,0:T(8,128)S(1)}, u32[]{:S(2)}, u32[]{:S(2)}) collective-permute-start(f32[96,256]{1,0:T(8,128)S(1)} %fusion.3), channel_id=1, source_target_pairs={{0,8},{4,12},{8,0},{12,4},{1,9},{5,13},{9,1},{13,5},{2,10},{6,14},... | collective-permute-start | bytes 294920 | tf_op jit(solution)/shard_map/ppermute | solution.py:34
  111.0 1.1 convert_element_type.22.rest_1_
  112.3 1.1 convert_element_type.23.rest_2_
  113.4 1.6 %final.1 = f32[1024,256]{1,0:T(8,128)} custom-call(f32[256,1024]{1,0:T(8,128)S(1)} %get-tuple-element.33.own_ref, f32[272,1024]{1,0:T(8,128)S(1)} %convert_element_type.21.rest_0_, f32[272,1024]{1,0:T(8,128)S(1)} %convert_element_type.22.rest_1_, f32[272,1024]{1,0:T(8,128)S(1)} %convert_element_type.23.rest_2_), custom_call_target="tpu_custom_call" | custom-call | flops 1000 | bytes 1000 | tf_op jit(solution)/shard_map/final/pallas_call | solution.py:168
  (64 shorter events, 9.7 us)
Async XLA Ops:
  0.6 5.4 %copy-start.2 = (bf16[1024,256]{1,0:T(8,128)(2,1)S(1)}, bf16[1024,256]{1,0:T(8,128)(2,1)}, u32[]{:S(2)}) copy-start(bf16[1024,256]{1,0:T(8,128)(2,1)} %param.5) | copy-start | bytes 1572868
  5.6 24.0 %copy-start.1 = (f32[2,256]{1,0:T(2,128)S(1)}, f32[2,256]{1,0:T(2,128)}, u32[]{:S(2)}) copy-start(f32[2,256]{1,0:T(2,128)} %scales_ref.1) | copy-start | bytes 6148
  5.6 35.8 %collective-permute-start = (bf16[2,256,4096]{2,1,0:T(8,128)(2,1)}, bf16[2,256,4096]{2,1,0:T(8,128)(2,1)}, u32[]{:S(2)}, u32[]{:S(2)}) collective-permute-start(bf16[2,256,4096]{2,1,0:T(8,128)(2,1)} %half.1), channel_id=1, source_target_pairs={{0,4},{4,0},{8,12},{12,8},{1,5},{5,1},{9,13},{13,9},{2,6},{6,2},{1... | collective-permute-start | bytes 12582920 | tf_op jit(solution)/shard_map/ppermute | solution.py:34
  6.1 23.7 %copy-start = (f32[256,256]{1,0:T(8,128)S(1)}, f32[256,256]{1,0:T(8,128)}, u32[]{:S(2)}) copy-start(f32[256,256]{1,0:T(8,128)} %core_ref.1) | copy-start | bytes 786436
  6.1 16.4 %collective-permute-start.1 = (bf16[512,256]{1,0:T(8,128)(2,1)S(1)}, bf16[512,256]{1,0:T(8,128)(2,1)S(1)}, u32[]{:S(2)}, u32[]{:S(2)}) collective-permute-start(bf16[512,256]{1,0:T(8,128)(2,1)S(1)} %slice.45.first_ref), channel_id=1, source_target_pairs={{0,2},{1,3},{2,0},{3,1},{4,6},{5,7},{6,4},{7,5},{8,10},{9,11},{10,... | collective-permute-start | bytes 786440 | tf_op jit(solution)/shard_map/ppermute | solution.py:34
  9.8 12.9 %collective-permute-start.2 = (bf16[512,256]{1,0:T(8,128)(2,1)S(1)}, bf16[512,256]{1,0:T(8,128)(2,1)S(1)}, u32[]{:S(2)}, u32[]{:S(2)}) collective-permute-start(bf16[512,256]{1,0:T(8,128)(2,1)S(1)} %slice.45.first_ref), channel_id=1, source_target_pairs={{0,1},{1,0},{2,3},{3,2},{4,5},{5,4},{6,7},{7,6},{8,9},{9,8},{10,11... | collective-permute-start | bytes 786440 | tf_op jit(solution)/shard_map/ppermute | solution.py:34
  11.3 13.1 %collective-permute-start.3 = (bf16[512,256]{1,0:T(8,128)(2,1)S(1)}, bf16[512,256]{1,0:T(8,128)(2,1)S(1)}, u32[]{:S(2)}, u32[]{:S(2)}) collective-permute-start(bf16[512,256]{1,0:T(8,128)(2,1)S(1)} %slice.45.first_ref), channel_id=1, source_target_pairs={{0,3},{16,19}} | collective-permute-start | bytes 786440 | tf_op jit(solution)/shard_map/ppermute | solution.py:252
  24.5 5.4 %collective-permute-start.4 = (bf16[512,256]{1,0:T(8,128)(2,1)S(1)}, bf16[512,256]{1,0:T(8,128)(2,1)S(1)}, u32[]{:S(2)}, u32[]{:S(2)}) collective-permute-start(bf16[512,256]{1,0:T(8,128)(2,1)S(1)} %get-tuple-element.47), channel_id=1, source_target_pairs={{0,4},{1,5},{2,6},{3,7},{16,20},{17,21},{18,22},{19,23}} | collective-permute-start | bytes 786440 | tf_op jit(solution)/shard_map/ppermute | solution.py:256
  25.8 8.0 %collective-permute-start.5 = (bf16[512,256]{1,0:T(8,128)(2,1)S(1)}, bf16[512,256]{1,0:T(8,128)(2,1)S(1)}, u32[]{:S(2)}, u32[]{:S(2)}) collective-permute-start(bf16[512,256]{1,0:T(8,128)(2,1)S(1)} %get-tuple-element.47), channel_id=1, source_target_pairs={{0,8},{1,9},{2,10},{3,11},{16,24},{17,25},{18,26},{19,27}} | collective-permute-start | bytes 786440 | tf_op jit(solution)/shard_map/ppermute | solution.py:256
  27.2 6.8 %collective-permute-start.6 = (bf16[512,256]{1,0:T(8,128)(2,1)S(1)}, bf16[512,256]{1,0:T(8,128)(2,1)S(1)}, u32[]{:S(2)}, u32[]{:S(2)}) collective-permute-start(bf16[512,256]{1,0:T(8,128)(2,1)S(1)} %get-tuple-element.47), channel_id=1, source_target_pairs={{0,12},{1,13},{2,14},{3,15},{16,28},{17,29},{18,30},{19,31}} | collective-permute-start | bytes 786440 | tf_op jit(solution)/shard_map/ppermute | solution.py:256
  28.5 11.3 %collective-permute-start.7 = (bf16[512,256]{1,0:T(8,128)(2,1)S(1)}, bf16[512,256]{1,0:T(8,128)(2,1)S(1)}, u32[]{:S(2)}, u32[]{:S(2)}) collective-permute-start(bf16[512,256]{1,0:T(8,128)(2,1)S(1)} %get-tuple-element.46.second_ref), channel_id=1, source_target_pairs={{0,2},{1,3},{2,0},{3,1},{4,6},{5,7},{6,4},{7,5},{8,10},{9,11},{10,... | collective-permute-start | bytes 786440 | tf_op jit(solution)/shard_map/ppermute | solution.py:34
  30.0 32.8 %collective-permute-start.10 = (bf16[512,256]{1,0:T(8,128)(2,1)S(1)}, bf16[512,256]{1,0:T(8,128)(2,1)S(1)}, u32[]{:S(2)}, u32[]{:S(2)}) collective-permute-start(bf16[512,256]{1,0:T(8,128)(2,1)S(1)} %get-tuple-element.46.second_ref), channel_id=1, source_target_pairs={{0,1},{1,0},{2,3},{3,2},{4,5},{5,4},{6,7},{7,6},{8,9},{9,8},{10,11... | collective-permute-start | bytes 786440 | tf_op jit(solution)/shard_map/ppermute | solution.py:34
  33.8 18.9 %collective-permute-start.8 = (bf16[512,256]{1,0:T(8,128)(2,1)S(1)}, bf16[512,256]{1,0:T(8,128)(2,1)S(1)}, u32[]{:S(2)}, u32[]{:S(2)}) collective-permute-start(bf16[512,256]{1,0:T(8,128)(2,1)S(1)} %collective-permute-done.1.first_ref), channel_id=1, source_target_pairs={{0,1},{1,0},{2,3},{3,2},{4,5},{5,4},{6,7},{7,6},{8,9},{9,8},{10,11... | collective-permute-start | bytes 786440 | tf_op jit(solution)/shard_map/ppermute | solution.py:34
  39.8 17.9 %collective-permute-start.9 = (bf16[512,256]{1,0:T(8,128)(2,1)S(1)}, bf16[512,256]{1,0:T(8,128)(2,1)S(1)}, u32[]{:S(2)}, u32[]{:S(2)}) collective-permute-start(bf16[512,256]{1,0:T(8,128)(2,1)S(1)} %collective-permute-done.7.second_ref), channel_id=1, source_target_pairs={{0,1},{1,0},{2,3},{3,2},{4,5},{5,4},{6,7},{7,6},{8,9},{9,8},{10,11... | collective-permute-start | bytes 786440 | tf_op jit(solution)/shard_map/ppermute | solution.py:34
  46.5 25.1 %collective-permute-start.13 = (f16[272,1024]{1,0:T(8,128)(2,1)}, f16[272,1024]{1,0:T(8,128)(2,1)}, u32[]{:S(2)}, u32[]{:S(2)}) collective-permute-start(f16[272,1024]{1,0:T(8,128)(2,1)} %convert_element_type.18), channel_id=1, source_target_pairs={{0,2},{1,3},{2,0},{3,1},{4,6},{5,7},{6,4},{7,5},{8,10},{9,11},{10,... | collective-permute-start | bytes 1671176 | tf_op jit(solution)/shard_map/ppermute | solution.py:34
  69.5 2.1 %collective-permute-start.12 = (f32[392,256]{1,0:T(8,128)}, f32[392,256]{1,0:T(8,128)}, u32[]{:S(2)}, u32[]{:S(2)}) collective-permute-start(f32[392,256]{1,0:T(8,128)} %get-tuple-element.42), channel_id=1, source_target_pairs={{0,4},{4,0},{8,12},{12,8},{1,5},{5,1},{9,13},{13,9},{2,6},{6,2},{1... | collective-permute-start | bytes 1204232 | tf_op jit(solution)/shard_map/ppermute | solution.py:34
  72.6 3.6 %copy-start.3 = (f16[272,1024]{1,0:T(8,128)(2,1)S(1)}, f16[272,1024]{1,0:T(8,128)(2,1)}, u32[]{:S(2)}) copy-start(f16[272,1024]{1,0:T(8,128)(2,1)} %convert_element_type.19) | copy-start | bytes 1671172
  72.7 7.9 %collective-permute-start.15 = (f32[200,256]{1,0:T(8,128)S(1)}, f32[200,256]{1,0:T(8,128)S(1)}, u32[]{:S(2)}, u32[]{:S(2)}) collective-permute-start(f32[200,256]{1,0:T(8,128)S(1)} %pad_maximum_fusion), channel_id=1, source_target_pairs={{0,8},{4,12},{8,0},{12,4},{1,9},{5,13},{9,1},{13,5},{2,10},{6,14},... | collective-permute-start | bytes 614408 | tf_op jit(solution)/shard_map/ppermute | solution.py:34
  76.2 36.1 %collective-permute-start.14 = (f16[272,1024]{1,0:T(8,128)(2,1)S(1)}, f16[272,1024]{1,0:T(8,128)(2,1)}, u32[]{:S(2)}, u32[]{:S(2)}) collective-permute-start(f16[272,1024]{1,0:T(8,128)(2,1)S(1)} %copy-done.3), channel_id=1, source_target_pairs={{0,3},{1,2},{2,1},{3,0},{4,7},{5,6},{6,5},{7,4},{8,11},{9,10},{10,... | collective-permute-start | bytes 1671176 | tf_op jit(solution)/shard_map/ppermute | solution.py:34
  79.4 32.8 %collective-permute-start.11 = (f16[272,1024]{1,0:T(8,128)(2,1)}, f16[272,1024]{1,0:T(8,128)(2,1)S(1)}, u32[]{:S(2)}, u32[]{:S(2)}) collective-permute-start(f16[272,1024]{1,0:T(8,128)(2,1)} %convert_element_type.20), channel_id=1, source_target_pairs={{0,1},{1,0},{2,3},{3,2},{4,5},{5,4},{6,7},{7,6},{8,9},{9,8},{10,11... | collective-permute-start | bytes 1671176 | tf_op jit(solution)/shard_map/ppermute | solution.py:34
  80.7 27.0 %collective-permute-start.18 = (f32[96,256]{1,0:T(8,128)S(1)}, f32[96,256]{1,0:T(8,128)S(1)}, u32[]{:S(2)}, u32[]{:S(2)}) collective-permute-start(f32[96,256]{1,0:T(8,128)S(1)} %get-tuple-element.60), channel_id=1, source_target_pairs={{0,3},{1,2},{2,1},{3,0},{4,7},{5,6},{6,5},{7,4},{8,11},{9,10},{10,... | collective-permute-start | bytes 294920 | tf_op jit(solution)/shard_map/ppermute | solution.py:34
  83.6 25.5 %collective-permute-start.17 = (f32[96,256]{1,0:T(8,128)S(1)}, f32[96,256]{1,0:T(8,128)S(1)}, u32[]{:S(2)}, u32[]{:S(2)}) collective-permute-start(f32[96,256]{1,0:T(8,128)S(1)} %get-tuple-element.59), channel_id=1, source_target_pairs={{0,2},{1,3},{2,0},{3,1},{4,6},{5,7},{6,4},{7,5},{8,10},{9,11},{10,... | collective-permute-start | bytes 294920 | tf_op jit(solution)/shard_map/ppermute | solution.py:34
  83.6 26.2 %collective-permute-start.16 = (f32[96,256]{1,0:T(8,128)S(1)}, f32[96,256]{1,0:T(8,128)S(1)}, u32[]{:S(2)}, u32[]{:S(2)}) collective-permute-start(f32[96,256]{1,0:T(8,128)S(1)} %get-tuple-element.58), channel_id=1, source_target_pairs={{0,1},{1,0},{2,3},{3,2},{4,5},{5,4},{6,7},{7,6},{8,9},{9,8},{10,11... | collective-permute-start | bytes 294920 | tf_op jit(solution)/shard_map/ppermute | solution.py:34
  109.8 5.2 %collective-permute-start.19 = (f32[96,256]{1,0:T(8,128)S(1)}, f32[96,256]{1,0:T(8,128)S(1)}, u32[]{:S(2)}, u32[]{:S(2)}) collective-permute-start(f32[96,256]{1,0:T(8,128)S(1)} %fusion.3), channel_id=1, source_target_pairs={{0,8},{4,12},{8,0},{12,4},{1,9},{5,13},{9,1},{13,5},{2,10},{6,14},... | collective-permute-start | bytes 294920 | tf_op jit(solution)/shard_map/ppermute | solution.py:34
  115.1 1.5 %collective-permute-start.20 = (f32[192,256]{1,0:T(8,128)S(1)}, f32[192,256]{1,0:T(8,128)S(1)}, u32[]{:S(2)}, u32[]{:S(2)}) collective-permute-start(f32[192,256]{1,0:T(8,128)S(1)} %pad_maximum_fusion.2), channel_id=1, source_target_pairs={{0,4},{4,0},{8,12},{12,8},{1,5},{5,1},{9,13},{13,9},{2,6},{6,2},{1... | collective-permute-start | bytes 589832 | tf_op jit(solution)/shard_map/ppermute | solution.py:34

commit v3 on v2

--- a/solution.py
+++ b/solution.py
@@ -85,7 +85,7 @@
         ),
         out_shape=jax.ShapeDtypeStruct((months, rows, half), trade.dtype),
         compiler_params=pltpu.CompilerParams(vmem_limit_bytes=VMEM_LIMIT),
-        cost_estimate=SMALL,
+        cost_estimate=LARGE,
         name="half",
     )(at, trade)
 
@@ -96,9 +96,20 @@
     return value * jnp.exp2(15.0 - exponent), jnp.broadcast_to(exponent, (16, value.shape[1]))
 
 
-def piece_kernel(scaled, at_ref, own_ref, other_ref, first_ref, second_ref, mapped_ref, turned_ref, grad_ref, proj_ref):
+def decoded(value):
+    return value[:P_SIZE, :] * jnp.exp2(value[P_SIZE : P_SIZE + 1, :] - 15.0)
+
+
+def piece_kernel(kind, chained, count, at_ref, own_ref, other_ref, *rest):
+    blocks, (mapped_ref, turned_ref), rest = rest[:count], rest[count : count + 2], rest[count + 2 :]
+    before_ref, outs = (rest[0], rest[1:]) if chained else (None, rest)
+    grads, proj_ref = outs[:-1], outs[-1]
     step, width = pl.program_id(0), own_ref.shape[3]
-    block = jnp.where(step == 0, first_ref[...], second_ref[...])
+    at = pl.multiple_of(step * width, width)
+    if count == 1:
+        block = blocks[0][pl.ds(at, width), :]
+    else:
+        block = jnp.where(step == 0, blocks[0][...], blocks[1][...])
     months, rows = mapped_ref.shape[0], mapped_ref.shape[1] // 2
     parts = []
     for month in range(months):
@@ -108,28 +119,41 @@
             parts.append((flows.astype(F32) - model).astype(BF16))
     residual = jnp.concatenate(parts, 0)
     grad = dot(turned_ref[...], residual, NN)
-    at = pl.multiple_of(step * width, width)
-    if scaled:
+    if kind == "own":
+        grads[0][:, pl.ds(at, width)] = grad
+    else:
         value, exponent = encoded(grad)
-        grad_ref[:P_SIZE, pl.ds(at, width)] = value
-        grad_ref[P_SIZE:, pl.ds(at, width)] = exponent
-    else:
-        grad_ref[:, pl.ds(at, width)] = grad
+        if kind == "whole":
+            grads[0][:P_SIZE, pl.ds(at, width)] = value
+            grads[0][P_SIZE:, pl.ds(at, width)] = exponent
+        else:
+            for index, ref in enumerate(grads):
+
+                @pl.when(step == index)
+                def _():
+                    ref[:P_SIZE, :] = value
+                    ref[P_SIZE:, :] = exponent
+
     projected = dot(residual, block, NN).reshape(proj_ref.shape)
 
     @pl.when(step == 0)
     def _():
-        proj_ref[...] = projected
+        proj_ref[...] = before_ref[...] + projected if chained else projected
 
     @pl.when(step > 0)
     def _():
         proj_ref[...] += projected
 
 
-def piece_call(at, trade, other, blocks, mapped, turned, scaled, cost, label):
+def piece_call(at, trade, other, blocks, mapped, turned, before, kind, cost, label):
     months, size = mapped.shape[0], mapped.shape[1]
-    rows, width = size // 2, blocks[0].shape[0]
-    vmem = pl.BlockSpec(memory_space=pltpu.VMEM)
+    rows, width = size // 2, sum(block.shape[0] for block in blocks) // 2
+    vmem = pl.BlockSpec(memory_space=pltpu.VMEM)
+    grads = {
+        "own": [(P_SIZE, 2 * width)],
+        "whole": [(P_SIZE + 16, 2 * width)],
+        "split": [(P_SIZE + 16, width)] * 2,
+    }[kind]
     spec = pltpu.PrefetchScalarGridSpec(
         num_scalar_prefetch=1,
         grid=(2,),
@@ -137,51 +161,82 @@
             pl.BlockSpec((months, 1, rows, width), lambda j, s: (0, 0, 0, s[0] * 2 + j)),
             pl.BlockSpec((months, rows, width), lambda j, s: (0, 0, s[1] * 2 + j)),
         ]
-        + [vmem] * 4,
-        out_specs=[vmem, vmem],
+        + [vmem] * (2 + len(blocks) + len(before)),
+        out_specs=[vmem] * (len(grads) + 1),
     )
     return pl.pallas_call(
-        functools.partial(piece_kernel, scaled),
+        functools.partial(piece_kernel, kind, len(before) > 0, len(blocks)),
         grid_spec=spec,
-        out_shape=[
-            jax.ShapeDtypeStruct((P_SIZE + 16 if scaled else P_SIZE, 2 * width), F32),
-            jax.ShapeDtypeStruct((months, size, P_SIZE), F32),
-        ],
+        out_shape=[jax.ShapeDtypeStruct(shape, F32) for shape in grads]
+        + [jax.ShapeDtypeStruct((months, size, P_SIZE), F32)],
         compiler_params=pltpu.CompilerParams(vmem_limit_bytes=VMEM_LIMIT),
         cost_estimate=cost,
         name=label,
-    )(at, trade, other, *blocks, mapped, turned)
-
-
-def final_kernel(coef, own_ref, *rest):
-    received, out_ref = rest[:-1], rest[-1]
-    total = own_ref[...]
-    for ref in received:
-        total = total + ref[:P_SIZE, :] * jnp.exp2(ref[P_SIZE : P_SIZE + 1, :] - 15.0)
+    )(at, trade, other, *blocks, mapped, turned, *before)
+
+
+def relay_kernel(received_ref, own_ref, *outs):
+    step = pl.program_id(0)
+    value, exponent = encoded(decoded(received_ref[...]) + own_ref[...])
+    for index, ref in enumerate(outs):
+
+        @pl.when(step == index)
+        def _():
+            ref[:P_SIZE, :] = value
+            ref[P_SIZE:, :] = exponent
+
+
+def relay_call(received, own):
+    width = own.shape[1] // 2
+    vmem = pl.BlockSpec(memory_space=pltpu.VMEM)
+    return pl.pallas_call(
+        relay_kernel,
+        grid=(2,),
+        in_specs=[
+            pl.BlockSpec((P_SIZE + 16, width), lambda j: (0, j)),
+            pl.BlockSpec((P_SIZE, width), lambda j: (0, j)),
+        ],
+        out_specs=[vmem, vmem],
+        out_shape=[jax.ShapeDtypeStruct((P_SIZE + 16, width), F32)] * 2,
+        compiler_params=pltpu.CompilerParams(vmem_limit_bytes=VMEM_LIMIT),
+        cost_estimate=SMALL,
+        name="relay",
+    )(received, own)
+
+
+def final_kernel(coef, own_ref, near_ref, first_ref, second_ref, out_ref):
+    far = jnp.where(pl.program_id(0) == 0, first_ref[...], second_ref[...])
+    total = own_ref[...] + decoded(near_ref[...]) + decoded(far)
     out_ref[...] = (-coef * total).T
 
 
-def final_call(coef, own, received):
+def final_call(coef, own, near, halves):
     columns = own.shape[1]
     width = columns // 2
-    tall = pl.BlockSpec((P_SIZE + 16, width), lambda j: (0, j))
+    vmem = pl.BlockSpec(memory_space=pltpu.VMEM)
     return pl.pallas_call(
         functools.partial(final_kernel, coef),
         grid=(2,),
-        in_specs=[pl.BlockSpec((P_SIZE, width), lambda j: (0, j))] + [tall] * len(received),
+        in_specs=[
+            pl.BlockSpec((P_SIZE, width), lambda j: (0, j)),
+            pl.BlockSpec((P_SIZE + 16, width), lambda j: (0, j)),
+            vmem,
+            vmem,
+        ],
         out_specs=pl.BlockSpec((width, P_SIZE), lambda j: (j, 0)),
         out_shape=jax.ShapeDtypeStruct((columns, P_SIZE), F32),
         compiler_params=pltpu.CompilerParams(vmem_limit_bytes=VMEM_LIMIT),
         cost_estimate=SMALL,
         name="final",
-    )(own, *received)
+    )(own, near, *halves)
 
 
 def terms_kernel(cuts, at_ref, window_ref, inner_ref, core_ref, scales_ref, columns_ref, *rest):
-    projs, (keep_ref, send_ref, acc_ref) = rest[:-3], rest[-3:]
+    projs, outs, acc_ref = rest[:-5], rest[-5:-1], rest[-1]
     months, size = projs[0].shape[0], projs[0].shape[1]
     rows = size // 2
-    at = at_ref[0]
+    tile, cut = at_ref[0], at_ref[1]
+    at = tile % 2
     own = window_ref[pl.ds(pl.multiple_of(at * rows, rows), rows), :]
     other = window_ref[pl.ds(pl.multiple_of((1 - at) * rows, rows), rows), :]
     window = jnp.concatenate([own, other], 0)
@@ -204,109 +259,142 @@
     acc_ref[pl.ds(pl.multiple_of(at * rows, rows), rows), :] = acc_window[:rows]
     acc_ref[pl.ds(pl.multiple_of((1 - at) * rows, rows), rows), :] = acc_window[rows:]
     acc_ref[size:, :] = acc_core
-    w = size // (4 * cuts)
-    q = P_SIZE // 4
-    half = cuts * w + q
-    for ref, which in ((keep_ref, at), (send_ref, 1 - at)):
-        for x in range(2):
-            for cut in range(cuts):
-                start = pl.multiple_of(cut * 4 * w + which * 2 * w + x * w, 8)
-                ref[x * half + cut * w : x * half + (cut + 1) * w, :] = acc_ref[pl.ds(start, w), :]
-            start = pl.multiple_of(size + which * 2 * q + x * q, 8)
-            ref[x * half + cuts * w : (x + 1) * half, :] = acc_ref[pl.ds(start, q), :]
-        ref[2 * half :, :] = diagonal
-
-
-def terms_call(cuts, core_at, window, inner, core, scales, projs):
+    w, q = size // (4 * cuts), P_SIZE // 4
+    for mask, ref in enumerate(outs):
+        for turn in range(cuts):
+            start = pl.multiple_of((cut ^ turn) * 4 * w + (tile ^ mask) * w, 8)
+            ref[turn * w : (turn + 1) * w, :] = acc_ref[pl.ds(start, w), :]
+        start = pl.multiple_of(size + (tile ^ mask) * q, 8)
+        ref[cuts * w : cuts * w + q, :] = acc_ref[pl.ds(start, q), :]
+        ref[cuts * w + q :, :] = diagonal
+
+
+def terms_call(cuts, place, window, inner, core, scales, projs):
     months, size = projs[0].shape[0], projs[0].shape[1]
-    high = size // 2 + P_SIZE // 2 + 8
+    high = size // 4 + P_SIZE // 4 + 8
     vmem = pl.BlockSpec(memory_space=pltpu.VMEM)
     return pl.pallas_call(
         functools.partial(terms_kernel, cuts),
         in_specs=[pl.BlockSpec(memory_space=pltpu.SMEM)] + [vmem] * (5 + len(projs)),
-        out_specs=[vmem, vmem],
-        out_shape=[jax.ShapeDtypeStruct((high, P_SIZE), F32)] * 2,
+        out_specs=[vmem] * 4,
+        out_shape=[jax.ShapeDtypeStruct((high, P_SIZE), F32)] * 4,
         scratch_shapes=[pltpu.VMEM((size + P_SIZE, P_SIZE), F32)],
         compiler_params=pltpu.CompilerParams(vmem_limit_bytes=VMEM_LIMIT),
         cost_estimate=SMALL,
         name="terms",
-    )(core_at, window, inner, core, scales, scales.T, *projs)
+    )(place, window, inner, core, scales, scales.T, *projs)
+
+
+def quarter_kernel(coef, cuts, months, own_ref, *rest):
+    received, outs, diagonal_ref = rest[:3], rest[3:-1], rest[-1]
+    total = own_ref[...]
+    for ref in received:
+        total = total + ref[...]
+    w, q = (total.shape[0] - 8 - P_SIZE // 4) // cuts, P_SIZE // 4
+    for turn, ref in enumerate(outs):
+        ref[:w, :] = total[turn * w : (turn + 1) * w, :]
+        ref[w:, :] = total[cuts * w : cuts * w + q, :]
+    diagonal_ref[...] = -coef * total[cuts * w + q : cuts * w + q + months, :]
+
+
+def quarter_call(coef, cuts, months, own, received):
+    w, q = (own.shape[0] - 8 - P_SIZE // 4) // cuts, P_SIZE // 4
+    vmem = pl.BlockSpec(memory_space=pltpu.VMEM)
+    return pl.pallas_call(
+        functools.partial(quarter_kernel, coef, cuts, months),
+        in_specs=[vmem] * 4,
+        out_specs=[vmem] * (cuts + 1),
+        out_shape=[jax.ShapeDtypeStruct((w + q, P_SIZE), F32)] * cuts
+        + [jax.ShapeDtypeStruct((months, P_SIZE), F32)],
+        cost_estimate=SMALL,
+        name="quarter",
+    )(own, *received)
+
+
+def join_kernel(coef, at_ref, *rest):
+    parts, (window_ref, core_ref) = rest[:4], rest[4:]
+    tile = at_ref[0]
+    w, q = window_ref.shape[0] // 4, core_ref.shape[0] // 4
+    for mask, ref in enumerate(parts):
+        window_ref[pl.ds(pl.multiple_of((tile ^ mask) * w, 8), w), :] = -coef * ref[:w, :]
+        core_ref[pl.ds(pl.multiple_of((tile ^ mask) * q, 8), q), :] = -coef * ref[w:, :]
+
+
+def join_call(coef, place, parts):
+    q = P_SIZE // 4
+    w = parts[0].shape[0] - q
+    vmem = pl.BlockSpec(memory_space=pltpu.VMEM)
+    return pl.pallas_call(
+        functools.partial(join_kernel, coef),
+        in_specs=[pl.BlockSpec(memory_space=pltpu.SMEM)] + [vmem] * 4,
+        out_specs=[vmem] * 2,
+        out_shape=[jax.ShapeDtypeStruct((4 * w, P_SIZE), F32), jax.ShapeDtypeStruct((P_SIZE, P_SIZE), F32)],
+        cost_estimate=SMALL,
+        name="join",
+    )(place, *parts)
 
 
 def body_line(trade, factor, scales, core):
     cuts = lax.axis_size("cuts")
     tile, cut = lax.axis_index("tile"), lax.axis_index("cuts")
-    x, at = tile // 2, tile % 2
+    at = tile % 2
     months, rows = trade.shape[0], trade.shape[2]
     size, piece = 2 * rows, factor.shape[0]
     coef = 1.0 / math.sqrt(months * cuts * size)
+    place = jnp.stack([tile, cut]).astype(jnp.int32)
     core_at = at.astype(jnp.int32).reshape(1)
     inner = scales[:, :, None] * core[None] * scales[:, None, :]
     hold = lax.optimization_barrier
 
     half = cuts * piece
     give = half_call((1 - at).astype(jnp.int32).reshape(1), trade, half)
+
+    parts = [factor[:size], factor[size:]]
+    second = lax.ppermute(parts[0], ("tile", "cuts"), [(0, 2)])
+    far = [swapped(value, "cuts", 3) for value in parts]
+    near = [swapped(value, "cuts", 1) for value in parts]
+    second, near[0], far[0], give = hold((second, near[0], far[0], give))
+    first = near[0]
     other = swapped(give, "tile", 1)
-
-    parts = [factor[:size], factor[size:]]
-    third = lax.ppermute(parts[0], ("tile", "cuts"), [(0, 3)])
-    middle = [swapped(value, "cuts", 2) for value in parts]
-    near = [swapped(value, "cuts", 1) for value in parts]
-    line = jnp.where(cut == 0, parts[0], jnp.where(cut == 1, near[0], jnp.where(cut == 2, middle[0], third)))
+    line = jnp.where(cut == 0, parts[0], jnp.where(cut == 1, first, jnp.where(cut == 2, second, far[0])))
     out = [lax.ppermute(line, "tile", [(0, target)]) for target in (1, 2, 3)]
-    out, middle[1] = hold((out, middle[1]))
-    far = [swapped(value, "cuts", 1) for value in middle]
     window = jnp.where(tile == 0, line, sum(out[1:], out[0]))
     mapped, turned = mapped_call(core_at, window, inner)
 
-    def piece_of(which, block, scaled, cost, label, after=None):
+    def piece_of(which, blocks, kind, cost, label, before, after=None):
         where = jnp.stack([at * cuts + which, which]).astype(jnp.int32)
         if after is not None:
             where, _ = hold((where, after))
-        return piece_call(where, trade, other, block, mapped, turned, scaled, cost, label)
-
-    grad_middle, proj_middle = piece_of(cut ^ 2, middle, True, SMALL, "piece_middle")
-    grad_middle = grad_middle.astype(F16)
-    from_middle = swapped(grad_middle, "cuts", 2)
-    grad_own, proj_own = piece_of(cut, parts, False, LARGE, "piece_own", grad_middle)
-    grad_far, proj_far = piece_of(cut ^ 3, far, True, SMALL, "piece_far", proj_own)
+        return piece_call(where, trade, other, blocks, mapped, turned, before, kind, cost, label)
+
+    grad_own, proj = piece_of(cut, [factor], "own", LARGE, "piece_own", [])
+    far[1], _ = hold((far[1], proj))
+    middle = [swapped(value, "cuts", 1) for value in far]
+    grad_far, proj = piece_of(cut ^ 3, far, "whole", SMALL, "piece_far", [proj], proj)
     grad_far = grad_far.astype(F16)
-    from_far = swapped(grad_far, "cuts", 3)
-    grad_near, proj_near = piece_of(cut ^ 1, near, True, SMALL, "piece_near", grad_far)
+    joined = swapped(grad_far, "cuts", 1)
+    grad_near, proj = piece_of(cut ^ 1, near, "whole", LARGE, "piece_near", [proj], grad_far)
     grad_near = grad_near.astype(F16)
     from_near = swapped(grad_near, "cuts", 1)
-
-    keep, send = terms_call(cuts, core_at, window, inner, core, scales, [proj_near, proj_own, proj_middle, proj_far])
-    send, from_middle = hold((swapped(send, "tile", 1), from_middle))
-    both = keep + send
-    w, q = size // (4 * cuts), P_SIZE // 4
-    part = cuts * w + q
-    low, high, diagonal = both[:part], both[part : 2 * part], both[2 * part :]
-    keep = jnp.concatenate([jnp.where(x == 0, low, high), diagonal], 0)
-    send = jnp.concatenate([jnp.where(x == 0, high, low), diagonal], 0)
-    quarter = keep + swapped(send, "tile", 2)
-    diagonal = quarter[part : part + months]
-    core_part = quarter[cuts * w : part]
-
-    def for_cut(which):
-        return jnp.concatenate([lax.dynamic_slice_in_dim(quarter, which * w, w, 0), core_part], 0)
-
-    total = for_cut(cut)
-    for mask in range(1, cuts):
-        total = total + swapped(for_cut(cut ^ mask), "cuts", mask)
-
-    def joined_pair(mine, theirs, first):
-        return jnp.where(first, mine, theirs), jnp.where(first, theirs, mine)
-
-    first, second = joined_pair(total, swapped(total, "tile", 2), x == 0)
-    line_total = jnp.concatenate([first[:w], second[:w], first[w:], second[w:]], 0)
-    first, second = joined_pair(line_total, swapped(line_total, "tile", 1), at == 0)
-    grad_window = jnp.concatenate([first[: 2 * w], second[: 2 * w]], 0)
-    grad_core = jnp.concatenate([first[2 * w :], second[2 * w :]], 0)
-
-    received = [value.astype(F32) for value in (from_near, from_middle, from_far)]
-    grad_factor = final_call(coef, grad_own, received)
-    return (grad_factor, -coef * grad_window, -coef * grad_core, -coef * diagonal)
+    grad_middle, proj = piece_of(cut ^ 2, middle, "own", SMALL, "piece_middle", [proj], grad_near)
+
+    own, *send = terms_call(cuts, place, window, inner, core, scales, [proj])
+    joined, send[2] = hold((joined, send[2]))
+    received = [swapped(value, "tile", mask + 1) for mask, value in enumerate(send)]
+    passed = list(relay_call(joined.astype(F32), grad_middle))
+    from_middle = swapped(passed[0].astype(F16), "cuts", 2)
+    own, *send, grad_scales = quarter_call(coef, cuts, months, own, received)
+    send, passed[1] = hold((send, passed[1]))
+    from_middle_second = swapped(passed[1].astype(F16), "cuts", 2)
+    send = [swapped(value, "cuts", mask + 1) for mask, value in enumerate(send)]
+    send, from_near, from_middle = hold((send, from_near, from_middle))
+    total = own + sum(send)
+    quarters = [swapped(total, "tile", mask) for mask in (1, 2, 3)]
+    grad_window, grad_core = join_call(coef, place, [total] + quarters)
+
+    halves = [from_middle.astype(F32), from_middle_second.astype(F32)]
+    grad_factor = final_call(coef, grad_own, from_near.astype(F32), halves)
+    return (grad_factor, grad_window, grad_core, grad_scales)
 
 
 def from_root(block, axis, source):

time: 119 us -> 109 us (0.916)
  waiting for transfers between devices: 50.5 us -> 32.2 us
  Pallas kernels: 26.3 us -> 30.3 us
  local copies, waits for them, and re-layouts: 0.26 us -> 3.19 us
  starting transfers between devices: 31.2 us -> 33.3 us
    ppermute x17 -> x20, waiting for transfers between devices: 48.7 us -> 31.9 us  [swapped(): return lax.ppermute(value, axis, pairs)]
    pallas_call x4 -> x7, Pallas kernels: 16.5 us -> 20.9 us  [the longest x4 16.6 us: piece_call(): pl.pallas_call(functools.partial(piece_kernel, kind, len(before) > 0, len...]
    ppermute x1, starting transfers between devices: 1.87 us -> 5.96 us  [body_line(): second = lax.ppermute(parts[0], ('tile', 'cuts'), [(0, 2)])]
    ppermute x17 -> x20, starting transfers between devices: 25.4 us -> 22 us  [swapped(): return lax.ppermute(value, axis, pairs)]
    unnamed x9 -> x39, local copies, waits for them, and re-layouts: 0.15 us -> 2.22 us
    mul x3 -> x0, other arithmetic: 1.97 us -> none  [the longest x1 0.72 us: body_line(): -coef * grad_core]
    slice x1, other arithmetic: 0.06 us -> 1.72 us  [body_line(): parts = [factor[:size], factor[size:]]]
    ppermute x1, waiting for transfers between devices: 1.81 us -> 0.35 us  [body_line(): second = lax.ppermute(parts[0], ('tile', 'cuts'), [(0, 2)])]
  transfers between devices with their start and end apart: 21 -> 24, of which waited for: 11 -> 13; matrix products, arithmetic and copies ran while one was open for 5% -> 7% of each run, Pallas kernels for 18% -> 27%
where the time goes in v3:
time: 109 us; the launch traced here: 108 us
  starting transfers between devices  33.3 us (31%)
  waiting for transfers between devices  32.2 us (30%)
  Pallas kernels  30.3 us (28%)
  other arithmetic  8.41 us (8%)
  local copies, waits for them, and re-layouts  3.19 us (3%)
    ppermute x20, waiting for transfers between devices, swapped(): return lax.ppermute(value, axis, pairs)  31.9 us
    ppermute x20, starting transfers between devices, swapped(): return lax.ppermute(value, axis, pairs)  22 us
    pallas_call x4, Pallas kernels, piece_call(): pl.pallas_call(functools.partial(piece_kernel, kind, len(before) > 0, len...  16.6 us
    ppermute x1, starting transfers between devices, body_line(): second = lax.ppermute(parts[0], ('tile', 'cuts'), [(0, 2)])  5.96 us
    ppermute x3, starting transfers between devices, body_line(): out = [lax.ppermute(line, 'tile', [(0, target)]) for target in (1, 2, 3)]  5.36 us
    pallas_call x1, Pallas kernels, half_call(): pl.pallas_call(half_kernel, grid_spec=pltpu.PrefetchScalarGridSpec(num_sc...  4.97 us
    pallas_call x1, Pallas kernels, terms_call(): pl.pallas_call(functools.partial(terms_kernel, cuts), in_specs=[pl.BlockS...  2.24 us
    unnamed x39, local copies, waits for them, and re-layouts  2.22 us
  transfers between devices with their start and end apart: 24, of which 13 were waited for; matrix products, arithmetic and copies ran while one was open for 7% of the time, Pallas kernels for 27%

profile of v3, /device:TPU:0, one launch (start us, length us, event | category | flops | bytes accessed | tf_op | source)
XLA Modules:
  0.0 108.3 jit_solution(15854780861926437344)
XLA Ops:
  1.6 6.0 %collective-permute-start = (bf16[512,256]{1,0:T(8,128)(2,1)S(1)}, bf16[512,256]{1,0:T(8,128)(2,1)S(1)}, u32[]{:S(2)}, u32[]{:S(2)}) collective-permute-start(bf16[512,256]{1,0:T(8,128)(2,1)S(1)} %slice.6), channel_id=1, source_target_pairs={{0,2},{16,18}} | collective-permute-start | bytes 786440 | tf_op jit(solution)/shard_map/ppermute | solution.py:353
  8.5 5.0 %half.1 = bf16[2,256,4096]{2,1,0:T(8,128)(2,1)} custom-call(s32[1]{0:T(128)} %bitcast.2.at_ref, bf16[2,1,256,8192]{3,2,1,0:T(8,128)(2,1)} %own_ref.7), custom_call_target="tpu_custom_call" | custom-call | flops 99999997952 | bytes 100000000 | tf_op jit(solution)/shard_map/half/pallas_call | solution.py:78
  13.8 2.8 %collective-permute-done.1.rest_0_ = bf16[512,256]{1,0:T(8,128)(2,1)S(1)} collective-permute-done((bf16[512,256]{1,0:T(8,128)(2,1)S(1)}, bf16[512,256]{1,0:T(8,128)(2,1)S(1)}, u32[]{:S(2)}, u32[]{:S(2)}) %collective-permute-start.1) | collective-permute-done | bytes 262176 | tf_op jit(solution)/shard_map/ppermute | solution.py:34
  16.6 3.1 %collective-permute-done.2.rest_0_ = bf16[512,256]{1,0:T(8,128)(2,1)} collective-permute-done((bf16[512,256]{1,0:T(8,128)(2,1)S(1)}, bf16[512,256]{1,0:T(8,128)(2,1)}, u32[]{:S(2)}, u32[]{:S(2)}) %collective-permute-start.2) | collective-permute-done | bytes 262176 | tf_op jit(solution)/shard_map/ppermute | solution.py:34
  19.9 1.7 %fusion = (bf16[512,256]{1,0:T(8,128)(2,1)}, bf16[512,256]{1,0:T(8,128)(2,1)S(1)}) fusion(bf16[1024,256]{1,0:T(8,128)(2,1)S(1)} %copy-done.4, bf16[512,256]{1,0:T(8,128)(2,1)S(1)} %collective-permute-done.1.rest_0_, bf16[512,256]{1,0:T(8,128)(2,1)S(1)} %collective-permute-done, bf16[512,256]{1,0:T(8,128)(2,1)} %collective-permute-done.2.rest_0_, pred[]{:T(512)S(6)} %eq.17, ...), kind=kLoop, calls=%fused_computation.9 | loop fusion | flops 393216 | bytes 1835011 | tf_op jit(solution)/shard_map/slice | solution.py:352
  21.6 2.4 %collective-permute-start.4 = (bf16[512,256]{1,0:T(8,128)(2,1)S(1)}, bf16[512,256]{1,0:T(8,128)(2,1)S(1)}, u32[]{:S(2)}, u32[]{:S(2)}) collective-permute-start(bf16[512,256]{1,0:T(8,128)(2,1)S(1)} %get-tuple-element.89), channel_id=1, source_target_pairs={{0,4},{1,5},{2,6},{3,7},{16,20},{17,21},{18,22},{19,23}} | collective-permute-start | bytes 786440 | tf_op jit(solution)/shard_map/ppermute | solution.py:360
  24.0 1.6 %collective-permute-start.5 = (bf16[512,256]{1,0:T(8,128)(2,1)S(1)}, bf16[512,256]{1,0:T(8,128)(2,1)S(1)}, u32[]{:S(2)}, u32[]{:S(2)}) collective-permute-start(bf16[512,256]{1,0:T(8,128)(2,1)S(1)} %get-tuple-element.89), channel_id=1, source_target_pairs={{0,8},{1,9},{2,10},{3,11},{16,24},{17,25},{18,26},{19,27}} | collective-permute-start | bytes 786440 | tf_op jit(solution)/shard_map/ppermute | solution.py:360
  25.7 1.3 %collective-permute-start.6 = (bf16[512,256]{1,0:T(8,128)(2,1)S(1)}, bf16[512,256]{1,0:T(8,128)(2,1)S(1)}, u32[]{:S(2)}, u32[]{:S(2)}) collective-permute-start(bf16[512,256]{1,0:T(8,128)(2,1)S(1)} %get-tuple-element.89), channel_id=1, source_target_pairs={{0,12},{1,13},{2,14},{3,15},{16,28},{17,29},{18,30},{19,31}} | collective-permute-start | bytes 786440 | tf_op jit(solution)/shard_map/ppermute | solution.py:360
  27.2 3.9 %collective-permute-start.7 = (bf16[512,256]{1,0:T(8,128)(2,1)}, bf16[512,256]{1,0:T(8,128)(2,1)S(1)}, u32[]{:S(2)}, u32[]{:S(2)}) collective-permute-start(bf16[512,256]{1,0:T(8,128)(2,1)} %get-tuple-element.88), channel_id=1, source_target_pairs={{0,3},{1,2},{2,1},{3,0},{4,7},{5,6},{6,5},{7,4},{8,11},{9,10},{10,... | collective-permute-start | bytes 786440 | tf_op jit(solution)/shard_map/ppermute | solution.py:34
  31.1 2.0 %collective-permute-start.9 = (bf16[512,256]{1,0:T(8,128)(2,1)}, bf16[512,256]{1,0:T(8,128)(2,1)}, u32[]{:S(2)}, u32[]{:S(2)}) collective-permute-start(bf16[512,256]{1,0:T(8,128)(2,1)} %collective-permute-done.2.rest_0_), channel_id=1, source_target_pairs={{0,1},{1,0},{2,3},{3,2},{4,5},{5,4},{6,7},{7,6},{8,9},{9,8},{10,11... | collective-permute-start | bytes 786440 | tf_op jit(solution)/shard_map/ppermute | solution.py:34
  34.0 4.0 %piece_own.1 = (f32[256,1024]{1,0:T(8,128)S(1)}, f32[2,512,256]{2,1,0:T(8,128)S(1)}) custom-call(s32[2]{0:T(128)S(1)} %pad_add_fusion.at_ref, bf16[2,1,256,8192]{3,2,1,0:T(8,128)(2,1)} %own_ref.7, bf16[2,256,4096]{2,1,0:T(8,128)(2,1)} %collective-permute-done.3.other_ref, bf16[1024,256]{1,0:T(8,128)(2,1)S(1)} %copy-done.4, ...), custom_call_target="tpu_custom_call" | custom-call | flops 99999997952 | bytes 100000000 | tf_op jit(solution)/shard_map/piece_own/pallas_call | solution.py:167
  38.2 3.4 %collective-permute-start.10 = (bf16[512,256]{1,0:T(8,128)(2,1)S(1)}, bf16[512,256]{1,0:T(8,128)(2,1)}, u32[]{:S(2)}, u32[]{:S(2)}) collective-permute-start(bf16[512,256]{1,0:T(8,128)(2,1)S(1)} %collective-permute-done.7.rest_1_), channel_id=1, source_target_pairs={{0,1},{1,0},{2,3},{3,2},{4,5},{5,4},{6,7},{7,6},{8,9},{9,8},{10,11... | collective-permute-start | bytes 786440 | tf_op jit(solution)/shard_map/ppermute | solution.py:34
  41.6 4.2 %piece_far.1 = (f32[272,1024]{1,0:T(8,128)S(1)}, f32[2,512,256]{2,1,0:T(8,128)S(1)}) custom-call(s32[2]{0:T(128)S(1)} %pad_add_fusion.4.at_ref, bf16[2,1,256,8192]{3,2,1,0:T(8,128)(2,1)} %own_ref.7, bf16[2,256,4096]{2,1,0:T(8,128)(2,1)} %collective-permute-done.3.other_ref, bf16[512,256]{1,0:T(8,128)(2,1)} %collective-permute-done.2.rest_0_, ...), custom_call_target="tpu_custom_call" | custom-call | flops 1000 | bytes 1000 | tf_op jit(solution)/shard_map/piece_far/pallas_call | solution.py:167
  46.8 4.2 %piece_near.1 = (f32[272,1024]{1,0:T(8,128)S(1)}, f32[2,512,256]{2,1,0:T(8,128)S(1)}) custom-call(s32[2]{0:T(128)S(1)} %pad_add_fusion.3.at_ref, bf16[2,1,256,8192]{3,2,1,0:T(8,128)(2,1)} %own_ref.7, bf16[2,256,4096]{2,1,0:T(8,128)(2,1)} %collective-permute-done.3.other_ref, bf16[512,256]{1,0:T(8,128)(2,1)S(1)} %copy-done.8, ...), custom_call_target="tpu_custom_call" | custom-call | flops 99999997952 | bytes 100000000 | tf_op jit(solution)/shard_map/piece_near/pallas_call | solution.py:167
  51.9 2.0 %collective-permute-start.18 = (f16[272,1024]{1,0:T(8,128)(2,1)}, f16[272,1024]{1,0:T(8,128)(2,1)}, u32[]{:S(2)}, u32[]{:S(2)}) collective-permute-start(f16[272,1024]{1,0:T(8,128)(2,1)} %convert_element_type.25), channel_id=1, source_target_pairs={{0,1},{1,0},{2,3},{3,2},{4,5},{5,4},{6,7},{7,6},{8,9},{9,8},{10,11... | collective-permute-start | bytes 1671176 | tf_op jit(solution)/shard_map/ppermute | solution.py:34
  55.0 4.2 %piece_middle.1 = (f32[256,1024]{1,0:T(8,128)S(1)}, f32[2,512,256]{2,1,0:T(8,128)S(1)}) custom-call(s32[2]{0:T(128)S(1)} %pad_add_fusion.2.at_ref, bf16[2,1,256,8192]{3,2,1,0:T(8,128)(2,1)} %own_ref.7, bf16[2,256,4096]{2,1,0:T(8,128)(2,1)} %collective-permute-done.3.other_ref, bf16[512,256]{1,0:T(8,128)(2,1)} %collective-permute-done.9.rest_0_, ...), custom_call_target="tpu_custom_call" | custom-call | flops 1000 | bytes 1000 | tf_op jit(solution)/shard_map/piece_middle/pallas_call | solution.py:167
  59.2 2.2 %terms.1 = (f32[200,256]{1,0:T(8,128)S(1)}, f32[200,256]{1,0:T(8,128)S(1)}, f32[200,256]{1,0:T(8,128)S(1)}, f32[200,256]{1,0:T(8,128)S(1)}) custom-call(s32[2]{0:T(128)S(1)} %pad_add_fusion.1.at_ref, bf16[512,256]{1,0:T(8,128)(2,1)S(1)} %copy-done.3, f32[2,256,256]{2,1,0:T(8,128)S(1)} %copy-done.1, f32[256,256]{1,0:T(8,128)S(1)} %copy-done.6, ...), custom_call_target="tpu_custom_call" | custom-call | flops 1000 | bytes 1000 | tf_op jit(solution)/shard_map/terms/pallas_call | solution.py:276
  62.2 4.8 %collective-permute-done.13 = f16[272,1024]{1,0:T(8,128)(2,1)} collective-permute-done((f16[272,1024]{1,0:T(8,128)(2,1)}, f16[272,1024]{1,0:T(8,128)(2,1)}, u32[]{:S(2)}, u32[]{:S(2)}) %collective-permute-start.13) | collective-permute-done | bytes 557088 | tf_op jit(solution)/shard_map/ppermute | solution.py:34
  67.0 1.1 %convert_element_type.26.received_ref = f32[272,1024]{1,0:T(8,128)S(1)} convert(f16[272,1024]{1,0:T(8,128)(2,1)} %collective-permute-done.13) | non-fusion elementwise | flops 278528 | bytes 1671168 | tf_op jit(solution)/shard_map/convert_element_type | solution.py:384
  69.7 4.4 %collective-permute-done.14.rest_2_ = f32[200,256]{1,0:T(8,128)S(1)} collective-permute-done((f32[200,256]{1,0:T(8,128)S(1)}, f32[200,256]{1,0:T(8,128)S(1)}, u32[]{:S(2)}, u32[]{:S(2)}) %collective-permute-start.14) | collective-permute-done | bytes 204832 | tf_op jit(solution)/shard_map/ppermute | solution.py:34
  74.7 2.0 %quarter.1 = (f32[96,256]{1,0:T(8,128)}, f32[96,256]{1,0:T(8,128)}, f32[96,256]{1,0:T(8,128)}, f32[96,256]{1,0:T(8,128)}, f32[2,256]{1,0:T(2,128)}) custom-call(f32[200,256]{1,0:T(8,128)} %copy-done.9, f32[200,256]{1,0:T(8,128)} %copy-done.14, f32[200,256]{1,0:T(8,128)} %copy-done.15, f32[200,256]{1,0:T(8,128)} %copy-done.16), custom_call_target="tpu_custom_call" | custom-call | flops 1000 | bytes 1000 | tf_op jit(solution)/shard_map/quarter/pallas_call | solution.py:303
  76.7 2.6 %collective-permute-start.15 = (f32[96,256]{1,0:T(8,128)}, f32[96,256]{1,0:T(8,128)S(1)}, u32[]{:S(2)}, u32[]{:S(2)}) collective-permute-start(f32[96,256]{1,0:T(8,128)} %get-tuple-element.74), channel_id=1, source_target_pairs={{0,1},{1,0},{2,3},{3,2},{4,5},{5,4},{6,7},{7,6},{8,9},{9,8},{10,11... | collective-permute-start | bytes 294920 | tf_op jit(solution)/shard_map/ppermute | solution.py:34
  79.3 2.4 %collective-permute-start.17 = (f32[96,256]{1,0:T(8,128)}, f32[96,256]{1,0:T(8,128)S(1)}, u32[]{:S(2)}, u32[]{:S(2)}) collective-permute-start(f32[96,256]{1,0:T(8,128)} %get-tuple-element.76), channel_id=1, source_target_pairs={{0,3},{1,2},{2,1},{3,0},{4,7},{5,6},{6,5},{7,4},{8,11},{9,10},{10,... | collective-permute-start | bytes 294920 | tf_op jit(solution)/shard_map/ppermute | solution.py:34
  81.8 1.6 %collective-permute-done.18 = f16[272,1024]{1,0:T(8,128)(2,1)} collective-permute-done((f16[272,1024]{1,0:T(8,128)(2,1)}, f16[272,1024]{1,0:T(8,128)(2,1)}, u32[]{:S(2)}, u32[]{:S(2)}) %collective-permute-start.18) | collective-permute-done | bytes 557088 | tf_op jit(solution)/shard_map/ppermute | solution.py:34
  83.4 2.4 %collective-permute-start.20 = (f16[272,512]{1,0:T(8,128)(2,1)S(1)}, f16[272,512]{1,0:T(8,128)(2,1)}, u32[]{:S(2)}, u32[]{:S(2)}) collective-permute-start(f16[272,512]{1,0:T(8,128)(2,1)S(1)} %convert_element_type.30), channel_id=1, source_target_pairs={{0,2},{1,3},{2,0},{3,1},{4,6},{5,7},{6,4},{7,5},{8,10},{9,11},{10,... | collective-permute-start | bytes 835592 | tf_op jit(solution)/shard_map/ppermute | solution.py:34
  85.8 1.1 %collective-permute-done.15 = f32[96,256]{1,0:T(8,128)S(1)} collective-permute-done((f32[96,256]{1,0:T(8,128)}, f32[96,256]{1,0:T(8,128)S(1)}, u32[]{:S(2)}, u32[]{:S(2)}) %collective-permute-start.15) | collective-permute-done | bytes 98336 | tf_op jit(solution)/shard_map/ppermute | solution.py:34
  86.9 9.2 %collective-permute-done.16 = f32[96,256]{1,0:T(8,128)S(1)} collective-permute-done((f32[96,256]{1,0:T(8,128)}, f32[96,256]{1,0:T(8,128)S(1)}, u32[]{:S(2)}, u32[]{:S(2)}) %collective-permute-start.16) | collective-permute-done | bytes 98336 | tf_op jit(solution)/shard_map/ppermute | solution.py:34
  97.1 1.0 collective-permute-start.22
  99.0 1.1 %convert_element_type.28.near_ref = f32[272,1024]{1,0:T(8,128)S(1)} convert(f16[272,1024]{1,0:T(8,128)(2,1)} %collective-permute-done.18) | non-fusion elementwise | flops 278528 | bytes 1671168 | tf_op jit(solution)/shard_map/convert_element_type | solution.py:396
  100.2 2.6 %collective-permute-done.22.rest_2_ = f32[96,256]{1,0:T(8,128)S(1)} collective-permute-done((f32[96,256]{1,0:T(8,128)S(1)}, f32[96,256]{1,0:T(8,128)S(1)}, u32[]{:S(2)}, u32[]{:S(2)}) %collective-permute-start.22) | collective-permute-done | bytes 98336 | tf_op jit(solution)/shard_map/ppermute | solution.py:34
  104.1 1.8 %join.1 = (f32[128,256]{1,0:T(8,128)}, f32[256,256]{1,0:T(8,128)}) custom-call(s32[2]{0:T(128)} %copy-done.12, f32[96,256]{1,0:T(8,128)} %copy-done.13, f32[96,256]{1,0:T(8,128)} %copy-done.17, f32[96,256]{1,0:T(8,128)} %copy-done.18, f32[96,256]{1,0:T(8,128)} %collective-permute-done.23.rest_3_), custom_call_target="tpu_custom_call" | custom-call | flops 1000 | bytes 1000 | tf_op jit(solution)/shard_map/join/pallas_call | solution.py:327
  106.9 1.4 %final.1 = f32[1024,256]{1,0:T(8,128)} custom-call(f32[256,1024]{1,0:T(8,128)S(1)} %get-tuple-element.52.own_ref, f32[272,1024]{1,0:T(8,128)S(1)} %convert_element_type.28.near_ref, f32[272,512]{1,0:T(8,128)S(1)} %convert_element_type.29.first_ref, f32[272,512]{1,0:T(8,128)S(1)} %convert_element_type.31.second_ref), custom_call_target="tpu_custom_call" | custom-call | flops 1000 | bytes 1000 | tf_op jit(solution)/shard_map/final/pallas_call | solution.py:217
  (84 shorter events, 13.6 us)
Async XLA Ops:
  1.6 12.2 %collective-permute-start = (bf16[512,256]{1,0:T(8,128)(2,1)S(1)}, bf16[512,256]{1,0:T(8,128)(2,1)S(1)}, u32[]{:S(2)}, u32[]{:S(2)}) collective-permute-start(bf16[512,256]{1,0:T(8,128)(2,1)S(1)} %slice.6), channel_id=1, source_target_pairs={{0,2},{16,18}} | collective-permute-start | bytes 786440 | tf_op jit(solution)/shard_map/ppermute | solution.py:353
  7.6 9.0 %collective-permute-start.1 = (bf16[512,256]{1,0:T(8,128)(2,1)S(1)}, bf16[512,256]{1,0:T(8,128)(2,1)S(1)}, u32[]{:S(2)}, u32[]{:S(2)}) collective-permute-start(bf16[512,256]{1,0:T(8,128)(2,1)S(1)} %slice.6), channel_id=1, source_target_pairs={{0,1},{1,0},{2,3},{3,2},{4,5},{5,4},{6,7},{7,6},{8,9},{9,8},{10,11... | collective-permute-start | bytes 786440 | tf_op jit(solution)/shard_map/ppermute | solution.py:34
  7.6 12.1 %collective-permute-start.2 = (bf16[512,256]{1,0:T(8,128)(2,1)S(1)}, bf16[512,256]{1,0:T(8,128)(2,1)}, u32[]{:S(2)}, u32[]{:S(2)}) collective-permute-start(bf16[512,256]{1,0:T(8,128)(2,1)S(1)} %slice.6), channel_id=1, source_target_pairs={{0,3},{1,2},{2,1},{3,0},{4,7},{5,6},{6,5},{7,4},{8,11},{9,10},{10,... | collective-permute-start | bytes 786440 | tf_op jit(solution)/shard_map/ppermute | solution.py:34
  8.5 11.4 %copy-start.4 = (bf16[1024,256]{1,0:T(8,128)(2,1)S(1)}, bf16[1024,256]{1,0:T(8,128)(2,1)}, u32[]{:S(2)}) copy-start(bf16[1024,256]{1,0:T(8,128)(2,1)} %rest_0_.1) | copy-start | bytes 1572868
  13.4 13.6 %copy-start.5 = (f32[256,256]{1,0:T(8,128)S(1)}, f32[256,256]{1,0:T(8,128)}, u32[]{:S(2)}) copy-start(f32[256,256]{1,0:T(8,128)} %core_ref.1) | copy-start | bytes 786436
  13.4 13.6 %copy-start.10 = (f32[2,256]{1,0:T(2,128)S(1)}, f32[2,256]{1,0:T(2,128)}, u32[]{:S(2)}) copy-start(f32[2,256]{1,0:T(2,128)} %scales_ref.1) | copy-start | bytes 6148
  16.6 10.6 %copy-start.7 = (bf16[512,256]{1,0:T(8,128)(2,1)}, bf16[512,256]{1,0:T(8,128)(2,1)S(1)}, u32[]{:S(2)}) copy-start(bf16[512,256]{1,0:T(8,128)(2,1)S(1)} %collective-permute-done.1.rest_0_) | copy-start | bytes 786436
  19.7 14.3 %collective-permute-start.3 = (bf16[2,256,4096]{2,1,0:T(8,128)(2,1)}, bf16[2,256,4096]{2,1,0:T(8,128)(2,1)}, u32[]{:S(2)}, u32[]{:S(2)}) collective-permute-start(bf16[2,256,4096]{2,1,0:T(8,128)(2,1)} %half.1), channel_id=1, source_target_pairs={{0,4},{4,0},{8,12},{12,8},{1,5},{5,1},{9,13},{13,9},{2,6},{6,2},{1... | collective-permute-start | bytes 12582920 | tf_op jit(solution)/shard_map/ppermute | solution.py:34
  21.6 9.5 %collective-permute-start.4 = (bf16[512,256]{1,0:T(8,128)(2,1)S(1)}, bf16[512,256]{1,0:T(8,128)(2,1)S(1)}, u32[]{:S(2)}, u32[]{:S(2)}) collective-permute-start(bf16[512,256]{1,0:T(8,128)(2,1)S(1)} %get-tuple-element.89), channel_id=1, source_target_pairs={{0,4},{1,5},{2,6},{3,7},{16,20},{17,21},{18,22},{19,23}} | collective-permute-start | bytes 786440 | tf_op jit(solution)/shard_map/ppermute | solution.py:360
  24.0 7.1 %collective-permute-start.5 = (bf16[512,256]{1,0:T(8,128)(2,1)S(1)}, bf16[512,256]{1,0:T(8,128)(2,1)S(1)}, u32[]{:S(2)}, u32[]{:S(2)}) collective-permute-start(bf16[512,256]{1,0:T(8,128)(2,1)S(1)} %get-tuple-element.89), channel_id=1, source_target_pairs={{0,8},{1,9},{2,10},{3,11},{16,24},{17,25},{18,26},{19,27}} | collective-permute-start | bytes 786440 | tf_op jit(solution)/shard_map/ppermute | solution.py:360
  25.7 7.5 %collective-permute-start.6 = (bf16[512,256]{1,0:T(8,128)(2,1)S(1)}, bf16[512,256]{1,0:T(8,128)(2,1)S(1)}, u32[]{:S(2)}, u32[]{:S(2)}) collective-permute-start(bf16[512,256]{1,0:T(8,128)(2,1)S(1)} %get-tuple-element.89), channel_id=1, source_target_pairs={{0,12},{1,13},{2,14},{3,15},{16,28},{17,29},{18,30},{19,31}} | collective-permute-start | bytes 786440 | tf_op jit(solution)/shard_map/ppermute | solution.py:360
  27.2 6.0 %copy-start = (f32[2,256,256]{2,1,0:T(8,128)}, f32[2,256,256]{2,1,0:T(8,128)S(1)}, u32[]{:S(2)}) copy-start(f32[2,256,256]{2,1,0:T(8,128)S(1)} %multiply_multiply_fusion.inner_ref) | copy-start | bytes 1572868
  27.2 11.0 %collective-permute-start.7 = (bf16[512,256]{1,0:T(8,128)(2,1)}, bf16[512,256]{1,0:T(8,128)(2,1)S(1)}, u32[]{:S(2)}, u32[]{:S(2)}) collective-permute-start(bf16[512,256]{1,0:T(8,128)(2,1)} %get-tuple-element.88), channel_id=1, source_target_pairs={{0,3},{1,2},{2,1},{3,0},{4,7},{5,6},{6,5},{7,4},{8,11},{9,10},{10,... | collective-permute-start | bytes 786440 | tf_op jit(solution)/shard_map/ppermute | solution.py:34
  31.1 15.7 %collective-permute-start.8 = (bf16[512,256]{1,0:T(8,128)(2,1)}, bf16[512,256]{1,0:T(8,128)(2,1)S(1)}, u32[]{:S(2)}, u32[]{:S(2)}) collective-permute-start(bf16[512,256]{1,0:T(8,128)(2,1)} %get-tuple-element.88), channel_id=1, source_target_pairs={{0,1},{1,0},{2,3},{3,2},{4,5},{5,4},{6,7},{7,6},{8,9},{9,8},{10,11... | collective-permute-start | bytes 786440 | tf_op jit(solution)/shard_map/ppermute | solution.py:34
  31.1 23.1 %collective-permute-start.9 = (bf16[512,256]{1,0:T(8,128)(2,1)}, bf16[512,256]{1,0:T(8,128)(2,1)}, u32[]{:S(2)}, u32[]{:S(2)}) collective-permute-start(bf16[512,256]{1,0:T(8,128)(2,1)} %collective-permute-done.2.rest_0_), channel_id=1, source_target_pairs={{0,1},{1,0},{2,3},{3,2},{4,5},{5,4},{6,7},{7,6},{8,9},{9,8},{10,11... | collective-permute-start | bytes 786440 | tf_op jit(solution)/shard_map/ppermute | solution.py:34
  38.2 16.7 %collective-permute-start.10 = (bf16[512,256]{1,0:T(8,128)(2,1)S(1)}, bf16[512,256]{1,0:T(8,128)(2,1)}, u32[]{:S(2)}, u32[]{:S(2)}) collective-permute-start(bf16[512,256]{1,0:T(8,128)(2,1)S(1)} %collective-permute-done.7.rest_1_), channel_id=1, source_target_pairs={{0,1},{1,0},{2,3},{3,2},{4,5},{5,4},{6,7},{7,6},{8,9},{9,8},{10,11... | collective-permute-start | bytes 786440 | tf_op jit(solution)/shard_map/ppermute | solution.py:34
  46.8 20.2 %collective-permute-start.13 = (f16[272,1024]{1,0:T(8,128)(2,1)}, f16[272,1024]{1,0:T(8,128)(2,1)}, u32[]{:S(2)}, u32[]{:S(2)}) collective-permute-start(f16[272,1024]{1,0:T(8,128)(2,1)} %convert_element_type.24), channel_id=1, source_target_pairs={{0,1},{1,0},{2,3},{3,2},{4,5},{5,4},{6,7},{7,6},{8,9},{9,8},{10,11... | collective-permute-start | bytes 1671176 | tf_op jit(solution)/shard_map/ppermute | solution.py:34
  51.9 31.5 %collective-permute-start.18 = (f16[272,1024]{1,0:T(8,128)(2,1)}, f16[272,1024]{1,0:T(8,128)(2,1)}, u32[]{:S(2)}, u32[]{:S(2)}) collective-permute-start(f16[272,1024]{1,0:T(8,128)(2,1)} %convert_element_type.25), channel_id=1, source_target_pairs={{0,1},{1,0},{2,3},{3,2},{4,5},{5,4},{6,7},{7,6},{8,9},{9,8},{10,11... | collective-permute-start | bytes 1671176 | tf_op jit(solution)/shard_map/ppermute | solution.py:34
  54.1 5.1 %copy-start.12 = (s32[2]{0:T(128)}, s32[2]{0:T(128)S(1)}, u32[]{:S(2)}) copy-start(s32[2]{0:T(128)S(1)} %pad_add_fusion.1.at_ref) | copy-start | bytes 28
  62.2 6.9 %collective-permute-start.11 = (f32[200,256]{1,0:T(8,128)S(1)}, f32[200,256]{1,0:T(8,128)S(1)}, u32[]{:S(2)}, u32[]{:S(2)}) collective-permute-start(f32[200,256]{1,0:T(8,128)S(1)} %get-tuple-element.64), channel_id=1, source_target_pairs={{0,4},{4,0},{8,12},{12,8},{1,5},{5,1},{9,13},{13,9},{2,6},{6,2},{1... | collective-permute-start | bytes 614408 | tf_op jit(solution)/shard_map/ppermute | solution.py:34
  62.2 7.5 %collective-permute-start.12 = (f32[200,256]{1,0:T(8,128)S(1)}, f32[200,256]{1,0:T(8,128)S(1)}, u32[]{:S(2)}, u32[]{:S(2)}) collective-permute-start(f32[200,256]{1,0:T(8,128)S(1)} %get-tuple-element.65), channel_id=1, source_target_pairs={{0,8},{4,12},{8,0},{12,4},{1,9},{5,13},{9,1},{13,5},{2,10},{6,14},... | collective-permute-start | bytes 614408 | tf_op jit(solution)/shard_map/ppermute | solution.py:34
  67.0 7.0 %collective-permute-start.14 = (f32[200,256]{1,0:T(8,128)S(1)}, f32[200,256]{1,0:T(8,128)S(1)}, u32[]{:S(2)}, u32[]{:S(2)}) collective-permute-start(f32[200,256]{1,0:T(8,128)S(1)} %get-tuple-element.67), channel_id=1, source_target_pairs={{0,12},{4,8},{8,4},{12,0},{1,13},{5,9},{9,5},{13,1},{2,14},{6,10},... | collective-permute-start | bytes 614408 | tf_op jit(solution)/shard_map/ppermute | solution.py:34
  68.7 17.1 %collective-permute-start.19 = (f16[272,512]{1,0:T(8,128)(2,1)S(1)}, f16[272,512]{1,0:T(8,128)(2,1)S(1)}, u32[]{:S(2)}, u32[]{:S(2)}) collective-permute-start(f16[272,512]{1,0:T(8,128)(2,1)S(1)} %convert_element_type.27), channel_id=1, source_target_pairs={{0,2},{1,3},{2,0},{3,1},{4,6},{5,7},{6,4},{7,5},{8,10},{9,11},{10,... | collective-permute-start | bytes 835592 | tf_op jit(solution)/shard_map/ppermute | solution.py:34
  69.1 4.9 %copy-start.14 = (f32[200,256]{1,0:T(8,128)}, f32[200,256]{1,0:T(8,128)S(1)}, u32[]{:S(2)}) copy-start(f32[200,256]{1,0:T(8,128)S(1)} %collective-permute-done.11.rest_0_) | copy-start | bytes 614404
  69.7 4.4 %copy-start.15 = (f32[200,256]{1,0:T(8,128)}, f32[200,256]{1,0:T(8,128)S(1)}, u32[]{:S(2)}) copy-start(f32[200,256]{1,0:T(8,128)S(1)} %collective-permute-done.12.rest_1_) | copy-start | bytes 614404
  76.7 10.2 %collective-permute-start.15 = (f32[96,256]{1,0:T(8,128)}, f32[96,256]{1,0:T(8,128)S(1)}, u32[]{:S(2)}, u32[]{:S(2)}) collective-permute-start(f32[96,256]{1,0:T(8,128)} %get-tuple-element.74), channel_id=1, source_target_pairs={{0,1},{1,0},{2,3},{3,2},{4,5},{5,4},{6,7},{7,6},{8,9},{9,8},{10,11... | collective-permute-start | bytes 294920 | tf_op jit(solution)/shard_map/ppermute | solution.py:34
  79.3 16.8 %collective-permute-start.16 = (f32[96,256]{1,0:T(8,128)}, f32[96,256]{1,0:T(8,128)S(1)}, u32[]{:S(2)}, u32[]{:S(2)}) collective-permute-start(f32[96,256]{1,0:T(8,128)} %get-tuple-element.75), channel_id=1, source_target_pairs={{0,2},{1,3},{2,0},{3,1},{4,6},{5,7},{6,4},{7,5},{8,10},{9,11},{10,... | collective-permute-start | bytes 294920 | tf_op jit(solution)/shard_map/ppermute | solution.py:34
  79.3 16.8 %collective-permute-start.17 = (f32[96,256]{1,0:T(8,128)}, f32[96,256]{1,0:T(8,128)S(1)}, u32[]{:S(2)}, u32[]{:S(2)}) collective-permute-start(f32[96,256]{1,0:T(8,128)} %get-tuple-element.76), channel_id=1, source_target_pairs={{0,3},{1,2},{2,1},{3,0},{4,7},{5,6},{6,5},{7,4},{8,11},{9,10},{10,... | collective-permute-start | bytes 294920 | tf_op jit(solution)/shard_map/ppermute | solution.py:34
  83.4 22.5 %collective-permute-start.20 = (f16[272,512]{1,0:T(8,128)(2,1)S(1)}, f16[272,512]{1,0:T(8,128)(2,1)}, u32[]{:S(2)}, u32[]{:S(2)}) collective-permute-start(f16[272,512]{1,0:T(8,128)(2,1)S(1)} %convert_element_type.30), channel_id=1, source_target_pairs={{0,2},{1,3},{2,0},{3,1},{4,6},{5,7},{6,4},{7,5},{8,10},{9,11},{10,... | collective-permute-start | bytes 835592 | tf_op jit(solution)/shard_map/ppermute | solution.py:34
  97.0 3.2 %collective-permute-start.21 = (f32[96,256]{1,0:T(8,128)S(1)}, f32[96,256]{1,0:T(8,128)S(1)}, u32[]{:S(2)}, u32[]{:S(2)}) collective-permute-start(f32[96,256]{1,0:T(8,128)S(1)} %add_add_fusion.rest_0_), channel_id=1, source_target_pairs={{0,4},{4,0},{8,12},{12,8},{1,5},{5,1},{9,13},{13,9},{2,6},{6,2},{1... | collective-permute-start | bytes 294920 | tf_op jit(solution)/shard_map/ppermute | solution.py:34
  97.1 5.7 %collective-permute-start.22 = (f32[96,256]{1,0:T(8,128)S(1)}, f32[96,256]{1,0:T(8,128)S(1)}, u32[]{:S(2)}, u32[]{:S(2)}) collective-permute-start(f32[96,256]{1,0:T(8,128)S(1)} %add_add_fusion.rest_0_), channel_id=1, source_target_pairs={{0,8},{4,12},{8,0},{12,4},{1,9},{5,13},{9,1},{13,5},{2,10},{6,14},... | collective-permute-start | bytes 294920 | tf_op jit(solution)/shard_map/ppermute | solution.py:34
  98.1 5.9 %collective-permute-start.23 = (f32[96,256]{1,0:T(8,128)S(1)}, f32[96,256]{1,0:T(8,128)}, u32[]{:S(2)}, u32[]{:S(2)}) collective-permute-start(f32[96,256]{1,0:T(8,128)S(1)} %add_add_fusion.rest_0_), channel_id=1, source_target_pairs={{0,12},{4,8},{8,4},{12,0},{1,13},{5,9},{9,5},{13,1},{2,14},{6,10},... | collective-permute-start | bytes 294920 | tf_op jit(solution)/shard_map/ppermute | solution.py:34
  (11 other events, 26.4 us)

commit v4 on v3

--- a/solution.py
+++ b/solution.py
@@ -14,6 +14,7 @@
 NT = (((1,), (1,)), ((), ()))
 TN = (((0,), (0,)), ((), ()))
 VMEM_LIMIT = 48 * 2**20
+VMEM_SMALL = 8 * 2**20
 LARGE = pl.CostEstimate(flops=10**11, bytes_accessed=10**8, transcendentals=0)
 SMALL = pl.CostEstimate(flops=1000, bytes_accessed=1000, transcendentals=0)
 
@@ -285,7 +286,7 @@
     )(place, window, inner, core, scales, scales.T, *projs)
 
 
-def quarter_kernel(coef, cuts, months, own_ref, *rest):
+def quarter_kernel(cuts, own_ref, *rest):
     received, outs, diagonal_ref = rest[:3], rest[3:-1], rest[-1]
     total = own_ref[...]
     for ref in received:
@@ -294,44 +295,47 @@
     for turn, ref in enumerate(outs):
         ref[:w, :] = total[turn * w : (turn + 1) * w, :]
         ref[w:, :] = total[cuts * w : cuts * w + q, :]
-    diagonal_ref[...] = -coef * total[cuts * w + q : cuts * w + q + months, :]
-
-
-def quarter_call(coef, cuts, months, own, received):
+    diagonal_ref[...] = total[cuts * w + q :, :]
+
+
+def quarter_call(cuts, own, received):
     w, q = (own.shape[0] - 8 - P_SIZE // 4) // cuts, P_SIZE // 4
     vmem = pl.BlockSpec(memory_space=pltpu.VMEM)
     return pl.pallas_call(
-        functools.partial(quarter_kernel, coef, cuts, months),
+        functools.partial(quarter_kernel, cuts),
         in_specs=[vmem] * 4,
         out_specs=[vmem] * (cuts + 1),
         out_shape=[jax.ShapeDtypeStruct((w + q, P_SIZE), F32)] * cuts
-        + [jax.ShapeDtypeStruct((months, P_SIZE), F32)],
+        + [jax.ShapeDtypeStruct((8, P_SIZE), F32)],
+        compiler_params=pltpu.CompilerParams(vmem_limit_bytes=VMEM_SMALL),
         cost_estimate=SMALL,
         name="quarter",
     )(own, *received)
 
 
 def join_kernel(coef, at_ref, *rest):
-    parts, (window_ref, core_ref) = rest[:4], rest[4:]
+    parts, diagonal_ref, (window_ref, core_ref, scales_ref) = rest[:4], rest[4], rest[5:]
     tile = at_ref[0]
     w, q = window_ref.shape[0] // 4, core_ref.shape[0] // 4
     for mask, ref in enumerate(parts):
         window_ref[pl.ds(pl.multiple_of((tile ^ mask) * w, 8), w), :] = -coef * ref[:w, :]
         core_ref[pl.ds(pl.multiple_of((tile ^ mask) * q, 8), q), :] = -coef * ref[w:, :]
-
-
-def join_call(coef, place, parts):
+    scales_ref[...] = -coef * diagonal_ref[: scales_ref.shape[0], :]
+
+
+def join_call(coef, months, place, parts, diagonal):
     q = P_SIZE // 4
     w = parts[0].shape[0] - q
     vmem = pl.BlockSpec(memory_space=pltpu.VMEM)
     return pl.pallas_call(
         functools.partial(join_kernel, coef),
-        in_specs=[pl.BlockSpec(memory_space=pltpu.SMEM)] + [vmem] * 4,
-        out_specs=[vmem] * 2,
-        out_shape=[jax.ShapeDtypeStruct((4 * w, P_SIZE), F32), jax.ShapeDtypeStruct((P_SIZE, P_SIZE), F32)],
+        in_specs=[pl.BlockSpec(memory_space=pltpu.SMEM)] + [vmem] * 5,
+        out_specs=[vmem] * 3,
+        out_shape=[jax.ShapeDtypeStruct((high, P_SIZE), F32) for high in (4 * w, P_SIZE, months)],
+        compiler_params=pltpu.CompilerParams(vmem_limit_bytes=VMEM_SMALL),
         cost_estimate=SMALL,
         name="join",
-    )(place, *parts)
+    )(place, *parts, diagonal)
 
 
 def body_line(trade, factor, scales, core):
@@ -379,21 +383,21 @@
     grad_middle, proj = piece_of(cut ^ 2, middle, "own", SMALL, "piece_middle", [proj], grad_near)
 
     own, *send = terms_call(cuts, place, window, inner, core, scales, [proj])
-    joined, send[2] = hold((joined, send[2]))
     received = [swapped(value, "tile", mask + 1) for mask, value in enumerate(send)]
+    joined, received[0] = hold((joined, received[0]))
     passed = list(relay_call(joined.astype(F32), grad_middle))
     from_middle = swapped(passed[0].astype(F16), "cuts", 2)
-    own, *send, grad_scales = quarter_call(coef, cuts, months, own, received)
+    own, *send, diagonal = quarter_call(cuts, own, received)
     send, passed[1] = hold((send, passed[1]))
     from_middle_second = swapped(passed[1].astype(F16), "cuts", 2)
     send = [swapped(value, "cuts", mask + 1) for mask, value in enumerate(send)]
     send, from_near, from_middle = hold((send, from_near, from_middle))
     total = own + sum(send)
     quarters = [swapped(total, "tile", mask) for mask in (1, 2, 3)]
-    grad_window, grad_core = join_call(coef, place, [total] + quarters)
-
     halves = [from_middle.astype(F32), from_middle_second.astype(F32)]
     grad_factor = final_call(coef, grad_own, from_near.astype(F32), halves)
+    quarters, grad_factor = hold((quarters, grad_factor))
+    grad_window, grad_core, grad_scales = join_call(coef, months, place, [total] + quarters, diagonal)
     return (grad_factor, grad_window, grad_core, grad_scales)
 
 

time: 109 us -> 106 us (0.972)
  other arithmetic: 8.41 us -> 2.16 us
  waiting for transfers between devices: 32.2 us -> 37.4 us
  starting transfers between devices: 33.3 us -> 35.7 us
  Pallas kernels: 30.3 us -> 27.9 us
  local copies, waits for them, and re-layouts: 3.19 us -> 1.13 us
    ppermute x20, waiting for transfers between devices: 31.9 us -> 37.1 us  [swapped(): return lax.ppermute(value, axis, pairs)]
    ppermute x20, starting transfers between devices: 22 us -> 24.3 us  [swapped(): return lax.ppermute(value, axis, pairs)]
    unnamed x39 -> x15, local copies, waits for them, and re-layouts: 2.22 us -> 0.16 us
    pallas_call x1, Pallas kernels: 1.99 us -> 0.05 us  [quarter_call(): pl.pallas_call(functools.partial(quarter_kernel, cuts), in_specs=[vmem] *...]
  transfers between devices with their start and end apart: 24 -> 24, of which waited for: 13 -> 12; matrix products, arithmetic and copies ran while one was open for 7% -> 2% of each run, Pallas kernels for 27% -> 25%
where the time goes in v4:
time: 106 us; the launch traced here: 105 us
  waiting for transfers between devices  37.4 us (35%)
  starting transfers between devices  35.7 us (34%)
  Pallas kernels  27.9 us (26%)
  other arithmetic  2.16 us (2%)
  local copies, waits for them, and re-layouts  1.13 us (1%)
    ppermute x20, waiting for transfers between devices, swapped(): return lax.ppermute(value, axis, pairs)  37.1 us
    ppermute x20, starting transfers between devices, swapped(): return lax.ppermute(value, axis, pairs)  24.3 us
    pallas_call x4, Pallas kernels, piece_call(): pl.pallas_call(functools.partial(piece_kernel, kind, len(before) > 0, len...  16.7 us
    ppermute x1, starting transfers between devices, body_line(): second = lax.ppermute(parts[0], ('tile', 'cuts'), [(0, 2)])  5.96 us
    ppermute x3, starting transfers between devices, body_line(): out = [lax.ppermute(line, 'tile', [(0, target)]) for target in (1, 2, 3)]  5.37 us
    pallas_call x1, Pallas kernels, half_call(): pl.pallas_call(half_kernel, grid_spec=pltpu.PrefetchScalarGridSpec(num_sc...  4.95 us
    pallas_call x1, Pallas kernels, terms_call(): pl.pallas_call(functools.partial(terms_kernel, cuts), in_specs=[pl.BlockS...  2.23 us
  transfers between devices with their start and end apart: 24, of which 12 were waited for; matrix products, arithmetic and copies ran while one was open for 2% of the time, Pallas kernels for 25%

profile of v4, /device:TPU:0, one launch (start us, length us, event | category | flops | bytes accessed | tf_op | source)
XLA Modules:
  0.0 105.2 jit_solution(17088419204995918436)
XLA Ops:
  0.6 1.0 slice.6
  1.6 6.0 %collective-permute-start = (bf16[512,256]{1,0:T(8,128)(2,1)S(1)}, bf16[512,256]{1,0:T(8,128)(2,1)S(1)}, u32[]{:S(2)}, u32[]{:S(2)}) collective-permute-start(bf16[512,256]{1,0:T(8,128)(2,1)S(1)} %slice.6), channel_id=1, source_target_pairs={{0,2},{16,18}} | collective-permute-start | bytes 786440 | tf_op jit(solution)/shard_map/ppermute | solution.py:357
  8.5 5.0 %half.1 = bf16[2,256,4096]{2,1,0:T(8,128)(2,1)} custom-call(s32[1]{0:T(128)} %bitcast.2.at_ref, bf16[2,1,256,8192]{3,2,1,0:T(8,128)(2,1)} %own_ref.7), custom_call_target="tpu_custom_call" | custom-call | flops 99999997952 | bytes 100000000 | tf_op jit(solution)/shard_map/half/pallas_call | solution.py:79
  13.8 2.8 %collective-permute-done.1.rest_0_ = bf16[512,256]{1,0:T(8,128)(2,1)S(1)} collective-permute-done((bf16[512,256]{1,0:T(8,128)(2,1)S(1)}, bf16[512,256]{1,0:T(8,128)(2,1)S(1)}, u32[]{:S(2)}, u32[]{:S(2)}) %collective-permute-start.1) | collective-permute-done | bytes 262176 | tf_op jit(solution)/shard_map/ppermute | solution.py:35
  16.6 3.1 %collective-permute-done.2.rest_0_ = bf16[512,256]{1,0:T(8,128)(2,1)} collective-permute-done((bf16[512,256]{1,0:T(8,128)(2,1)S(1)}, bf16[512,256]{1,0:T(8,128)(2,1)}, u32[]{:S(2)}, u32[]{:S(2)}) %collective-permute-start.2) | collective-permute-done | bytes 262176 | tf_op jit(solution)/shard_map/ppermute | solution.py:35
  20.0 1.0 fusion
  21.0 2.4 %collective-permute-start.3 = (bf16[512,256]{1,0:T(8,128)(2,1)S(1)}, bf16[512,256]{1,0:T(8,128)(2,1)S(1)}, u32[]{:S(2)}, u32[]{:S(2)}) collective-permute-start(bf16[512,256]{1,0:T(8,128)(2,1)S(1)} %get-tuple-element.99), channel_id=1, source_target_pairs={{0,4},{1,5},{2,6},{3,7},{16,20},{17,21},{18,22},{19,23}} | collective-permute-start | bytes 786440 | tf_op jit(solution)/shard_map/ppermute | solution.py:364
  23.4 1.6 %collective-permute-start.4 = (bf16[512,256]{1,0:T(8,128)(2,1)S(1)}, bf16[512,256]{1,0:T(8,128)(2,1)S(1)}, u32[]{:S(2)}, u32[]{:S(2)}) collective-permute-start(bf16[512,256]{1,0:T(8,128)(2,1)S(1)} %get-tuple-element.99), channel_id=1, source_target_pairs={{0,8},{1,9},{2,10},{3,11},{16,24},{17,25},{18,26},{19,27}} | collective-permute-start | bytes 786440 | tf_op jit(solution)/shard_map/ppermute | solution.py:364
  25.1 1.3 %collective-permute-start.5 = (bf16[512,256]{1,0:T(8,128)(2,1)S(1)}, bf16[512,256]{1,0:T(8,128)(2,1)S(1)}, u32[]{:S(2)}, u32[]{:S(2)}) collective-permute-start(bf16[512,256]{1,0:T(8,128)(2,1)S(1)} %get-tuple-element.99), channel_id=1, source_target_pairs={{0,12},{1,13},{2,14},{3,15},{16,28},{17,29},{18,30},{19,31}} | collective-permute-start | bytes 786440 | tf_op jit(solution)/shard_map/ppermute | solution.py:364
  26.8 3.9 %collective-permute-start.7 = (bf16[512,256]{1,0:T(8,128)(2,1)S(1)}, bf16[512,256]{1,0:T(8,128)(2,1)S(1)}, u32[]{:S(2)}, u32[]{:S(2)}) collective-permute-start(bf16[512,256]{1,0:T(8,128)(2,1)S(1)} %get-tuple-element.98), channel_id=1, source_target_pairs={{0,3},{1,2},{2,1},{3,0},{4,7},{5,6},{6,5},{7,4},{8,11},{9,10},{10,... | collective-permute-start | bytes 786440 | tf_op jit(solution)/shard_map/ppermute | solution.py:35
  30.7 2.0 %collective-permute-start.9 = (bf16[512,256]{1,0:T(8,128)(2,1)}, bf16[512,256]{1,0:T(8,128)(2,1)}, u32[]{:S(2)}, u32[]{:S(2)}) collective-permute-start(bf16[512,256]{1,0:T(8,128)(2,1)} %collective-permute-done.2.rest_0_), channel_id=1, source_target_pairs={{0,1},{1,0},{2,3},{3,2},{4,5},{5,4},{6,7},{7,6},{8,9},{9,8},{10,11... | collective-permute-start | bytes 786440 | tf_op jit(solution)/shard_map/ppermute | solution.py:35
  33.6 4.0 %piece_own.1 = (f32[256,1024]{1,0:T(8,128)S(1)}, f32[2,512,256]{2,1,0:T(8,128)S(1)}) custom-call(s32[2]{0:T(128)S(1)} %pad_add_fusion.4.at_ref, bf16[2,1,256,8192]{3,2,1,0:T(8,128)(2,1)} %own_ref.7, bf16[2,256,4096]{2,1,0:T(8,128)(2,1)} %collective-permute-done.6.other_ref, bf16[1024,256]{1,0:T(8,128)(2,1)S(1)} %copy-done.4, ...), custom_call_target="tpu_custom_call" | custom-call | flops 99999997952 | bytes 100000000 | tf_op jit(solution)/shard_map/piece_own/pallas_call | solution.py:168
  37.6 3.4 %collective-permute-start.10 = (bf16[512,256]{1,0:T(8,128)(2,1)S(1)}, bf16[512,256]{1,0:T(8,128)(2,1)S(1)}, u32[]{:S(2)}, u32[]{:S(2)}) collective-permute-start(bf16[512,256]{1,0:T(8,128)(2,1)S(1)} %collective-permute-done.7.rest_1_), channel_id=1, source_target_pairs={{0,1},{1,0},{2,3},{3,2},{4,5},{5,4},{6,7},{7,6},{8,9},{9,8},{10,11... | collective-permute-start | bytes 786440 | tf_op jit(solution)/shard_map/ppermute | solution.py:35
  41.0 4.3 %piece_far.1 = (f32[272,1024]{1,0:T(8,128)S(1)}, f32[2,512,256]{2,1,0:T(8,128)S(1)}) custom-call(s32[2]{0:T(128)S(1)} %pad_add_fusion.3.at_ref, bf16[2,1,256,8192]{3,2,1,0:T(8,128)(2,1)} %own_ref.7, bf16[2,256,4096]{2,1,0:T(8,128)(2,1)} %collective-permute-done.6.other_ref, bf16[512,256]{1,0:T(8,128)(2,1)} %collective-permute-done.2.rest_0_, ...), custom_call_target="tpu_custom_call" | custom-call | flops 1000 | bytes 1000 | tf_op jit(solution)/shard_map/piece_far/pallas_call | solution.py:168
  45.4 4.2 %piece_near.1 = (f32[272,1024]{1,0:T(8,128)S(1)}, f32[2,512,256]{2,1,0:T(8,128)S(1)}) custom-call(s32[2]{0:T(128)S(1)} %pad_add_fusion.2.at_ref, bf16[2,1,256,8192]{3,2,1,0:T(8,128)(2,1)} %own_ref.7, bf16[2,256,4096]{2,1,0:T(8,128)(2,1)} %collective-permute-done.6.other_ref, bf16[512,256]{1,0:T(8,128)(2,1)S(1)} %collective-permute-done.1.rest_0_, ...), custom_call_target="tpu_custom_call" | custom-call | flops 99999997952 | bytes 100000000 | tf_op jit(solution)/shard_map/piece_near/pallas_call | solution.py:168
  49.8 2.1 %collective-permute-start.18 = (f16[272,1024]{1,0:T(8,128)(2,1)S(1)}, f16[272,1024]{1,0:T(8,128)(2,1)S(1)}, u32[]{:S(2)}, u32[]{:S(2)}) collective-permute-start(f16[272,1024]{1,0:T(8,128)(2,1)S(1)} %convert_element_type.25), channel_id=1, source_target_pairs={{0,1},{1,0},{2,3},{3,2},{4,5},{5,4},{6,7},{7,6},{8,9},{9,8},{10,11... | collective-permute-start | bytes 1671176 | tf_op jit(solution)/shard_map/ppermute | solution.py:35
  51.9 2.4 %collective-permute-done.10.rest_1_ = bf16[512,256]{1,0:T(8,128)(2,1)S(1)} collective-permute-done((bf16[512,256]{1,0:T(8,128)(2,1)S(1)}, bf16[512,256]{1,0:T(8,128)(2,1)S(1)}, u32[]{:S(2)}, u32[]{:S(2)}) %collective-permute-start.10) | collective-permute-done | bytes 262176 | tf_op jit(solution)/shard_map/ppermute | solution.py:35
  54.3 4.2 %piece_middle.1 = (f32[256,1024]{1,0:T(8,128)S(1)}, f32[2,512,256]{2,1,0:T(8,128)S(1)}) custom-call(s32[2]{0:T(128)S(1)} %pad_add_fusion.1.at_ref, bf16[2,1,256,8192]{3,2,1,0:T(8,128)(2,1)} %own_ref.7, bf16[2,256,4096]{2,1,0:T(8,128)(2,1)} %collective-permute-done.6.other_ref, bf16[512,256]{1,0:T(8,128)(2,1)} %collective-permute-done.9.rest_0_, ...), custom_call_target="tpu_custom_call" | custom-call | flops 1000 | bytes 1000 | tf_op jit(solution)/shard_map/piece_middle/pallas_call | solution.py:168
  58.5 2.2 %terms.1 = (f32[200,256]{1,0:T(8,128)S(1)}, f32[200,256]{1,0:T(8,128)S(1)}, f32[200,256]{1,0:T(8,128)S(1)}, f32[200,256]{1,0:T(8,128)S(1)}) custom-call(s32[2]{0:T(128)S(1)} %pad_add_fusion.at_ref, bf16[512,256]{1,0:T(8,128)(2,1)S(1)} %copy-done.3, f32[2,256,256]{2,1,0:T(8,128)S(1)} %copy-done.1, f32[256,256]{1,0:T(8,128)S(1)} %copy-done.5, ...), custom_call_target="tpu_custom_call" | custom-call | flops 1000 | bytes 1000 | tf_op jit(solution)/shard_map/terms/pallas_call | solution.py:277
  60.9 1.8 %collective-permute-start.14 = (f32[200,256]{1,0:T(8,128)S(1)}, f32[200,256]{1,0:T(8,128)S(1)}, u32[]{:S(2)}, u32[]{:S(2)}) collective-permute-start(f32[200,256]{1,0:T(8,128)S(1)} %get-tuple-element.71), channel_id=1, source_target_pairs={{0,12},{4,8},{8,4},{12,0},{1,13},{5,9},{9,5},{13,1},{2,14},{6,10},... | collective-permute-start | bytes 614408 | tf_op jit(solution)/shard_map/ppermute | solution.py:35
  62.7 3.5 %collective-permute-done.11 = f16[272,1024]{1,0:T(8,128)(2,1)S(1)} collective-permute-done((f16[272,1024]{1,0:T(8,128)(2,1)S(1)}, f16[272,1024]{1,0:T(8,128)(2,1)S(1)}, u32[]{:S(2)}, u32[]{:S(2)}) %collective-permute-start.11) | collective-permute-done | bytes 557088 | tf_op jit(solution)/shard_map/ppermute | solution.py:35
  66.9 1.8 %collective-permute-done.13.rest_1_ = f32[200,256]{1,0:T(8,128)S(1)} collective-permute-done((f32[200,256]{1,0:T(8,128)S(1)}, f32[200,256]{1,0:T(8,128)S(1)}, u32[]{:S(2)}, u32[]{:S(2)}) %collective-permute-start.13) | collective-permute-done | bytes 204832 | tf_op jit(solution)/shard_map/ppermute | solution.py:35
  68.8 3.5 %collective-permute-done.14.rest_2_ = f32[200,256]{1,0:T(8,128)S(1)} collective-permute-done((f32[200,256]{1,0:T(8,128)S(1)}, f32[200,256]{1,0:T(8,128)S(1)}, u32[]{:S(2)}, u32[]{:S(2)}) %collective-permute-start.14) | collective-permute-done | bytes 204832 | tf_op jit(solution)/shard_map/ppermute | solution.py:35
  72.3 2.5 %collective-permute-start.15 = (f32[96,256]{1,0:T(8,128)S(1)}, f32[96,256]{1,0:T(8,128)S(1)}, u32[]{:S(2)}, u32[]{:S(2)}) collective-permute-start(f32[96,256]{1,0:T(8,128)S(1)} %get-tuple-element.79), channel_id=1, source_target_pairs={{0,1},{1,0},{2,3},{3,2},{4,5},{5,4},{6,7},{7,6},{8,9},{9,8},{10,11... | collective-permute-start | bytes 294920 | tf_op jit(solution)/shard_map/ppermute | solution.py:35
  74.9 2.4 %collective-permute-start.17 = (f32[96,256]{1,0:T(8,128)S(1)}, f32[96,256]{1,0:T(8,128)S(1)}, u32[]{:S(2)}, u32[]{:S(2)}) collective-permute-start(f32[96,256]{1,0:T(8,128)S(1)} %get-tuple-element.81), channel_id=1, source_target_pairs={{0,3},{1,2},{2,1},{3,0},{4,7},{5,6},{6,5},{7,4},{8,11},{9,10},{10,... | collective-permute-start | bytes 294920 | tf_op jit(solution)/shard_map/ppermute | solution.py:35
  77.3 6.0 %collective-permute-done.18 = f16[272,1024]{1,0:T(8,128)(2,1)S(1)} collective-permute-done((f16[272,1024]{1,0:T(8,128)(2,1)S(1)}, f16[272,1024]{1,0:T(8,128)(2,1)S(1)}, u32[]{:S(2)}, u32[]{:S(2)}) %collective-permute-start.18) | collective-permute-done | bytes 557088 | tf_op jit(solution)/shard_map/ppermute | solution.py:35
  83.3 3.1 %collective-permute-start.23 = (f16[272,512]{1,0:T(8,128)(2,1)S(1)}, f16[272,512]{1,0:T(8,128)(2,1)S(1)}, u32[]{:S(2)}, u32[]{:S(2)}) collective-permute-start(f16[272,512]{1,0:T(8,128)(2,1)S(1)} %convert_element_type.30), channel_id=1, source_target_pairs={{0,2},{1,3},{2,0},{3,1},{4,6},{5,7},{6,4},{7,5},{8,10},{9,11},{10,... | collective-permute-start | bytes 835592 | tf_op jit(solution)/shard_map/ppermute | solution.py:35
  87.3 1.1 %collective-permute-done.16 = f32[96,256]{1,0:T(8,128)S(1)} collective-permute-done((f32[96,256]{1,0:T(8,128)S(1)}, f32[96,256]{1,0:T(8,128)S(1)}, u32[]{:S(2)}, u32[]{:S(2)}) %collective-permute-start.16) | collective-permute-done | bytes 98336 | tf_op jit(solution)/shard_map/ppermute | solution.py:35
  89.9 1.1 %collective-permute-start.22 = (f32[96,256]{1,0:T(8,128)S(1)}, f32[96,256]{1,0:T(8,128)S(1)}, u32[]{:S(2)}, u32[]{:S(2)}) collective-permute-start(f32[96,256]{1,0:T(8,128)S(1)} %add_add_fusion.rest_0_), channel_id=1, source_target_pairs={{0,12},{4,8},{8,4},{12,0},{1,13},{5,9},{9,5},{13,1},{2,14},{6,10},... | collective-permute-start | bytes 294920 | tf_op jit(solution)/shard_map/ppermute | solution.py:35
  91.1 11.3 %collective-permute-done.23 = f16[272,512]{1,0:T(8,128)(2,1)S(1)} collective-permute-done((f16[272,512]{1,0:T(8,128)(2,1)S(1)}, f16[272,512]{1,0:T(8,128)(2,1)S(1)}, u32[]{:S(2)}, u32[]{:S(2)}) %collective-permute-start.23) | collective-permute-done | bytes 278560 | tf_op jit(solution)/shard_map/ppermute | solution.py:35
  102.5 1.4 %final.1 = f32[1024,256]{1,0:T(8,128)} custom-call(f32[256,1024]{1,0:T(8,128)S(1)} %get-tuple-element.86.own_ref, f32[272,1024]{1,0:T(8,128)S(1)} %convert_element_type.28.near_ref, f32[272,512]{1,0:T(8,128)S(1)} %convert_element_type.29.first_ref, f32[272,512]{1,0:T(8,128)S(1)} %convert_element_type.31.second_ref), custom_call_target="tpu_custom_call" | custom-call | flops 1000 | bytes 1000 | tf_op jit(solution)/shard_map/final/pallas_call | solution.py:218
  103.9 1.3 %join.1 = (f32[128,256]{1,0:T(8,128)}, f32[256,256]{1,0:T(8,128)}, f32[2,256]{1,0:T(2,128)}) custom-call(s32[2]{0:T(128)S(1)} %pad_add_fusion.at_ref, f32[96,256]{1,0:T(8,128)S(1)} %add_add_fusion.rest_0_, f32[96,256]{1,0:T(8,128)S(1)} %collective-permute-done.20.rest_1_, f32[96,256]{1,0:T(8,128)S(1)} %collective-permute-done.21.rest_2_, ...), custom_call_target="tpu_custom_call" | custom-call | flops 1000 | bytes 1000 | tf_op jit(solution)/shard_map/join/pallas_call | solution.py:330
  (60 shorter events, 6.4 us)
Async XLA Ops:
  1.6 12.2 %collective-permute-start = (bf16[512,256]{1,0:T(8,128)(2,1)S(1)}, bf16[512,256]{1,0:T(8,128)(2,1)S(1)}, u32[]{:S(2)}, u32[]{:S(2)}) collective-permute-start(bf16[512,256]{1,0:T(8,128)(2,1)S(1)} %slice.6), channel_id=1, source_target_pairs={{0,2},{16,18}} | collective-permute-start | bytes 786440 | tf_op jit(solution)/shard_map/ppermute | solution.py:357
  7.6 9.0 %collective-permute-start.1 = (bf16[512,256]{1,0:T(8,128)(2,1)S(1)}, bf16[512,256]{1,0:T(8,128)(2,1)S(1)}, u32[]{:S(2)}, u32[]{:S(2)}) collective-permute-start(bf16[512,256]{1,0:T(8,128)(2,1)S(1)} %slice.6), channel_id=1, source_target_pairs={{0,1},{1,0},{2,3},{3,2},{4,5},{5,4},{6,7},{7,6},{8,9},{9,8},{10,11... | collective-permute-start | bytes 786440 | tf_op jit(solution)/shard_map/ppermute | solution.py:35
  7.6 12.1 %collective-permute-start.2 = (bf16[512,256]{1,0:T(8,128)(2,1)S(1)}, bf16[512,256]{1,0:T(8,128)(2,1)}, u32[]{:S(2)}, u32[]{:S(2)}) collective-permute-start(bf16[512,256]{1,0:T(8,128)(2,1)S(1)} %slice.6), channel_id=1, source_target_pairs={{0,3},{1,2},{2,1},{3,0},{4,7},{5,6},{6,5},{7,4},{8,11},{9,10},{10,... | collective-permute-start | bytes 786440 | tf_op jit(solution)/shard_map/ppermute | solution.py:35
  8.5 11.5 %copy-start.4 = (bf16[1024,256]{1,0:T(8,128)(2,1)S(1)}, bf16[1024,256]{1,0:T(8,128)(2,1)}, u32[]{:S(2)}) copy-start(bf16[1024,256]{1,0:T(8,128)(2,1)} %rest_0_.1) | copy-start | bytes 1572868
  13.4 13.1 %copy-start.6 = (f32[2,256]{1,0:T(2,128)S(1)}, f32[2,256]{1,0:T(2,128)}, u32[]{:S(2)}) copy-start(f32[2,256]{1,0:T(2,128)} %scales_ref.1) | copy-start | bytes 6148
  13.4 13.2 %copy-start.5 = (f32[256,256]{1,0:T(8,128)S(1)}, f32[256,256]{1,0:T(8,128)}, u32[]{:S(2)}) copy-start(f32[256,256]{1,0:T(8,128)} %core_ref.1) | copy-start | bytes 786436
  19.7 13.8 %collective-permute-start.6 = (bf16[2,256,4096]{2,1,0:T(8,128)(2,1)}, bf16[2,256,4096]{2,1,0:T(8,128)(2,1)}, u32[]{:S(2)}, u32[]{:S(2)}) collective-permute-start(bf16[2,256,4096]{2,1,0:T(8,128)(2,1)} %half.1), channel_id=1, source_target_pairs={{0,4},{4,0},{8,12},{12,8},{1,5},{5,1},{9,13},{13,9},{2,6},{6,2},{1... | collective-permute-start | bytes 12582920 | tf_op jit(solution)/shard_map/ppermute | solution.py:35
  21.0 9.7 %collective-permute-start.3 = (bf16[512,256]{1,0:T(8,128)(2,1)S(1)}, bf16[512,256]{1,0:T(8,128)(2,1)S(1)}, u32[]{:S(2)}, u32[]{:S(2)}) collective-permute-start(bf16[512,256]{1,0:T(8,128)(2,1)S(1)} %get-tuple-element.99), channel_id=1, source_target_pairs={{0,4},{1,5},{2,6},{3,7},{16,20},{17,21},{18,22},{19,23}} | collective-permute-start | bytes 786440 | tf_op jit(solution)/shard_map/ppermute | solution.py:364
  23.4 7.3 %collective-permute-start.4 = (bf16[512,256]{1,0:T(8,128)(2,1)S(1)}, bf16[512,256]{1,0:T(8,128)(2,1)S(1)}, u32[]{:S(2)}, u32[]{:S(2)}) collective-permute-start(bf16[512,256]{1,0:T(8,128)(2,1)S(1)} %get-tuple-element.99), channel_id=1, source_target_pairs={{0,8},{1,9},{2,10},{3,11},{16,24},{17,25},{18,26},{19,27}} | collective-permute-start | bytes 786440 | tf_op jit(solution)/shard_map/ppermute | solution.py:364
  25.1 7.6 %collective-permute-start.5 = (bf16[512,256]{1,0:T(8,128)(2,1)S(1)}, bf16[512,256]{1,0:T(8,128)(2,1)S(1)}, u32[]{:S(2)}, u32[]{:S(2)}) collective-permute-start(bf16[512,256]{1,0:T(8,128)(2,1)S(1)} %get-tuple-element.99), channel_id=1, source_target_pairs={{0,12},{1,13},{2,14},{3,15},{16,28},{17,29},{18,30},{19,31}} | collective-permute-start | bytes 786440 | tf_op jit(solution)/shard_map/ppermute | solution.py:364
  26.8 6.0 %copy-start = (f32[2,256,256]{2,1,0:T(8,128)}, f32[2,256,256]{2,1,0:T(8,128)S(1)}, u32[]{:S(2)}) copy-start(f32[2,256,256]{2,1,0:T(8,128)S(1)} %multiply_multiply_fusion.inner_ref) | copy-start | bytes 1572868
  26.8 10.8 %collective-permute-start.7 = (bf16[512,256]{1,0:T(8,128)(2,1)S(1)}, bf16[512,256]{1,0:T(8,128)(2,1)S(1)}, u32[]{:S(2)}, u32[]{:S(2)}) collective-permute-start(bf16[512,256]{1,0:T(8,128)(2,1)S(1)} %get-tuple-element.98), channel_id=1, source_target_pairs={{0,3},{1,2},{2,1},{3,0},{4,7},{5,6},{6,5},{7,4},{8,11},{9,10},{10,... | collective-permute-start | bytes 786440 | tf_op jit(solution)/shard_map/ppermute | solution.py:35
  30.7 14.7 %collective-permute-start.8 = (bf16[512,256]{1,0:T(8,128)(2,1)S(1)}, bf16[512,256]{1,0:T(8,128)(2,1)S(1)}, u32[]{:S(2)}, u32[]{:S(2)}) collective-permute-start(bf16[512,256]{1,0:T(8,128)(2,1)S(1)} %get-tuple-element.98), channel_id=1, source_target_pairs={{0,1},{1,0},{2,3},{3,2},{4,5},{5,4},{6,7},{7,6},{8,9},{9,8},{10,11... | collective-permute-start | bytes 786440 | tf_op jit(solution)/shard_map/ppermute | solution.py:35
  30.7 21.2 %collective-permute-start.9 = (bf16[512,256]{1,0:T(8,128)(2,1)}, bf16[512,256]{1,0:T(8,128)(2,1)}, u32[]{:S(2)}, u32[]{:S(2)}) collective-permute-start(bf16[512,256]{1,0:T(8,128)(2,1)} %collective-permute-done.2.rest_0_), channel_id=1, source_target_pairs={{0,1},{1,0},{2,3},{3,2},{4,5},{5,4},{6,7},{7,6},{8,9},{9,8},{10,11... | collective-permute-start | bytes 786440 | tf_op jit(solution)/shard_map/ppermute | solution.py:35
  32.8 0.8 copy-start.2
  37.6 16.7 %collective-permute-start.10 = (bf16[512,256]{1,0:T(8,128)(2,1)S(1)}, bf16[512,256]{1,0:T(8,128)(2,1)S(1)}, u32[]{:S(2)}, u32[]{:S(2)}) collective-permute-start(bf16[512,256]{1,0:T(8,128)(2,1)S(1)} %collective-permute-done.7.rest_1_), channel_id=1, source_target_pairs={{0,1},{1,0},{2,3},{3,2},{4,5},{5,4},{6,7},{7,6},{8,9},{9,8},{10,11... | collective-permute-start | bytes 786440 | tf_op jit(solution)/shard_map/ppermute | solution.py:35
  45.4 20.9 %collective-permute-start.11 = (f16[272,1024]{1,0:T(8,128)(2,1)S(1)}, f16[272,1024]{1,0:T(8,128)(2,1)S(1)}, u32[]{:S(2)}, u32[]{:S(2)}) collective-permute-start(f16[272,1024]{1,0:T(8,128)(2,1)S(1)} %convert_element_type.24), channel_id=1, source_target_pairs={{0,1},{1,0},{2,3},{3,2},{4,5},{5,4},{6,7},{7,6},{8,9},{9,8},{10,11... | collective-permute-start | bytes 1671176 | tf_op jit(solution)/shard_map/ppermute | solution.py:35
  49.8 33.6 %collective-permute-start.18 = (f16[272,1024]{1,0:T(8,128)(2,1)S(1)}, f16[272,1024]{1,0:T(8,128)(2,1)S(1)}, u32[]{:S(2)}, u32[]{:S(2)}) collective-permute-start(f16[272,1024]{1,0:T(8,128)(2,1)S(1)} %convert_element_type.25), channel_id=1, source_target_pairs={{0,1},{1,0},{2,3},{3,2},{4,5},{5,4},{6,7},{7,6},{8,9},{9,8},{10,11... | collective-permute-start | bytes 1671176 | tf_op jit(solution)/shard_map/ppermute | solution.py:35
  54.3 4.2 %copy-start.1 = (f32[2,256,256]{2,1,0:T(8,128)S(1)}, f32[2,256,256]{2,1,0:T(8,128)}, u32[]{:S(2)}) copy-start(f32[2,256,256]{2,1,0:T(8,128)} %copy-done) | copy-start | bytes 1572868
  54.3 4.2 %copy-start.3 = (bf16[512,256]{1,0:T(8,128)(2,1)S(1)}, bf16[512,256]{1,0:T(8,128)(2,1)}, u32[]{:S(2)}) copy-start(bf16[512,256]{1,0:T(8,128)(2,1)} %copy-done.2) | copy-start | bytes 786436
  60.8 1.9 %collective-permute-start.12 = (f32[200,256]{1,0:T(8,128)S(1)}, f32[200,256]{1,0:T(8,128)S(1)}, u32[]{:S(2)}, u32[]{:S(2)}) collective-permute-start(f32[200,256]{1,0:T(8,128)S(1)} %get-tuple-element.68), channel_id=1, source_target_pairs={{0,4},{4,0},{8,12},{12,8},{1,5},{5,1},{9,13},{13,9},{2,6},{6,2},{1... | collective-permute-start | bytes 614408 | tf_op jit(solution)/shard_map/ppermute | solution.py:35
  60.8 7.9 %collective-permute-start.13 = (f32[200,256]{1,0:T(8,128)S(1)}, f32[200,256]{1,0:T(8,128)S(1)}, u32[]{:S(2)}, u32[]{:S(2)}) collective-permute-start(f32[200,256]{1,0:T(8,128)S(1)} %get-tuple-element.70), channel_id=1, source_target_pairs={{0,8},{4,12},{8,0},{12,4},{1,9},{5,13},{9,1},{13,5},{2,10},{6,14},... | collective-permute-start | bytes 614408 | tf_op jit(solution)/shard_map/ppermute | solution.py:35
  60.9 11.3 %collective-permute-start.14 = (f32[200,256]{1,0:T(8,128)S(1)}, f32[200,256]{1,0:T(8,128)S(1)}, u32[]{:S(2)}, u32[]{:S(2)}) collective-permute-start(f32[200,256]{1,0:T(8,128)S(1)} %get-tuple-element.71), channel_id=1, source_target_pairs={{0,12},{4,8},{8,4},{12,0},{1,13},{5,9},{9,5},{13,1},{2,14},{6,10},... | collective-permute-start | bytes 614408 | tf_op jit(solution)/shard_map/ppermute | solution.py:35
  66.9 22.1 %collective-permute-start.19 = (f16[272,512]{1,0:T(8,128)(2,1)S(1)}, f16[272,512]{1,0:T(8,128)(2,1)S(1)}, u32[]{:S(2)}, u32[]{:S(2)}) collective-permute-start(f16[272,512]{1,0:T(8,128)(2,1)S(1)} %convert_element_type.27), channel_id=1, source_target_pairs={{0,2},{1,3},{2,0},{3,1},{4,6},{5,7},{6,4},{7,5},{8,10},{9,11},{10,... | collective-permute-start | bytes 835592 | tf_op jit(solution)/shard_map/ppermute | solution.py:35
  72.3 15.0 %collective-permute-start.15 = (f32[96,256]{1,0:T(8,128)S(1)}, f32[96,256]{1,0:T(8,128)S(1)}, u32[]{:S(2)}, u32[]{:S(2)}) collective-permute-start(f32[96,256]{1,0:T(8,128)S(1)} %get-tuple-element.79), channel_id=1, source_target_pairs={{0,1},{1,0},{2,3},{3,2},{4,5},{5,4},{6,7},{7,6},{8,9},{9,8},{10,11... | collective-permute-start | bytes 294920 | tf_op jit(solution)/shard_map/ppermute | solution.py:35
  74.9 13.6 %collective-permute-start.16 = (f32[96,256]{1,0:T(8,128)S(1)}, f32[96,256]{1,0:T(8,128)S(1)}, u32[]{:S(2)}, u32[]{:S(2)}) collective-permute-start(f32[96,256]{1,0:T(8,128)S(1)} %get-tuple-element.80), channel_id=1, source_target_pairs={{0,2},{1,3},{2,0},{3,1},{4,6},{5,7},{6,4},{7,5},{8,10},{9,11},{10,... | collective-permute-start | bytes 294920 | tf_op jit(solution)/shard_map/ppermute | solution.py:35
  74.9 14.1 %collective-permute-start.17 = (f32[96,256]{1,0:T(8,128)S(1)}, f32[96,256]{1,0:T(8,128)S(1)}, u32[]{:S(2)}, u32[]{:S(2)}) collective-permute-start(f32[96,256]{1,0:T(8,128)S(1)} %get-tuple-element.81), channel_id=1, source_target_pairs={{0,3},{1,2},{2,1},{3,0},{4,7},{5,6},{6,5},{7,4},{8,11},{9,10},{10,... | collective-permute-start | bytes 294920 | tf_op jit(solution)/shard_map/ppermute | solution.py:35
  83.3 19.1 %collective-permute-start.23 = (f16[272,512]{1,0:T(8,128)(2,1)S(1)}, f16[272,512]{1,0:T(8,128)(2,1)S(1)}, u32[]{:S(2)}, u32[]{:S(2)}) collective-permute-start(f16[272,512]{1,0:T(8,128)(2,1)S(1)} %convert_element_type.30), channel_id=1, source_target_pairs={{0,2},{1,3},{2,0},{3,1},{4,6},{5,7},{6,4},{7,5},{8,10},{9,11},{10,... | collective-permute-start | bytes 835592 | tf_op jit(solution)/shard_map/ppermute | solution.py:35
  89.0 14.9 %collective-permute-start.20 = (f32[96,256]{1,0:T(8,128)S(1)}, f32[96,256]{1,0:T(8,128)S(1)}, u32[]{:S(2)}, u32[]{:S(2)}) collective-permute-start(f32[96,256]{1,0:T(8,128)S(1)} %add_add_fusion.rest_0_), channel_id=1, source_target_pairs={{0,4},{4,0},{8,12},{12,8},{1,5},{5,1},{9,13},{13,9},{2,6},{6,2},{1... | collective-permute-start | bytes 294920 | tf_op jit(solution)/shard_map/ppermute | solution.py:35
  89.1 14.8 %collective-permute-start.21 = (f32[96,256]{1,0:T(8,128)S(1)}, f32[96,256]{1,0:T(8,128)S(1)}, u32[]{:S(2)}, u32[]{:S(2)}) collective-permute-start(f32[96,256]{1,0:T(8,128)S(1)} %add_add_fusion.rest_0_), channel_id=1, source_target_pairs={{0,8},{4,12},{8,0},{12,4},{1,9},{5,13},{9,1},{13,5},{2,10},{6,14},... | collective-permute-start | bytes 294920 | tf_op jit(solution)/shard_map/ppermute | solution.py:35
  89.9 14.0 %collective-permute-start.22 = (f32[96,256]{1,0:T(8,128)S(1)}, f32[96,256]{1,0:T(8,128)S(1)}, u32[]{:S(2)}, u32[]{:S(2)}) collective-permute-start(f32[96,256]{1,0:T(8,128)S(1)} %add_add_fusion.rest_0_), channel_id=1, source_target_pairs={{0,12},{4,8},{8,4},{12,0},{1,13},{5,9},{9,5},{13,1},{2,14},{6,10},... | collective-permute-start | bytes 294920 | tf_op jit(solution)/shard_map/ppermute | solution.py:35

commit v5 on v4

--- a/solution.py
+++ b/solution.py
@@ -62,7 +62,7 @@
             pl.BlockSpec(memory_space=pltpu.VMEM),
         ],
         out_specs=[pl.BlockSpec(memory_space=pltpu.VMEM)] * 2,
-        compiler_params=pltpu.CompilerParams(vmem_limit_bytes=VMEM_LIMIT),
+        compiler_params=pltpu.CompilerParams(vmem_limit_bytes=VMEM_SMALL),
         cost_estimate=SMALL,
         name="mapped",
     )(core_at, window, inner)
@@ -120,21 +120,12 @@
             parts.append((flows.astype(F32) - model).astype(BF16))
     residual = jnp.concatenate(parts, 0)
     grad = dot(turned_ref[...], residual, NN)
-    if kind == "own":
+    if kind == "plain":
         grads[0][:, pl.ds(at, width)] = grad
     else:
         value, exponent = encoded(grad)
-        if kind == "whole":
-            grads[0][:P_SIZE, pl.ds(at, width)] = value
-            grads[0][P_SIZE:, pl.ds(at, width)] = exponent
-        else:
-            for index, ref in enumerate(grads):
-
-                @pl.when(step == index)
-                def _():
-                    ref[:P_SIZE, :] = value
-                    ref[P_SIZE:, :] = exponent
-
+        grads[0][:P_SIZE, pl.ds(at, width)] = value
+        grads[0][P_SIZE:, pl.ds(at, width)] = exponent
     projected = dot(residual, block, NN).reshape(proj_ref.shape)
 
     @pl.when(step == 0)
@@ -151,9 +142,8 @@
     rows, width = size // 2, sum(block.shape[0] for block in blocks) // 2
     vmem = pl.BlockSpec(memory_space=pltpu.VMEM)
     grads = {
-        "own": [(P_SIZE, 2 * width)],
-        "whole": [(P_SIZE + 16, 2 * width)],
-        "split": [(P_SIZE + 16, width)] * 2,
+        "plain": [(P_SIZE, 2 * width)],
+        "coded": [(P_SIZE + 16, 2 * width)],
     }[kind]
     spec = pltpu.PrefetchScalarGridSpec(
         num_scalar_prefetch=1,
@@ -199,7 +189,7 @@
         ],
         out_specs=[vmem, vmem],
         out_shape=[jax.ShapeDtypeStruct((P_SIZE + 16, width), F32)] * 2,
-        compiler_params=pltpu.CompilerParams(vmem_limit_bytes=VMEM_LIMIT),
+        compiler_params=pltpu.CompilerParams(vmem_limit_bytes=VMEM_SMALL),
         cost_estimate=SMALL,
         name="relay",
     )(received, own)
@@ -226,7 +216,7 @@
         ],
         out_specs=pl.BlockSpec((width, P_SIZE), lambda j: (j, 0)),
         out_shape=jax.ShapeDtypeStruct((columns, P_SIZE), F32),
-        compiler_params=pltpu.CompilerParams(vmem_limit_bytes=VMEM_LIMIT),
+        compiler_params=pltpu.CompilerParams(vmem_limit_bytes=VMEM_SMALL),
         cost_estimate=SMALL,
         name="final",
     )(own, near, *halves)
@@ -280,7 +270,7 @@
         out_specs=[vmem] * 4,
         out_shape=[jax.ShapeDtypeStruct((high, P_SIZE), F32)] * 4,
         scratch_shapes=[pltpu.VMEM((size + P_SIZE, P_SIZE), F32)],
-        compiler_params=pltpu.CompilerParams(vmem_limit_bytes=VMEM_LIMIT),
+        compiler_params=pltpu.CompilerParams(vmem_limit_bytes=VMEM_SMALL),
         cost_estimate=SMALL,
         name="terms",
     )(place, window, inner, core, scales, scales.T, *projs)
@@ -358,10 +348,9 @@
     far = [swapped(value, "cuts", 3) for value in parts]
     near = [swapped(value, "cuts", 1) for value in parts]
     second, near[0], far[0], give = hold((second, near[0], far[0], give))
-    first = near[0]
     other = swapped(give, "tile", 1)
-    line = jnp.where(cut == 0, parts[0], jnp.where(cut == 1, first, jnp.where(cut == 2, second, far[0])))
-    out = [lax.ppermute(line, "tile", [(0, target)]) for target in (1, 2, 3)]
+    line = jnp.where(cut == 0, parts[0], jnp.where(cut == 1, near[0], jnp.where(cut == 2, second, far[0])))
+    out = [lax.ppermute(line, "tile", [(0, target)]) for target in (3, 2, 1)]
     window = jnp.where(tile == 0, line, sum(out[1:], out[0]))
     mapped, turned = mapped_call(core_at, window, inner)
 
@@ -371,16 +360,16 @@
             where, _ = hold((where, after))
         return piece_call(where, trade, other, blocks, mapped, turned, before, kind, cost, label)
 
-    grad_own, proj = piece_of(cut, [factor], "own", LARGE, "piece_own", [])
+    grad_own, proj = piece_of(cut, [factor], "plain", LARGE, "piece_own", [])
     far[1], _ = hold((far[1], proj))
     middle = [swapped(value, "cuts", 1) for value in far]
-    grad_far, proj = piece_of(cut ^ 3, far, "whole", SMALL, "piece_far", [proj], proj)
+    grad_far, proj = piece_of(cut ^ 3, far, "coded", SMALL, "piece_far", [proj], proj)
     grad_far = grad_far.astype(F16)
     joined = swapped(grad_far, "cuts", 1)
-    grad_near, proj = piece_of(cut ^ 1, near, "whole", LARGE, "piece_near", [proj], grad_far)
+    grad_near, proj = piece_of(cut ^ 1, near, "coded", LARGE, "piece_near", [proj], grad_far)
     grad_near = grad_near.astype(F16)
     from_near = swapped(grad_near, "cuts", 1)
-    grad_middle, proj = piece_of(cut ^ 2, middle, "own", SMALL, "piece_middle", [proj], grad_near)
+    grad_middle, proj = piece_of(cut ^ 2, middle, "plain", SMALL, "piece_middle", [proj], grad_near)
 
     own, *send = terms_call(cuts, place, window, inner, core, scales, [proj])
     received = [swapped(value, "tile", mask + 1) for mask, value in enumerate(send)]

time: 106 us -> 105 us (level)
  starting transfers between devices: 35.7 us -> 31.9 us
  waiting for transfers between devices: 37.4 us -> 40.4 us
    ppermute x20, starting transfers between devices: 24.3 us -> 19.8 us  [swapped(): return lax.ppermute(value, axis, pairs)]
    ppermute x3, waiting for transfers between devices: 0.01 us -> 1.6 us  [body_line(): out = [lax.ppermute(line, 'tile', [(0, target)]) for target in (3, 2, 1)]]
    ppermute x20, waiting for transfers between devices: 37.1 us -> 38.4 us  [swapped(): return lax.ppermute(value, axis, pairs)]
where the time goes in v5:
time: 105 us; the launch traced here: 104 us
  waiting for transfers between devices  40.4 us (38%)
  starting transfers between devices  31.9 us (30%)
  Pallas kernels  27.9 us (27%)
  other arithmetic  2.15 us (2%)
  local copies, waits for them, and re-layouts  1.13 us (1%)
    ppermute x20, waiting for transfers between devices, swapped(): return lax.ppermute(value, axis, pairs)  38.4 us
    ppermute x20, starting transfers between devices, swapped(): return lax.ppermute(value, axis, pairs)  19.8 us
    pallas_call x4, Pallas kernels, piece_call(): pl.pallas_call(functools.partial(piece_kernel, kind, len(before) > 0, len...  16.6 us
    ppermute x3, starting transfers between devices, body_line(): out = [lax.ppermute(line, 'tile', [(0, target)]) for target in (3, 2, 1)]  6.11 us
    ppermute x1, starting transfers between devices, body_line(): second = lax.ppermute(parts[0], ('tile', 'cuts'), [(0, 2)])  5.96 us
    pallas_call x1, Pallas kernels, half_call(): pl.pallas_call(half_kernel, grid_spec=pltpu.PrefetchScalarGridSpec(num_sc...  4.95 us
    pallas_call x1, Pallas kernels, terms_call(): pl.pallas_call(functools.partial(terms_kernel, cuts), in_specs=[pl.BlockS...  2.22 us
  transfers between devices with their start and end apart: 24, of which 12 were waited for; matrix products, arithmetic and copies ran while one was open for 2% of the time, Pallas kernels for 25%

profile of v5, /device:TPU:0, one launch (start us, length us, event | category | flops | bytes accessed | tf_op | source)
XLA Modules:
  0.0 104.3 jit_solution(15984646177329842001)
XLA Ops:
  1.6 6.0 %collective-permute-start = (bf16[512,256]{1,0:T(8,128)(2,1)S(1)}, bf16[512,256]{1,0:T(8,128)(2,1)S(1)}, u32[]{:S(2)}, u32[]{:S(2)}) collective-permute-start(bf16[512,256]{1,0:T(8,128)(2,1)S(1)} %slice.6), channel_id=1, source_target_pairs={{0,2},{16,18}} | collective-permute-start | bytes 786440 | tf_op jit(solution)/shard_map/ppermute | solution.py:347
  8.5 5.0 %half.1 = bf16[2,256,4096]{2,1,0:T(8,128)(2,1)} custom-call(s32[1]{0:T(128)} %bitcast.2.at_ref, bf16[2,1,256,8192]{3,2,1,0:T(8,128)(2,1)} %own_ref.7), custom_call_target="tpu_custom_call" | custom-call | flops 99999997952 | bytes 100000000 | tf_op jit(solution)/shard_map/half/pallas_call | solution.py:79
  13.8 2.8 %collective-permute-done.1.rest_0_ = bf16[512,256]{1,0:T(8,128)(2,1)S(1)} collective-permute-done((bf16[512,256]{1,0:T(8,128)(2,1)S(1)}, bf16[512,256]{1,0:T(8,128)(2,1)S(1)}, u32[]{:S(2)}, u32[]{:S(2)}) %collective-permute-start.1) | collective-permute-done | bytes 262176 | tf_op jit(solution)/shard_map/ppermute | solution.py:35
  16.6 3.1 %collective-permute-done.2.rest_0_ = bf16[512,256]{1,0:T(8,128)(2,1)} collective-permute-done((bf16[512,256]{1,0:T(8,128)(2,1)S(1)}, bf16[512,256]{1,0:T(8,128)(2,1)}, u32[]{:S(2)}, u32[]{:S(2)}) %collective-permute-start.2) | collective-permute-done | bytes 262176 | tf_op jit(solution)/shard_map/ppermute | solution.py:35
  20.0 1.0 fusion
  21.0 3.5 %collective-permute-start.3 = (bf16[512,256]{1,0:T(8,128)(2,1)S(1)}, bf16[512,256]{1,0:T(8,128)(2,1)S(1)}, u32[]{:S(2)}, u32[]{:S(2)}) collective-permute-start(bf16[512,256]{1,0:T(8,128)(2,1)S(1)} %get-tuple-element.99), channel_id=1, source_target_pairs={{0,12},{1,13},{2,14},{3,15},{16,28},{17,29},{18,30},{19,31}} | collective-permute-start | bytes 786440 | tf_op jit(solution)/shard_map/ppermute | solution.py:353
  24.5 1.3 %collective-permute-start.4 = (bf16[512,256]{1,0:T(8,128)(2,1)S(1)}, bf16[512,256]{1,0:T(8,128)(2,1)S(1)}, u32[]{:S(2)}, u32[]{:S(2)}) collective-permute-start(bf16[512,256]{1,0:T(8,128)(2,1)S(1)} %get-tuple-element.99), channel_id=1, source_target_pairs={{0,8},{1,9},{2,10},{3,11},{16,24},{17,25},{18,26},{19,27}} | collective-permute-start | bytes 786440 | tf_op jit(solution)/shard_map/ppermute | solution.py:353
  25.8 1.3 %collective-permute-start.5 = (bf16[512,256]{1,0:T(8,128)(2,1)S(1)}, bf16[512,256]{1,0:T(8,128)(2,1)S(1)}, u32[]{:S(2)}, u32[]{:S(2)}) collective-permute-start(bf16[512,256]{1,0:T(8,128)(2,1)S(1)} %get-tuple-element.99), channel_id=1, source_target_pairs={{0,4},{1,5},{2,6},{3,7},{16,20},{17,21},{18,22},{19,23}} | collective-permute-start | bytes 786440 | tf_op jit(solution)/shard_map/ppermute | solution.py:353
  27.5 2.0 %collective-permute-start.7 = (bf16[512,256]{1,0:T(8,128)(2,1)S(1)}, bf16[512,256]{1,0:T(8,128)(2,1)S(1)}, u32[]{:S(2)}, u32[]{:S(2)}) collective-permute-start(bf16[512,256]{1,0:T(8,128)(2,1)S(1)} %get-tuple-element.98), channel_id=1, source_target_pairs={{0,3},{1,2},{2,1},{3,0},{4,7},{5,6},{6,5},{7,4},{8,11},{9,10},{10,... | collective-permute-start | bytes 786440 | tf_op jit(solution)/shard_map/ppermute | solution.py:35
  29.6 1.6 %collective-permute-done.4 = bf16[512,256]{1,0:T(8,128)(2,1)S(1)} collective-permute-done((bf16[512,256]{1,0:T(8,128)(2,1)S(1)}, bf16[512,256]{1,0:T(8,128)(2,1)S(1)}, u32[]{:S(2)}, u32[]{:S(2)}) %collective-permute-start.4) | collective-permute-done | bytes 262176 | tf_op jit(solution)/shard_map/ppermute | solution.py:353
  32.6 4.0 %piece_own.1 = (f32[256,1024]{1,0:T(8,128)S(1)}, f32[2,512,256]{2,1,0:T(8,128)S(1)}) custom-call(s32[2]{0:T(128)S(1)} %pad_add_fusion.4.at_ref, bf16[2,1,256,8192]{3,2,1,0:T(8,128)(2,1)} %own_ref.7, bf16[2,256,4096]{2,1,0:T(8,128)(2,1)} %collective-permute-done.6.other_ref, bf16[1024,256]{1,0:T(8,128)(2,1)S(1)} %copy-done.4, ...), custom_call_target="tpu_custom_call" | custom-call | flops 99999997952 | bytes 100000000 | tf_op jit(solution)/shard_map/piece_own/pallas_call | solution.py:158
  36.6 2.0 %collective-permute-done.7.rest_1_ = bf16[512,256]{1,0:T(8,128)(2,1)S(1)} collective-permute-done((bf16[512,256]{1,0:T(8,128)(2,1)S(1)}, bf16[512,256]{1,0:T(8,128)(2,1)S(1)}, u32[]{:S(2)}, u32[]{:S(2)}) %collective-permute-start.7) | collective-permute-done | bytes 262176 | tf_op jit(solution)/shard_map/ppermute | solution.py:35
  38.6 2.3 %collective-permute-start.10 = (bf16[512,256]{1,0:T(8,128)(2,1)S(1)}, bf16[512,256]{1,0:T(8,128)(2,1)S(1)}, u32[]{:S(2)}, u32[]{:S(2)}) collective-permute-start(bf16[512,256]{1,0:T(8,128)(2,1)S(1)} %collective-permute-done.7.rest_1_), channel_id=1, source_target_pairs={{0,1},{1,0},{2,3},{3,2},{4,5},{5,4},{6,7},{7,6},{8,9},{9,8},{10,11... | collective-permute-start | bytes 786440 | tf_op jit(solution)/shard_map/ppermute | solution.py:35
  41.0 4.3 %piece_far.1 = (f32[272,1024]{1,0:T(8,128)S(1)}, f32[2,512,256]{2,1,0:T(8,128)S(1)}) custom-call(s32[2]{0:T(128)S(1)} %pad_add_fusion.3.at_ref, bf16[2,1,256,8192]{3,2,1,0:T(8,128)(2,1)} %own_ref.7, bf16[2,256,4096]{2,1,0:T(8,128)(2,1)} %collective-permute-done.6.other_ref, bf16[512,256]{1,0:T(8,128)(2,1)} %collective-permute-done.2.rest_0_, ...), custom_call_target="tpu_custom_call" | custom-call | flops 1000 | bytes 1000 | tf_op jit(solution)/shard_map/piece_far/pallas_call | solution.py:158
  45.4 4.2 %piece_near.1 = (f32[272,1024]{1,0:T(8,128)S(1)}, f32[2,512,256]{2,1,0:T(8,128)S(1)}) custom-call(s32[2]{0:T(128)S(1)} %pad_add_fusion.2.at_ref, bf16[2,1,256,8192]{3,2,1,0:T(8,128)(2,1)} %own_ref.7, bf16[2,256,4096]{2,1,0:T(8,128)(2,1)} %collective-permute-done.6.other_ref, bf16[512,256]{1,0:T(8,128)(2,1)S(1)} %collective-permute-done.1.rest_0_, ...), custom_call_target="tpu_custom_call" | custom-call | flops 99999997952 | bytes 100000000 | tf_op jit(solution)/shard_map/piece_near/pallas_call | solution.py:158
  49.7 2.1 %collective-permute-start.18 = (f16[272,1024]{1,0:T(8,128)(2,1)S(1)}, f16[272,1024]{1,0:T(8,128)(2,1)S(1)}, u32[]{:S(2)}, u32[]{:S(2)}) collective-permute-start(f16[272,1024]{1,0:T(8,128)(2,1)S(1)} %convert_element_type.25), channel_id=1, source_target_pairs={{0,1},{1,0},{2,3},{3,2},{4,5},{5,4},{6,7},{7,6},{8,9},{9,8},{10,11... | collective-permute-start | bytes 1671176 | tf_op jit(solution)/shard_map/ppermute | solution.py:35
  51.9 1.3 %collective-permute-done.10.rest_1_ = bf16[512,256]{1,0:T(8,128)(2,1)S(1)} collective-permute-done((bf16[512,256]{1,0:T(8,128)(2,1)S(1)}, bf16[512,256]{1,0:T(8,128)(2,1)S(1)}, u32[]{:S(2)}, u32[]{:S(2)}) %collective-permute-start.10) | collective-permute-done | bytes 262176 | tf_op jit(solution)/shard_map/ppermute | solution.py:35
  53.2 4.1 %piece_middle.1 = (f32[256,1024]{1,0:T(8,128)S(1)}, f32[2,512,256]{2,1,0:T(8,128)S(1)}) custom-call(s32[2]{0:T(128)S(1)} %pad_add_fusion.1.at_ref, bf16[2,1,256,8192]{3,2,1,0:T(8,128)(2,1)} %own_ref.7, bf16[2,256,4096]{2,1,0:T(8,128)(2,1)} %collective-permute-done.6.other_ref, bf16[512,256]{1,0:T(8,128)(2,1)} %collective-permute-done.9.rest_0_, ...), custom_call_target="tpu_custom_call" | custom-call | flops 1000 | bytes 1000 | tf_op jit(solution)/shard_map/piece_middle/pallas_call | solution.py:158
  57.4 2.2 %terms.1 = (f32[200,256]{1,0:T(8,128)S(1)}, f32[200,256]{1,0:T(8,128)S(1)}, f32[200,256]{1,0:T(8,128)S(1)}, f32[200,256]{1,0:T(8,128)S(1)}) custom-call(s32[2]{0:T(128)S(1)} %pad_add_fusion.at_ref, bf16[512,256]{1,0:T(8,128)(2,1)S(1)} %copy-done.3, f32[2,256,256]{2,1,0:T(8,128)S(1)} %copy-done.1, f32[256,256]{1,0:T(8,128)S(1)} %copy-done.5, ...), custom_call_target="tpu_custom_call" | custom-call | flops 1000 | bytes 1000 | tf_op jit(solution)/shard_map/terms/pallas_call | solution.py:267
  59.7 1.8 %collective-permute-start.14 = (f32[200,256]{1,0:T(8,128)S(1)}, f32[200,256]{1,0:T(8,128)S(1)}, u32[]{:S(2)}, u32[]{:S(2)}) collective-permute-start(f32[200,256]{1,0:T(8,128)S(1)} %get-tuple-element.71), channel_id=1, source_target_pairs={{0,12},{4,8},{8,4},{12,0},{1,13},{5,9},{9,5},{13,1},{2,14},{6,10},... | collective-permute-start | bytes 614408 | tf_op jit(solution)/shard_map/ppermute | solution.py:35
  61.5 3.6 %collective-permute-done.11 = f16[272,1024]{1,0:T(8,128)(2,1)S(1)} collective-permute-done((f16[272,1024]{1,0:T(8,128)(2,1)S(1)}, f16[272,1024]{1,0:T(8,128)(2,1)S(1)}, u32[]{:S(2)}, u32[]{:S(2)}) %collective-permute-start.11) | collective-permute-done | bytes 557088 | tf_op jit(solution)/shard_map/ppermute | solution.py:35
  65.8 2.9 %collective-permute-start.19 = (f16[272,512]{1,0:T(8,128)(2,1)S(1)}, f16[272,512]{1,0:T(8,128)(2,1)S(1)}, u32[]{:S(2)}, u32[]{:S(2)}) collective-permute-start(f16[272,512]{1,0:T(8,128)(2,1)S(1)} %convert_element_type.27), channel_id=1, source_target_pairs={{0,2},{1,3},{2,0},{3,1},{4,6},{5,7},{6,4},{7,5},{8,10},{9,11},{10,... | collective-permute-start | bytes 835592 | tf_op jit(solution)/shard_map/ppermute | solution.py:35
  68.7 2.4 %collective-permute-done.14.rest_2_ = f32[200,256]{1,0:T(8,128)S(1)} collective-permute-done((f32[200,256]{1,0:T(8,128)S(1)}, f32[200,256]{1,0:T(8,128)S(1)}, u32[]{:S(2)}, u32[]{:S(2)}) %collective-permute-start.14) | collective-permute-done | bytes 204832 | tf_op jit(solution)/shard_map/ppermute | solution.py:35
  71.1 2.6 %collective-permute-start.15 = (f32[96,256]{1,0:T(8,128)S(1)}, f32[96,256]{1,0:T(8,128)S(1)}, u32[]{:S(2)}, u32[]{:S(2)}) collective-permute-start(f32[96,256]{1,0:T(8,128)S(1)} %get-tuple-element.79), channel_id=1, source_target_pairs={{0,1},{1,0},{2,3},{3,2},{4,5},{5,4},{6,7},{7,6},{8,9},{9,8},{10,11... | collective-permute-start | bytes 294920 | tf_op jit(solution)/shard_map/ppermute | solution.py:35
  74.5 1.6 %collective-permute-start.17 = (f32[96,256]{1,0:T(8,128)S(1)}, f32[96,256]{1,0:T(8,128)S(1)}, u32[]{:S(2)}, u32[]{:S(2)}) collective-permute-start(f32[96,256]{1,0:T(8,128)S(1)} %get-tuple-element.81), channel_id=1, source_target_pairs={{0,3},{1,2},{2,1},{3,0},{4,7},{5,6},{6,5},{7,4},{8,11},{9,10},{10,... | collective-permute-start | bytes 294920 | tf_op jit(solution)/shard_map/ppermute | solution.py:35
  76.2 9.6 %collective-permute-done.18 = f16[272,1024]{1,0:T(8,128)(2,1)S(1)} collective-permute-done((f16[272,1024]{1,0:T(8,128)(2,1)S(1)}, f16[272,1024]{1,0:T(8,128)(2,1)S(1)}, u32[]{:S(2)}, u32[]{:S(2)}) %collective-permute-start.18) | collective-permute-done | bytes 557088 | tf_op jit(solution)/shard_map/ppermute | solution.py:35
  85.8 1.5 %collective-permute-done.15 = f32[96,256]{1,0:T(8,128)S(1)} collective-permute-done((f32[96,256]{1,0:T(8,128)S(1)}, f32[96,256]{1,0:T(8,128)S(1)}, u32[]{:S(2)}, u32[]{:S(2)}) %collective-permute-start.15) | collective-permute-done | bytes 98336 | tf_op jit(solution)/shard_map/ppermute | solution.py:35
  87.3 3.5 %collective-permute-done.17 = f32[96,256]{1,0:T(8,128)S(1)} collective-permute-done((f32[96,256]{1,0:T(8,128)S(1)}, f32[96,256]{1,0:T(8,128)S(1)}, u32[]{:S(2)}, u32[]{:S(2)}) %collective-permute-start.17) | collective-permute-done | bytes 98336 | tf_op jit(solution)/shard_map/ppermute | solution.py:35
  91.0 1.8 %collective-permute-start.22 = (f32[96,256]{1,0:T(8,128)S(1)}, f32[96,256]{1,0:T(8,128)S(1)}, u32[]{:S(2)}, u32[]{:S(2)}) collective-permute-start(f32[96,256]{1,0:T(8,128)S(1)} %add_add_fusion.rest_0_), channel_id=1, source_target_pairs={{0,12},{4,8},{8,4},{12,0},{1,13},{5,9},{9,5},{13,1},{2,14},{6,10},... | collective-permute-start | bytes 294920 | tf_op jit(solution)/shard_map/ppermute | solution.py:35
  93.0 8.5 %collective-permute-done.23 = f16[272,512]{1,0:T(8,128)(2,1)S(1)} collective-permute-done((f16[272,512]{1,0:T(8,128)(2,1)S(1)}, f16[272,512]{1,0:T(8,128)(2,1)S(1)}, u32[]{:S(2)}, u32[]{:S(2)}) %collective-permute-start.23) | collective-permute-done | bytes 278560 | tf_op jit(solution)/shard_map/ppermute | solution.py:35
  101.5 1.5 %final.1 = f32[1024,256]{1,0:T(8,128)} custom-call(f32[256,1024]{1,0:T(8,128)S(1)} %get-tuple-element.86.own_ref, f32[272,1024]{1,0:T(8,128)S(1)} %convert_element_type.28.near_ref, f32[272,512]{1,0:T(8,128)S(1)} %convert_element_type.29.first_ref, f32[272,512]{1,0:T(8,128)S(1)} %convert_element_type.31.second_ref), custom_call_target="tpu_custom_call" | custom-call | flops 1000 | bytes 1000 | tf_op jit(solution)/shard_map/final/pallas_call | solution.py:208
  103.0 1.3 %join.1 = (f32[128,256]{1,0:T(8,128)}, f32[256,256]{1,0:T(8,128)}, f32[2,256]{1,0:T(2,128)}) custom-call(s32[2]{0:T(128)S(1)} %pad_add_fusion.at_ref, f32[96,256]{1,0:T(8,128)S(1)} %add_add_fusion.rest_0_, f32[96,256]{1,0:T(8,128)S(1)} %collective-permute-done.20.rest_1_, f32[96,256]{1,0:T(8,128)S(1)} %collective-permute-done.21.rest_2_, ...), custom_call_target="tpu_custom_call" | custom-call | flops 1000 | bytes 1000 | tf_op jit(solution)/shard_map/join/pallas_call | solution.py:320
  (60 shorter events, 6.5 us)
Async XLA Ops:
  1.6 12.2 %collective-permute-start = (bf16[512,256]{1,0:T(8,128)(2,1)S(1)}, bf16[512,256]{1,0:T(8,128)(2,1)S(1)}, u32[]{:S(2)}, u32[]{:S(2)}) collective-permute-start(bf16[512,256]{1,0:T(8,128)(2,1)S(1)} %slice.6), channel_id=1, source_target_pairs={{0,2},{16,18}} | collective-permute-start | bytes 786440 | tf_op jit(solution)/shard_map/ppermute | solution.py:347
  7.6 9.0 %collective-permute-start.1 = (bf16[512,256]{1,0:T(8,128)(2,1)S(1)}, bf16[512,256]{1,0:T(8,128)(2,1)S(1)}, u32[]{:S(2)}, u32[]{:S(2)}) collective-permute-start(bf16[512,256]{1,0:T(8,128)(2,1)S(1)} %slice.6), channel_id=1, source_target_pairs={{0,1},{1,0},{2,3},{3,2},{4,5},{5,4},{6,7},{7,6},{8,9},{9,8},{10,11... | collective-permute-start | bytes 786440 | tf_op jit(solution)/shard_map/ppermute | solution.py:35
  7.6 12.1 %collective-permute-start.2 = (bf16[512,256]{1,0:T(8,128)(2,1)S(1)}, bf16[512,256]{1,0:T(8,128)(2,1)}, u32[]{:S(2)}, u32[]{:S(2)}) collective-permute-start(bf16[512,256]{1,0:T(8,128)(2,1)S(1)} %slice.6), channel_id=1, source_target_pairs={{0,3},{1,2},{2,1},{3,0},{4,7},{5,6},{6,5},{7,4},{8,11},{9,10},{10,... | collective-permute-start | bytes 786440 | tf_op jit(solution)/shard_map/ppermute | solution.py:35
  8.5 11.5 %copy-start.4 = (bf16[1024,256]{1,0:T(8,128)(2,1)S(1)}, bf16[1024,256]{1,0:T(8,128)(2,1)}, u32[]{:S(2)}) copy-start(bf16[1024,256]{1,0:T(8,128)(2,1)} %rest_0_.1) | copy-start | bytes 1572868
  13.4 13.8 %copy-start.6 = (f32[2,256]{1,0:T(2,128)S(1)}, f32[2,256]{1,0:T(2,128)}, u32[]{:S(2)}) copy-start(f32[2,256]{1,0:T(2,128)} %scales_ref.1) | copy-start | bytes 6148
  13.4 13.9 %copy-start.5 = (f32[256,256]{1,0:T(8,128)S(1)}, f32[256,256]{1,0:T(8,128)}, u32[]{:S(2)}) copy-start(f32[256,256]{1,0:T(8,128)} %core_ref.1) | copy-start | bytes 786436
  19.7 12.8 %collective-permute-start.6 = (bf16[2,256,4096]{2,1,0:T(8,128)(2,1)}, bf16[2,256,4096]{2,1,0:T(8,128)(2,1)}, u32[]{:S(2)}, u32[]{:S(2)}) collective-permute-start(bf16[2,256,4096]{2,1,0:T(8,128)(2,1)} %half.1), channel_id=1, source_target_pairs={{0,4},{4,0},{8,12},{12,8},{1,5},{5,1},{9,13},{13,9},{2,6},{6,2},{1... | collective-permute-start | bytes 12582920 | tf_op jit(solution)/shard_map/ppermute | solution.py:35
  21.0 8.6 %collective-permute-start.3 = (bf16[512,256]{1,0:T(8,128)(2,1)S(1)}, bf16[512,256]{1,0:T(8,128)(2,1)S(1)}, u32[]{:S(2)}, u32[]{:S(2)}) collective-permute-start(bf16[512,256]{1,0:T(8,128)(2,1)S(1)} %get-tuple-element.99), channel_id=1, source_target_pairs={{0,12},{1,13},{2,14},{3,15},{16,28},{17,29},{18,30},{19,31}} | collective-permute-start | bytes 786440 | tf_op jit(solution)/shard_map/ppermute | solution.py:353
  24.5 6.7 %collective-permute-start.4 = (bf16[512,256]{1,0:T(8,128)(2,1)S(1)}, bf16[512,256]{1,0:T(8,128)(2,1)S(1)}, u32[]{:S(2)}, u32[]{:S(2)}) collective-permute-start(bf16[512,256]{1,0:T(8,128)(2,1)S(1)} %get-tuple-element.99), channel_id=1, source_target_pairs={{0,8},{1,9},{2,10},{3,11},{16,24},{17,25},{18,26},{19,27}} | collective-permute-start | bytes 786440 | tf_op jit(solution)/shard_map/ppermute | solution.py:353
  25.8 5.9 %collective-permute-start.5 = (bf16[512,256]{1,0:T(8,128)(2,1)S(1)}, bf16[512,256]{1,0:T(8,128)(2,1)S(1)}, u32[]{:S(2)}, u32[]{:S(2)}) collective-permute-start(bf16[512,256]{1,0:T(8,128)(2,1)S(1)} %get-tuple-element.99), channel_id=1, source_target_pairs={{0,4},{1,5},{2,6},{3,7},{16,20},{17,21},{18,22},{19,23}} | collective-permute-start | bytes 786440 | tf_op jit(solution)/shard_map/ppermute | solution.py:353
  27.5 4.3 %copy-start = (f32[2,256,256]{2,1,0:T(8,128)}, f32[2,256,256]{2,1,0:T(8,128)S(1)}, u32[]{:S(2)}) copy-start(f32[2,256,256]{2,1,0:T(8,128)S(1)} %multiply_multiply_fusion.inner_ref) | copy-start | bytes 1572868
  27.5 11.1 %collective-permute-start.7 = (bf16[512,256]{1,0:T(8,128)(2,1)S(1)}, bf16[512,256]{1,0:T(8,128)(2,1)S(1)}, u32[]{:S(2)}, u32[]{:S(2)}) collective-permute-start(bf16[512,256]{1,0:T(8,128)(2,1)S(1)} %get-tuple-element.98), channel_id=1, source_target_pairs={{0,3},{1,2},{2,1},{3,0},{4,7},{5,6},{6,5},{7,4},{8,11},{9,10},{10,... | collective-permute-start | bytes 786440 | tf_op jit(solution)/shard_map/ppermute | solution.py:35
  29.6 15.9 %collective-permute-start.8 = (bf16[512,256]{1,0:T(8,128)(2,1)S(1)}, bf16[512,256]{1,0:T(8,128)(2,1)S(1)}, u32[]{:S(2)}, u32[]{:S(2)}) collective-permute-start(bf16[512,256]{1,0:T(8,128)(2,1)S(1)} %get-tuple-element.98), channel_id=1, source_target_pairs={{0,1},{1,0},{2,3},{3,2},{4,5},{5,4},{6,7},{7,6},{8,9},{9,8},{10,11... | collective-permute-start | bytes 786440 | tf_op jit(solution)/shard_map/ppermute | solution.py:35
  31.2 20.7 %collective-permute-start.9 = (bf16[512,256]{1,0:T(8,128)(2,1)}, bf16[512,256]{1,0:T(8,128)(2,1)}, u32[]{:S(2)}, u32[]{:S(2)}) collective-permute-start(bf16[512,256]{1,0:T(8,128)(2,1)} %collective-permute-done.2.rest_0_), channel_id=1, source_target_pairs={{0,1},{1,0},{2,3},{3,2},{4,5},{5,4},{6,7},{7,6},{8,9},{9,8},{10,11... | collective-permute-start | bytes 786440 | tf_op jit(solution)/shard_map/ppermute | solution.py:35
  31.8 0.8 copy-start.2
  38.6 14.6 %collective-permute-start.10 = (bf16[512,256]{1,0:T(8,128)(2,1)S(1)}, bf16[512,256]{1,0:T(8,128)(2,1)S(1)}, u32[]{:S(2)}, u32[]{:S(2)}) collective-permute-start(bf16[512,256]{1,0:T(8,128)(2,1)S(1)} %collective-permute-done.7.rest_1_), channel_id=1, source_target_pairs={{0,1},{1,0},{2,3},{3,2},{4,5},{5,4},{6,7},{7,6},{8,9},{9,8},{10,11... | collective-permute-start | bytes 786440 | tf_op jit(solution)/shard_map/ppermute | solution.py:35
  45.4 19.8 %collective-permute-start.11 = (f16[272,1024]{1,0:T(8,128)(2,1)S(1)}, f16[272,1024]{1,0:T(8,128)(2,1)S(1)}, u32[]{:S(2)}, u32[]{:S(2)}) collective-permute-start(f16[272,1024]{1,0:T(8,128)(2,1)S(1)} %convert_element_type.24), channel_id=1, source_target_pairs={{0,1},{1,0},{2,3},{3,2},{4,5},{5,4},{6,7},{7,6},{8,9},{9,8},{10,11... | collective-permute-start | bytes 1671176 | tf_op jit(solution)/shard_map/ppermute | solution.py:35
  49.7 36.1 %collective-permute-start.18 = (f16[272,1024]{1,0:T(8,128)(2,1)S(1)}, f16[272,1024]{1,0:T(8,128)(2,1)S(1)}, u32[]{:S(2)}, u32[]{:S(2)}) collective-permute-start(f16[272,1024]{1,0:T(8,128)(2,1)S(1)} %convert_element_type.25), channel_id=1, source_target_pairs={{0,1},{1,0},{2,3},{3,2},{4,5},{5,4},{6,7},{7,6},{8,9},{9,8},{10,11... | collective-permute-start | bytes 1671176 | tf_op jit(solution)/shard_map/ppermute | solution.py:35
  53.2 4.2 %copy-start.1 = (f32[2,256,256]{2,1,0:T(8,128)S(1)}, f32[2,256,256]{2,1,0:T(8,128)}, u32[]{:S(2)}) copy-start(f32[2,256,256]{2,1,0:T(8,128)} %copy-done) | copy-start | bytes 1572868
  53.2 4.2 %copy-start.3 = (bf16[512,256]{1,0:T(8,128)(2,1)S(1)}, bf16[512,256]{1,0:T(8,128)(2,1)}, u32[]{:S(2)}) copy-start(bf16[512,256]{1,0:T(8,128)(2,1)} %copy-done.2) | copy-start | bytes 786436
  59.6 1.9 %collective-permute-start.12 = (f32[200,256]{1,0:T(8,128)S(1)}, f32[200,256]{1,0:T(8,128)S(1)}, u32[]{:S(2)}, u32[]{:S(2)}) collective-permute-start(f32[200,256]{1,0:T(8,128)S(1)} %get-tuple-element.68), channel_id=1, source_target_pairs={{0,4},{4,0},{8,12},{12,8},{1,5},{5,1},{9,13},{13,9},{2,6},{6,2},{1... | collective-permute-start | bytes 614408 | tf_op jit(solution)/shard_map/ppermute | solution.py:35
  59.7 9.0 %collective-permute-start.13 = (f32[200,256]{1,0:T(8,128)S(1)}, f32[200,256]{1,0:T(8,128)S(1)}, u32[]{:S(2)}, u32[]{:S(2)}) collective-permute-start(f32[200,256]{1,0:T(8,128)S(1)} %get-tuple-element.70), channel_id=1, source_target_pairs={{0,8},{4,12},{8,0},{12,4},{1,9},{5,13},{9,1},{13,5},{2,10},{6,14},... | collective-permute-start | bytes 614408 | tf_op jit(solution)/shard_map/ppermute | solution.py:35
  59.7 11.3 %collective-permute-start.14 = (f32[200,256]{1,0:T(8,128)S(1)}, f32[200,256]{1,0:T(8,128)S(1)}, u32[]{:S(2)}, u32[]{:S(2)}) collective-permute-start(f32[200,256]{1,0:T(8,128)S(1)} %get-tuple-element.71), channel_id=1, source_target_pairs={{0,12},{4,8},{8,4},{12,0},{1,13},{5,9},{9,5},{13,1},{2,14},{6,10},... | collective-permute-start | bytes 614408 | tf_op jit(solution)/shard_map/ppermute | solution.py:35
  65.8 25.1 %collective-permute-start.19 = (f16[272,512]{1,0:T(8,128)(2,1)S(1)}, f16[272,512]{1,0:T(8,128)(2,1)S(1)}, u32[]{:S(2)}, u32[]{:S(2)}) collective-permute-start(f16[272,512]{1,0:T(8,128)(2,1)S(1)} %convert_element_type.27), channel_id=1, source_target_pairs={{0,2},{1,3},{2,0},{3,1},{4,6},{5,7},{6,4},{7,5},{8,10},{9,11},{10,... | collective-permute-start | bytes 835592 | tf_op jit(solution)/shard_map/ppermute | solution.py:35
  71.1 16.2 %collective-permute-start.15 = (f32[96,256]{1,0:T(8,128)S(1)}, f32[96,256]{1,0:T(8,128)S(1)}, u32[]{:S(2)}, u32[]{:S(2)}) collective-permute-start(f32[96,256]{1,0:T(8,128)S(1)} %get-tuple-element.79), channel_id=1, source_target_pairs={{0,1},{1,0},{2,3},{3,2},{4,5},{5,4},{6,7},{7,6},{8,9},{9,8},{10,11... | collective-permute-start | bytes 294920 | tf_op jit(solution)/shard_map/ppermute | solution.py:35
  73.7 13.6 %collective-permute-start.16 = (f32[96,256]{1,0:T(8,128)S(1)}, f32[96,256]{1,0:T(8,128)S(1)}, u32[]{:S(2)}, u32[]{:S(2)}) collective-permute-start(f32[96,256]{1,0:T(8,128)S(1)} %get-tuple-element.80), channel_id=1, source_target_pairs={{0,2},{1,3},{2,0},{3,1},{4,6},{5,7},{6,4},{7,5},{8,10},{9,11},{10,... | collective-permute-start | bytes 294920 | tf_op jit(solution)/shard_map/ppermute | solution.py:35
  74.5 16.4 %collective-permute-start.17 = (f32[96,256]{1,0:T(8,128)S(1)}, f32[96,256]{1,0:T(8,128)S(1)}, u32[]{:S(2)}, u32[]{:S(2)}) collective-permute-start(f32[96,256]{1,0:T(8,128)S(1)} %get-tuple-element.81), channel_id=1, source_target_pairs={{0,3},{1,2},{2,1},{3,0},{4,7},{5,6},{6,5},{7,4},{8,11},{9,10},{10,... | collective-permute-start | bytes 294920 | tf_op jit(solution)/shard_map/ppermute | solution.py:35
  85.8 15.6 %collective-permute-start.23 = (f16[272,512]{1,0:T(8,128)(2,1)S(1)}, f16[272,512]{1,0:T(8,128)(2,1)S(1)}, u32[]{:S(2)}, u32[]{:S(2)}) collective-permute-start(f16[272,512]{1,0:T(8,128)(2,1)S(1)} %convert_element_type.30), channel_id=1, source_target_pairs={{0,2},{1,3},{2,0},{3,1},{4,6},{5,7},{6,4},{7,5},{8,10},{9,11},{10,... | collective-permute-start | bytes 835592 | tf_op jit(solution)/shard_map/ppermute | solution.py:35
  90.9 12.1 %collective-permute-start.20 = (f32[96,256]{1,0:T(8,128)S(1)}, f32[96,256]{1,0:T(8,128)S(1)}, u32[]{:S(2)}, u32[]{:S(2)}) collective-permute-start(f32[96,256]{1,0:T(8,128)S(1)} %add_add_fusion.rest_0_), channel_id=1, source_target_pairs={{0,4},{4,0},{8,12},{12,8},{1,5},{5,1},{9,13},{13,9},{2,6},{6,2},{1... | collective-permute-start | bytes 294920 | tf_op jit(solution)/shard_map/ppermute | solution.py:35
  91.0 12.0 %collective-permute-start.21 = (f32[96,256]{1,0:T(8,128)S(1)}, f32[96,256]{1,0:T(8,128)S(1)}, u32[]{:S(2)}, u32[]{:S(2)}) collective-permute-start(f32[96,256]{1,0:T(8,128)S(1)} %add_add_fusion.rest_0_), channel_id=1, source_target_pairs={{0,8},{4,12},{8,0},{12,4},{1,9},{5,13},{9,1},{13,5},{2,10},{6,14},... | collective-permute-start | bytes 294920 | tf_op jit(solution)/shard_map/ppermute | solution.py:35
  91.0 12.0 %collective-permute-start.22 = (f32[96,256]{1,0:T(8,128)S(1)}, f32[96,256]{1,0:T(8,128)S(1)}, u32[]{:S(2)}, u32[]{:S(2)}) collective-permute-start(f32[96,256]{1,0:T(8,128)S(1)} %add_add_fusion.rest_0_), channel_id=1, source_target_pairs={{0,12},{4,8},{8,4},{12,0},{1,13},{5,9},{9,5},{13,1},{2,14},{6,10},... | collective-permute-start | bytes 294920 | tf_op jit(solution)/shard_map/ppermute | solution.py:35

commit v6 on v5

--- a/solution.py
+++ b/solution.py
@@ -369,10 +369,10 @@
     grad_near, proj = piece_of(cut ^ 1, near, "coded", LARGE, "piece_near", [proj], grad_far)
     grad_near = grad_near.astype(F16)
     from_near = swapped(grad_near, "cuts", 1)
-    grad_middle, proj = piece_of(cut ^ 2, middle, "plain", SMALL, "piece_middle", [proj], grad_near)
+    grad_middle, proj = piece_of(cut ^ 2, middle, "plain", LARGE, "piece_middle", [proj], grad_near)
 
     own, *send = terms_call(cuts, place, window, inner, core, scales, [proj])
-    received = [swapped(value, "tile", mask + 1) for mask, value in enumerate(send)]
+    received = [swapped(send[mask - 1], "tile", mask) for mask in (3, 2, 1)][::-1]
     joined, received[0] = hold((joined, received[0]))
     passed = list(relay_call(joined.astype(F32), grad_middle))
     from_middle = swapped(passed[0].astype(F16), "cuts", 2)
@@ -382,7 +382,7 @@
     send = [swapped(value, "cuts", mask + 1) for mask, value in enumerate(send)]
     send, from_near, from_middle = hold((send, from_near, from_middle))
     total = own + sum(send)
-    quarters = [swapped(total, "tile", mask) for mask in (1, 2, 3)]
+    quarters = [swapped(total, "tile", mask) for mask in (3, 2, 1)][::-1]
     halves = [from_middle.astype(F32), from_middle_second.astype(F32)]
     grad_factor = final_call(coef, grad_own, from_near.astype(F32), halves)
     quarters, grad_factor = hold((quarters, grad_factor))

time: 105 us -> 105 us (level)
  other arithmetic: 2.15 us -> 3.98 us
  waiting for transfers between devices: 40.4 us -> 38.7 us
    ppermute x20, waiting for transfers between devices: 38.4 us -> 36.7 us  [swapped(): return lax.ppermute(value, axis, pairs)]
  transfers between devices with their start and end apart: 24 -> 24, of which waited for: 12 -> 12; matrix products, arithmetic and copies ran while one was open for 2% -> 4% of each run, Pallas kernels for 25% -> 25%
where the time goes in v6:
time: 105 us; the launch traced here: 104 us
  waiting for transfers between devices  38.7 us (37%)
  starting transfers between devices  31.8 us (30%)
  Pallas kernels  27.9 us (27%)
  other arithmetic  3.98 us (4%)
  local copies, waits for them, and re-layouts  1.13 us (1%)
    ppermute x20, waiting for transfers between devices, swapped(): return lax.ppermute(value, axis, pairs)  36.7 us
    ppermute x20, starting transfers between devices, swapped(): return lax.ppermute(value, axis, pairs)  19.7 us
    pallas_call x4, Pallas kernels, piece_call(): pl.pallas_call(functools.partial(piece_kernel, kind, len(before) > 0, len...  16.7 us
    ppermute x3, starting transfers between devices, body_line(): out = [lax.ppermute(line, 'tile', [(0, target)]) for target in (3, 2, 1)]  6.11 us
    ppermute x1, starting transfers between devices, body_line(): second = lax.ppermute(parts[0], ('tile', 'cuts'), [(0, 2)])  5.96 us
    pallas_call x1, Pallas kernels, half_call(): pl.pallas_call(half_kernel, grid_spec=pltpu.PrefetchScalarGridSpec(num_sc...  4.95 us
    pallas_call x1, Pallas kernels, terms_call(): pl.pallas_call(functools.partial(terms_kernel, cuts), in_specs=[pl.BlockS...  2.22 us
  transfers between devices with their start and end apart: 24, of which 12 were waited for; matrix products, arithmetic and copies ran while one was open for 4% of the time, Pallas kernels for 25%

profile of v6, /device:TPU:0, one launch (start us, length us, event | category | flops | bytes accessed | tf_op | source)
XLA Modules:
  0.0 104.4 jit_solution(12771447327986218192)
XLA Ops:
  1.6 6.0 %collective-permute-start = (bf16[512,256]{1,0:T(8,128)(2,1)S(1)}, bf16[512,256]{1,0:T(8,128)(2,1)S(1)}, u32[]{:S(2)}, u32[]{:S(2)}) collective-permute-start(bf16[512,256]{1,0:T(8,128)(2,1)S(1)} %slice.6), channel_id=1, source_target_pairs={{0,2},{16,18}} | collective-permute-start | bytes 786440 | tf_op jit(solution)/shard_map/ppermute | solution.py:347
  8.5 5.0 %half.1 = bf16[2,256,4096]{2,1,0:T(8,128)(2,1)} custom-call(s32[1]{0:T(128)} %bitcast.2.at_ref, bf16[2,1,256,8192]{3,2,1,0:T(8,128)(2,1)} %own_ref.7), custom_call_target="tpu_custom_call" | custom-call | flops 99999997952 | bytes 100000000 | tf_op jit(solution)/shard_map/half/pallas_call | solution.py:79
  13.8 2.8 %collective-permute-done.1.rest_0_ = bf16[512,256]{1,0:T(8,128)(2,1)S(1)} collective-permute-done((bf16[512,256]{1,0:T(8,128)(2,1)S(1)}, bf16[512,256]{1,0:T(8,128)(2,1)S(1)}, u32[]{:S(2)}, u32[]{:S(2)}) %collective-permute-start.1) | collective-permute-done | bytes 262176 | tf_op jit(solution)/shard_map/ppermute | solution.py:35
  16.6 3.1 %collective-permute-done.2.rest_0_ = bf16[512,256]{1,0:T(8,128)(2,1)} collective-permute-done((bf16[512,256]{1,0:T(8,128)(2,1)S(1)}, bf16[512,256]{1,0:T(8,128)(2,1)}, u32[]{:S(2)}, u32[]{:S(2)}) %collective-permute-start.2) | collective-permute-done | bytes 262176 | tf_op jit(solution)/shard_map/ppermute | solution.py:35
  20.0 1.0 fusion
  21.1 3.5 %collective-permute-start.3 = (bf16[512,256]{1,0:T(8,128)(2,1)S(1)}, bf16[512,256]{1,0:T(8,128)(2,1)S(1)}, u32[]{:S(2)}, u32[]{:S(2)}) collective-permute-start(bf16[512,256]{1,0:T(8,128)(2,1)S(1)} %get-tuple-element.99), channel_id=1, source_target_pairs={{0,12},{1,13},{2,14},{3,15},{16,28},{17,29},{18,30},{19,31}} | collective-permute-start | bytes 786440 | tf_op jit(solution)/shard_map/ppermute | solution.py:353
  24.6 1.3 %collective-permute-start.4 = (bf16[512,256]{1,0:T(8,128)(2,1)S(1)}, bf16[512,256]{1,0:T(8,128)(2,1)S(1)}, u32[]{:S(2)}, u32[]{:S(2)}) collective-permute-start(bf16[512,256]{1,0:T(8,128)(2,1)S(1)} %get-tuple-element.99), channel_id=1, source_target_pairs={{0,8},{1,9},{2,10},{3,11},{16,24},{17,25},{18,26},{19,27}} | collective-permute-start | bytes 786440 | tf_op jit(solution)/shard_map/ppermute | solution.py:353
  25.9 1.3 %collective-permute-start.5 = (bf16[512,256]{1,0:T(8,128)(2,1)S(1)}, bf16[512,256]{1,0:T(8,128)(2,1)S(1)}, u32[]{:S(2)}, u32[]{:S(2)}) collective-permute-start(bf16[512,256]{1,0:T(8,128)(2,1)S(1)} %get-tuple-element.99), channel_id=1, source_target_pairs={{0,4},{1,5},{2,6},{3,7},{16,20},{17,21},{18,22},{19,23}} | collective-permute-start | bytes 786440 | tf_op jit(solution)/shard_map/ppermute | solution.py:353
  27.6 2.0 %collective-permute-start.7 = (bf16[512,256]{1,0:T(8,128)(2,1)S(1)}, bf16[512,256]{1,0:T(8,128)(2,1)S(1)}, u32[]{:S(2)}, u32[]{:S(2)}) collective-permute-start(bf16[512,256]{1,0:T(8,128)(2,1)S(1)} %get-tuple-element.98), channel_id=1, source_target_pairs={{0,3},{1,2},{2,1},{3,0},{4,7},{5,6},{6,5},{7,4},{8,11},{9,10},{10,... | collective-permute-start | bytes 786440 | tf_op jit(solution)/shard_map/ppermute | solution.py:35
  29.6 1.6 %collective-permute-done.4 = bf16[512,256]{1,0:T(8,128)(2,1)S(1)} collective-permute-done((bf16[512,256]{1,0:T(8,128)(2,1)S(1)}, bf16[512,256]{1,0:T(8,128)(2,1)S(1)}, u32[]{:S(2)}, u32[]{:S(2)}) %collective-permute-start.4) | collective-permute-done | bytes 262176 | tf_op jit(solution)/shard_map/ppermute | solution.py:353
  32.6 4.0 %piece_own.1 = (f32[256,1024]{1,0:T(8,128)S(1)}, f32[2,512,256]{2,1,0:T(8,128)S(1)}) custom-call(s32[2]{0:T(128)S(1)} %pad_add_fusion.4.at_ref, bf16[2,1,256,8192]{3,2,1,0:T(8,128)(2,1)} %own_ref.7, bf16[2,256,4096]{2,1,0:T(8,128)(2,1)} %collective-permute-done.6.other_ref, bf16[1024,256]{1,0:T(8,128)(2,1)S(1)} %copy-done.4, ...), custom_call_target="tpu_custom_call" | custom-call | flops 99999997952 | bytes 100000000 | tf_op jit(solution)/shard_map/piece_own/pallas_call | solution.py:158
  36.7 2.0 %collective-permute-done.7.rest_1_ = bf16[512,256]{1,0:T(8,128)(2,1)S(1)} collective-permute-done((bf16[512,256]{1,0:T(8,128)(2,1)S(1)}, bf16[512,256]{1,0:T(8,128)(2,1)S(1)}, u32[]{:S(2)}, u32[]{:S(2)}) %collective-permute-start.7) | collective-permute-done | bytes 262176 | tf_op jit(solution)/shard_map/ppermute | solution.py:35
  38.7 2.3 %collective-permute-start.10 = (bf16[512,256]{1,0:T(8,128)(2,1)S(1)}, bf16[512,256]{1,0:T(8,128)(2,1)S(1)}, u32[]{:S(2)}, u32[]{:S(2)}) collective-permute-start(bf16[512,256]{1,0:T(8,128)(2,1)S(1)} %collective-permute-done.7.rest_1_), channel_id=1, source_target_pairs={{0,1},{1,0},{2,3},{3,2},{4,5},{5,4},{6,7},{7,6},{8,9},{9,8},{10,11... | collective-permute-start | bytes 786440 | tf_op jit(solution)/shard_map/ppermute | solution.py:35
  41.0 4.3 %piece_far.1 = (f32[272,1024]{1,0:T(8,128)S(1)}, f32[2,512,256]{2,1,0:T(8,128)S(1)}) custom-call(s32[2]{0:T(128)S(1)} %pad_add_fusion.3.at_ref, bf16[2,1,256,8192]{3,2,1,0:T(8,128)(2,1)} %own_ref.7, bf16[2,256,4096]{2,1,0:T(8,128)(2,1)} %collective-permute-done.6.other_ref, bf16[512,256]{1,0:T(8,128)(2,1)} %collective-permute-done.2.rest_0_, ...), custom_call_target="tpu_custom_call" | custom-call | flops 1000 | bytes 1000 | tf_op jit(solution)/shard_map/piece_far/pallas_call | solution.py:158
  46.2 4.2 %piece_near.1 = (f32[272,1024]{1,0:T(8,128)S(1)}, f32[2,512,256]{2,1,0:T(8,128)S(1)}) custom-call(s32[2]{0:T(128)S(1)} %pad_add_fusion.2.at_ref, bf16[2,1,256,8192]{3,2,1,0:T(8,128)(2,1)} %own_ref.7, bf16[2,256,4096]{2,1,0:T(8,128)(2,1)} %collective-permute-done.6.other_ref, bf16[512,256]{1,0:T(8,128)(2,1)S(1)} %collective-permute-done.1.rest_0_, ...), custom_call_target="tpu_custom_call" | custom-call | flops 99999997952 | bytes 100000000 | tf_op jit(solution)/shard_map/piece_near/pallas_call | solution.py:158
  50.5 2.1 %collective-permute-start.18 = (f16[272,1024]{1,0:T(8,128)(2,1)S(1)}, f16[272,1024]{1,0:T(8,128)(2,1)S(1)}, u32[]{:S(2)}, u32[]{:S(2)}) collective-permute-start(f16[272,1024]{1,0:T(8,128)(2,1)S(1)} %convert_element_type.25), channel_id=1, source_target_pairs={{0,1},{1,0},{2,3},{3,2},{4,5},{5,4},{6,7},{7,6},{8,9},{9,8},{10,11... | collective-permute-start | bytes 1671176 | tf_op jit(solution)/shard_map/ppermute | solution.py:35
  53.2 4.2 %piece_middle.1 = (f32[256,1024]{1,0:T(8,128)S(1)}, f32[2,512,256]{2,1,0:T(8,128)S(1)}) custom-call(s32[2]{0:T(128)S(1)} %pad_add_fusion.1.at_ref, bf16[2,1,256,8192]{3,2,1,0:T(8,128)(2,1)} %own_ref.7, bf16[2,256,4096]{2,1,0:T(8,128)(2,1)} %collective-permute-done.6.other_ref, bf16[512,256]{1,0:T(8,128)(2,1)} %collective-permute-done.9.rest_0_, ...), custom_call_target="tpu_custom_call" | custom-call | flops 99999997952 | bytes 100000000 | tf_op jit(solution)/shard_map/piece_middle/pallas_call | solution.py:158
  57.4 2.2 %terms.1 = (f32[200,256]{1,0:T(8,128)S(1)}, f32[200,256]{1,0:T(8,128)S(1)}, f32[200,256]{1,0:T(8,128)S(1)}, f32[200,256]{1,0:T(8,128)S(1)}) custom-call(s32[2]{0:T(128)S(1)} %pad_add_fusion.at_ref, bf16[512,256]{1,0:T(8,128)(2,1)S(1)} %copy-done.3, f32[2,256,256]{2,1,0:T(8,128)S(1)} %copy-done.1, f32[256,256]{1,0:T(8,128)S(1)} %copy-done.5, ...), custom_call_target="tpu_custom_call" | custom-call | flops 1000 | bytes 1000 | tf_op jit(solution)/shard_map/terms/pallas_call | solution.py:267
  59.9 1.7 %collective-permute-start.14 = (f32[200,256]{1,0:T(8,128)S(1)}, f32[200,256]{1,0:T(8,128)S(1)}, u32[]{:S(2)}, u32[]{:S(2)}) collective-permute-start(f32[200,256]{1,0:T(8,128)S(1)} %get-tuple-element.71), channel_id=1, source_target_pairs={{0,12},{4,8},{8,4},{12,0},{1,13},{5,9},{9,5},{13,1},{2,14},{6,10},... | collective-permute-start | bytes 614408 | tf_op jit(solution)/shard_map/ppermute | solution.py:35
  61.6 3.7 %collective-permute-done.11 = f16[272,1024]{1,0:T(8,128)(2,1)} collective-permute-done((f16[272,1024]{1,0:T(8,128)(2,1)}, f16[272,1024]{1,0:T(8,128)(2,1)}, u32[]{:S(2)}, u32[]{:S(2)}) %collective-permute-start.11) | collective-permute-done | bytes 557088 | tf_op jit(solution)/shard_map/ppermute | solution.py:35
  65.3 1.1 %convert_element_type.26.received_ref = f32[272,1024]{1,0:T(8,128)S(1)} convert(f16[272,1024]{1,0:T(8,128)(2,1)} %collective-permute-done.11) | non-fusion elementwise | flops 278528 | bytes 1671168 | tf_op jit(solution)/shard_map/convert_element_type | solution.py:377
  67.0 2.9 %collective-permute-start.19 = (f16[272,512]{1,0:T(8,128)(2,1)S(1)}, f16[272,512]{1,0:T(8,128)(2,1)S(1)}, u32[]{:S(2)}, u32[]{:S(2)}) collective-permute-start(f16[272,512]{1,0:T(8,128)(2,1)S(1)} %convert_element_type.27), channel_id=1, source_target_pairs={{0,2},{1,3},{2,0},{3,1},{4,6},{5,7},{6,4},{7,5},{8,10},{9,11},{10,... | collective-permute-start | bytes 835592 | tf_op jit(solution)/shard_map/ppermute | solution.py:35
  69.9 1.3 %collective-permute-done.14.rest_2_ = f32[200,256]{1,0:T(8,128)S(1)} collective-permute-done((f32[200,256]{1,0:T(8,128)S(1)}, f32[200,256]{1,0:T(8,128)S(1)}, u32[]{:S(2)}, u32[]{:S(2)}) %collective-permute-start.14) | collective-permute-done | bytes 204832 | tf_op jit(solution)/shard_map/ppermute | solution.py:35
  71.2 2.6 %collective-permute-start.15 = (f32[96,256]{1,0:T(8,128)S(1)}, f32[96,256]{1,0:T(8,128)S(1)}, u32[]{:S(2)}, u32[]{:S(2)}) collective-permute-start(f32[96,256]{1,0:T(8,128)S(1)} %get-tuple-element.79), channel_id=1, source_target_pairs={{0,1},{1,0},{2,3},{3,2},{4,5},{5,4},{6,7},{7,6},{8,9},{9,8},{10,11... | collective-permute-start | bytes 294920 | tf_op jit(solution)/shard_map/ppermute | solution.py:35
  74.6 1.7 %collective-permute-start.17 = (f32[96,256]{1,0:T(8,128)S(1)}, f32[96,256]{1,0:T(8,128)S(1)}, u32[]{:S(2)}, u32[]{:S(2)}) collective-permute-start(f32[96,256]{1,0:T(8,128)S(1)} %get-tuple-element.81), channel_id=1, source_target_pairs={{0,3},{1,2},{2,1},{3,0},{4,7},{5,6},{6,5},{7,4},{8,11},{9,10},{10,... | collective-permute-start | bytes 294920 | tf_op jit(solution)/shard_map/ppermute | solution.py:35
  76.3 9.6 %collective-permute-done.18 = f16[272,1024]{1,0:T(8,128)(2,1)S(1)} collective-permute-done((f16[272,1024]{1,0:T(8,128)(2,1)S(1)}, f16[272,1024]{1,0:T(8,128)(2,1)S(1)}, u32[]{:S(2)}, u32[]{:S(2)}) %collective-permute-start.18) | collective-permute-done | bytes 557088 | tf_op jit(solution)/shard_map/ppermute | solution.py:35
  85.9 1.5 %collective-permute-done.15 = f32[96,256]{1,0:T(8,128)S(1)} collective-permute-done((f32[96,256]{1,0:T(8,128)S(1)}, f32[96,256]{1,0:T(8,128)S(1)}, u32[]{:S(2)}, u32[]{:S(2)}) %collective-permute-start.15) | collective-permute-done | bytes 98336 | tf_op jit(solution)/shard_map/ppermute | solution.py:35
  87.4 3.5 %collective-permute-done.17 = f32[96,256]{1,0:T(8,128)S(1)} collective-permute-done((f32[96,256]{1,0:T(8,128)S(1)}, f32[96,256]{1,0:T(8,128)S(1)}, u32[]{:S(2)}, u32[]{:S(2)}) %collective-permute-start.17) | collective-permute-done | bytes 98336 | tf_op jit(solution)/shard_map/ppermute | solution.py:35
  91.1 1.8 %collective-permute-start.22 = (f32[96,256]{1,0:T(8,128)S(1)}, f32[96,256]{1,0:T(8,128)S(1)}, u32[]{:S(2)}, u32[]{:S(2)}) collective-permute-start(f32[96,256]{1,0:T(8,128)S(1)} %add_add_fusion.rest_0_), channel_id=1, source_target_pairs={{0,12},{4,8},{8,4},{12,0},{1,13},{5,9},{9,5},{13,1},{2,14},{6,10},... | collective-permute-start | bytes 294920 | tf_op jit(solution)/shard_map/ppermute | solution.py:35
  93.1 8.5 %collective-permute-done.23 = f16[272,512]{1,0:T(8,128)(2,1)S(1)} collective-permute-done((f16[272,512]{1,0:T(8,128)(2,1)S(1)}, f16[272,512]{1,0:T(8,128)(2,1)S(1)}, u32[]{:S(2)}, u32[]{:S(2)}) %collective-permute-start.23) | collective-permute-done | bytes 278560 | tf_op jit(solution)/shard_map/ppermute | solution.py:35
  101.6 1.5 %final.1 = f32[1024,256]{1,0:T(8,128)} custom-call(f32[256,1024]{1,0:T(8,128)S(1)} %get-tuple-element.86.own_ref, f32[272,1024]{1,0:T(8,128)S(1)} %convert_element_type.28.near_ref, f32[272,512]{1,0:T(8,128)S(1)} %convert_element_type.29.first_ref, f32[272,512]{1,0:T(8,128)S(1)} %convert_element_type.31.second_ref), custom_call_target="tpu_custom_call" | custom-call | flops 1000 | bytes 1000 | tf_op jit(solution)/shard_map/final/pallas_call | solution.py:208
  103.1 1.3 %join.1 = (f32[128,256]{1,0:T(8,128)}, f32[256,256]{1,0:T(8,128)}, f32[2,256]{1,0:T(2,128)}) custom-call(s32[2]{0:T(128)S(1)} %pad_add_fusion.at_ref, f32[96,256]{1,0:T(8,128)S(1)} %add_add_fusion.rest_0_, f32[96,256]{1,0:T(8,128)S(1)} %collective-permute-done.20.rest_1_, f32[96,256]{1,0:T(8,128)S(1)} %collective-permute-done.21.rest_2_, ...), custom_call_target="tpu_custom_call" | custom-call | flops 1000 | bytes 1000 | tf_op jit(solution)/shard_map/join/pallas_call | solution.py:320
  (60 shorter events, 7.9 us)
Async XLA Ops:
  1.6 12.2 %collective-permute-start = (bf16[512,256]{1,0:T(8,128)(2,1)S(1)}, bf16[512,256]{1,0:T(8,128)(2,1)S(1)}, u32[]{:S(2)}, u32[]{:S(2)}) collective-permute-start(bf16[512,256]{1,0:T(8,128)(2,1)S(1)} %slice.6), channel_id=1, source_target_pairs={{0,2},{16,18}} | collective-permute-start | bytes 786440 | tf_op jit(solution)/shard_map/ppermute | solution.py:347
  7.6 9.0 %collective-permute-start.1 = (bf16[512,256]{1,0:T(8,128)(2,1)S(1)}, bf16[512,256]{1,0:T(8,128)(2,1)S(1)}, u32[]{:S(2)}, u32[]{:S(2)}) collective-permute-start(bf16[512,256]{1,0:T(8,128)(2,1)S(1)} %slice.6), channel_id=1, source_target_pairs={{0,1},{1,0},{2,3},{3,2},{4,5},{5,4},{6,7},{7,6},{8,9},{9,8},{10,11... | collective-permute-start | bytes 786440 | tf_op jit(solution)/shard_map/ppermute | solution.py:35
  7.6 12.1 %collective-permute-start.2 = (bf16[512,256]{1,0:T(8,128)(2,1)S(1)}, bf16[512,256]{1,0:T(8,128)(2,1)}, u32[]{:S(2)}, u32[]{:S(2)}) collective-permute-start(bf16[512,256]{1,0:T(8,128)(2,1)S(1)} %slice.6), channel_id=1, source_target_pairs={{0,3},{1,2},{2,1},{3,0},{4,7},{5,6},{6,5},{7,4},{8,11},{9,10},{10,... | collective-permute-start | bytes 786440 | tf_op jit(solution)/shard_map/ppermute | solution.py:35
  8.5 11.6 %copy-start.4 = (bf16[1024,256]{1,0:T(8,128)(2,1)S(1)}, bf16[1024,256]{1,0:T(8,128)(2,1)}, u32[]{:S(2)}) copy-start(bf16[1024,256]{1,0:T(8,128)(2,1)} %rest_0_.1) | copy-start | bytes 1572868
  13.4 13.8 %copy-start.6 = (f32[2,256]{1,0:T(2,128)S(1)}, f32[2,256]{1,0:T(2,128)}, u32[]{:S(2)}) copy-start(f32[2,256]{1,0:T(2,128)} %scales_ref.1) | copy-start | bytes 6148
  13.4 14.0 %copy-start.5 = (f32[256,256]{1,0:T(8,128)S(1)}, f32[256,256]{1,0:T(8,128)}, u32[]{:S(2)}) copy-start(f32[256,256]{1,0:T(8,128)} %core_ref.1) | copy-start | bytes 786436
  19.7 12.9 %collective-permute-start.6 = (bf16[2,256,4096]{2,1,0:T(8,128)(2,1)}, bf16[2,256,4096]{2,1,0:T(8,128)(2,1)}, u32[]{:S(2)}, u32[]{:S(2)}) collective-permute-start(bf16[2,256,4096]{2,1,0:T(8,128)(2,1)} %half.1), channel_id=1, source_target_pairs={{0,4},{4,0},{8,12},{12,8},{1,5},{5,1},{9,13},{13,9},{2,6},{6,2},{1... | collective-permute-start | bytes 12582920 | tf_op jit(solution)/shard_map/ppermute | solution.py:35
  21.1 8.6 %collective-permute-start.3 = (bf16[512,256]{1,0:T(8,128)(2,1)S(1)}, bf16[512,256]{1,0:T(8,128)(2,1)S(1)}, u32[]{:S(2)}, u32[]{:S(2)}) collective-permute-start(bf16[512,256]{1,0:T(8,128)(2,1)S(1)} %get-tuple-element.99), channel_id=1, source_target_pairs={{0,12},{1,13},{2,14},{3,15},{16,28},{17,29},{18,30},{19,31}} | collective-permute-start | bytes 786440 | tf_op jit(solution)/shard_map/ppermute | solution.py:353
  24.6 6.7 %collective-permute-start.4 = (bf16[512,256]{1,0:T(8,128)(2,1)S(1)}, bf16[512,256]{1,0:T(8,128)(2,1)S(1)}, u32[]{:S(2)}, u32[]{:S(2)}) collective-permute-start(bf16[512,256]{1,0:T(8,128)(2,1)S(1)} %get-tuple-element.99), channel_id=1, source_target_pairs={{0,8},{1,9},{2,10},{3,11},{16,24},{17,25},{18,26},{19,27}} | collective-permute-start | bytes 786440 | tf_op jit(solution)/shard_map/ppermute | solution.py:353
  25.9 5.9 %collective-permute-start.5 = (bf16[512,256]{1,0:T(8,128)(2,1)S(1)}, bf16[512,256]{1,0:T(8,128)(2,1)S(1)}, u32[]{:S(2)}, u32[]{:S(2)}) collective-permute-start(bf16[512,256]{1,0:T(8,128)(2,1)S(1)} %get-tuple-element.99), channel_id=1, source_target_pairs={{0,4},{1,5},{2,6},{3,7},{16,20},{17,21},{18,22},{19,23}} | collective-permute-start | bytes 786440 | tf_op jit(solution)/shard_map/ppermute | solution.py:353
  27.6 4.3 %copy-start = (f32[2,256,256]{2,1,0:T(8,128)}, f32[2,256,256]{2,1,0:T(8,128)S(1)}, u32[]{:S(2)}) copy-start(f32[2,256,256]{2,1,0:T(8,128)S(1)} %multiply_multiply_fusion.inner_ref) | copy-start | bytes 1572868
  27.6 11.1 %collective-permute-start.7 = (bf16[512,256]{1,0:T(8,128)(2,1)S(1)}, bf16[512,256]{1,0:T(8,128)(2,1)S(1)}, u32[]{:S(2)}, u32[]{:S(2)}) collective-permute-start(bf16[512,256]{1,0:T(8,128)(2,1)S(1)} %get-tuple-element.98), channel_id=1, source_target_pairs={{0,3},{1,2},{2,1},{3,0},{4,7},{5,6},{6,5},{7,4},{8,11},{9,10},{10,... | collective-permute-start | bytes 786440 | tf_op jit(solution)/shard_map/ppermute | solution.py:35
  29.6 16.6 %collective-permute-start.8 = (bf16[512,256]{1,0:T(8,128)(2,1)S(1)}, bf16[512,256]{1,0:T(8,128)(2,1)S(1)}, u32[]{:S(2)}, u32[]{:S(2)}) collective-permute-start(bf16[512,256]{1,0:T(8,128)(2,1)S(1)} %get-tuple-element.98), channel_id=1, source_target_pairs={{0,1},{1,0},{2,3},{3,2},{4,5},{5,4},{6,7},{7,6},{8,9},{9,8},{10,11... | collective-permute-start | bytes 786440 | tf_op jit(solution)/shard_map/ppermute | solution.py:35
  31.2 21.3 %collective-permute-start.9 = (bf16[512,256]{1,0:T(8,128)(2,1)}, bf16[512,256]{1,0:T(8,128)(2,1)}, u32[]{:S(2)}, u32[]{:S(2)}) collective-permute-start(bf16[512,256]{1,0:T(8,128)(2,1)} %collective-permute-done.2.rest_0_), channel_id=1, source_target_pairs={{0,1},{1,0},{2,3},{3,2},{4,5},{5,4},{6,7},{7,6},{8,9},{9,8},{10,11... | collective-permute-start | bytes 786440 | tf_op jit(solution)/shard_map/ppermute | solution.py:35
  31.9 0.8 copy-start.2
  38.7 14.6 %collective-permute-start.10 = (bf16[512,256]{1,0:T(8,128)(2,1)S(1)}, bf16[512,256]{1,0:T(8,128)(2,1)S(1)}, u32[]{:S(2)}, u32[]{:S(2)}) collective-permute-start(bf16[512,256]{1,0:T(8,128)(2,1)S(1)} %collective-permute-done.7.rest_1_), channel_id=1, source_target_pairs={{0,1},{1,0},{2,3},{3,2},{4,5},{5,4},{6,7},{7,6},{8,9},{9,8},{10,11... | collective-permute-start | bytes 786440 | tf_op jit(solution)/shard_map/ppermute | solution.py:35
  46.2 19.1 %collective-permute-start.11 = (f16[272,1024]{1,0:T(8,128)(2,1)}, f16[272,1024]{1,0:T(8,128)(2,1)}, u32[]{:S(2)}, u32[]{:S(2)}) collective-permute-start(f16[272,1024]{1,0:T(8,128)(2,1)} %convert_element_type.24), channel_id=1, source_target_pairs={{0,1},{1,0},{2,3},{3,2},{4,5},{5,4},{6,7},{7,6},{8,9},{9,8},{10,11... | collective-permute-start | bytes 1671176 | tf_op jit(solution)/shard_map/ppermute | solution.py:35
  50.5 35.4 %collective-permute-start.18 = (f16[272,1024]{1,0:T(8,128)(2,1)S(1)}, f16[272,1024]{1,0:T(8,128)(2,1)S(1)}, u32[]{:S(2)}, u32[]{:S(2)}) collective-permute-start(f16[272,1024]{1,0:T(8,128)(2,1)S(1)} %convert_element_type.25), channel_id=1, source_target_pairs={{0,1},{1,0},{2,3},{3,2},{4,5},{5,4},{6,7},{7,6},{8,9},{9,8},{10,11... | collective-permute-start | bytes 1671176 | tf_op jit(solution)/shard_map/ppermute | solution.py:35
  53.2 4.2 %copy-start.1 = (f32[2,256,256]{2,1,0:T(8,128)S(1)}, f32[2,256,256]{2,1,0:T(8,128)}, u32[]{:S(2)}) copy-start(f32[2,256,256]{2,1,0:T(8,128)} %copy-done) | copy-start | bytes 1572868
  53.2 4.2 %copy-start.3 = (bf16[512,256]{1,0:T(8,128)(2,1)S(1)}, bf16[512,256]{1,0:T(8,128)(2,1)}, u32[]{:S(2)}) copy-start(bf16[512,256]{1,0:T(8,128)(2,1)} %copy-done.2) | copy-start | bytes 786436
  59.7 1.9 %collective-permute-start.12 = (f32[200,256]{1,0:T(8,128)S(1)}, f32[200,256]{1,0:T(8,128)S(1)}, u32[]{:S(2)}, u32[]{:S(2)}) collective-permute-start(f32[200,256]{1,0:T(8,128)S(1)} %get-tuple-element.68), channel_id=1, source_target_pairs={{0,4},{4,0},{8,12},{12,8},{1,5},{5,1},{9,13},{13,9},{2,6},{6,2},{1... | collective-permute-start | bytes 614408 | tf_op jit(solution)/shard_map/ppermute | solution.py:35
  59.7 10.1 %collective-permute-start.13 = (f32[200,256]{1,0:T(8,128)S(1)}, f32[200,256]{1,0:T(8,128)S(1)}, u32[]{:S(2)}, u32[]{:S(2)}) collective-permute-start(f32[200,256]{1,0:T(8,128)S(1)} %get-tuple-element.70), channel_id=1, source_target_pairs={{0,8},{4,12},{8,0},{12,4},{1,9},{5,13},{9,1},{13,5},{2,10},{6,14},... | collective-permute-start | bytes 614408 | tf_op jit(solution)/shard_map/ppermute | solution.py:35
  59.9 11.3 %collective-permute-start.14 = (f32[200,256]{1,0:T(8,128)S(1)}, f32[200,256]{1,0:T(8,128)S(1)}, u32[]{:S(2)}, u32[]{:S(2)}) collective-permute-start(f32[200,256]{1,0:T(8,128)S(1)} %get-tuple-element.71), channel_id=1, source_target_pairs={{0,12},{4,8},{8,4},{12,0},{1,13},{5,9},{9,5},{13,1},{2,14},{6,10},... | collective-permute-start | bytes 614408 | tf_op jit(solution)/shard_map/ppermute | solution.py:35
  67.0 24.0 %collective-permute-start.19 = (f16[272,512]{1,0:T(8,128)(2,1)S(1)}, f16[272,512]{1,0:T(8,128)(2,1)S(1)}, u32[]{:S(2)}, u32[]{:S(2)}) collective-permute-start(f16[272,512]{1,0:T(8,128)(2,1)S(1)} %convert_element_type.27), channel_id=1, source_target_pairs={{0,2},{1,3},{2,0},{3,1},{4,6},{5,7},{6,4},{7,5},{8,10},{9,11},{10,... | collective-permute-start | bytes 835592 | tf_op jit(solution)/shard_map/ppermute | solution.py:35
  71.2 16.2 %collective-permute-start.15 = (f32[96,256]{1,0:T(8,128)S(1)}, f32[96,256]{1,0:T(8,128)S(1)}, u32[]{:S(2)}, u32[]{:S(2)}) collective-permute-start(f32[96,256]{1,0:T(8,128)S(1)} %get-tuple-element.79), channel_id=1, source_target_pairs={{0,1},{1,0},{2,3},{3,2},{4,5},{5,4},{6,7},{7,6},{8,9},{9,8},{10,11... | collective-permute-start | bytes 294920 | tf_op jit(solution)/shard_map/ppermute | solution.py:35
  73.8 13.6 %collective-permute-start.16 = (f32[96,256]{1,0:T(8,128)S(1)}, f32[96,256]{1,0:T(8,128)S(1)}, u32[]{:S(2)}, u32[]{:S(2)}) collective-permute-start(f32[96,256]{1,0:T(8,128)S(1)} %get-tuple-element.80), channel_id=1, source_target_pairs={{0,2},{1,3},{2,0},{3,1},{4,6},{5,7},{6,4},{7,5},{8,10},{9,11},{10,... | collective-permute-start | bytes 294920 | tf_op jit(solution)/shard_map/ppermute | solution.py:35
  74.6 16.4 %collective-permute-start.17 = (f32[96,256]{1,0:T(8,128)S(1)}, f32[96,256]{1,0:T(8,128)S(1)}, u32[]{:S(2)}, u32[]{:S(2)}) collective-permute-start(f32[96,256]{1,0:T(8,128)S(1)} %get-tuple-element.81), channel_id=1, source_target_pairs={{0,3},{1,2},{2,1},{3,0},{4,7},{5,6},{6,5},{7,4},{8,11},{9,10},{10,... | collective-permute-start | bytes 294920 | tf_op jit(solution)/shard_map/ppermute | solution.py:35
  85.9 15.7 %collective-permute-start.23 = (f16[272,512]{1,0:T(8,128)(2,1)S(1)}, f16[272,512]{1,0:T(8,128)(2,1)S(1)}, u32[]{:S(2)}, u32[]{:S(2)}) collective-permute-start(f16[272,512]{1,0:T(8,128)(2,1)S(1)} %convert_element_type.30), channel_id=1, source_target_pairs={{0,2},{1,3},{2,0},{3,1},{4,6},{5,7},{6,4},{7,5},{8,10},{9,11},{10,... | collective-permute-start | bytes 835592 | tf_op jit(solution)/shard_map/ppermute | solution.py:35
  91.0 12.1 %collective-permute-start.20 = (f32[96,256]{1,0:T(8,128)S(1)}, f32[96,256]{1,0:T(8,128)S(1)}, u32[]{:S(2)}, u32[]{:S(2)}) collective-permute-start(f32[96,256]{1,0:T(8,128)S(1)} %add_add_fusion.rest_0_), channel_id=1, source_target_pairs={{0,4},{4,0},{8,12},{12,8},{1,5},{5,1},{9,13},{13,9},{2,6},{6,2},{1... | collective-permute-start | bytes 294920 | tf_op jit(solution)/shard_map/ppermute | solution.py:35
  91.0 12.0 %collective-permute-start.21 = (f32[96,256]{1,0:T(8,128)S(1)}, f32[96,256]{1,0:T(8,128)S(1)}, u32[]{:S(2)}, u32[]{:S(2)}) collective-permute-start(f32[96,256]{1,0:T(8,128)S(1)} %add_add_fusion.rest_0_), channel_id=1, source_target_pairs={{0,8},{4,12},{8,0},{12,4},{1,9},{5,13},{9,1},{13,5},{2,10},{6,14},... | collective-permute-start | bytes 294920 | tf_op jit(solution)/shard_map/ppermute | solution.py:35
  91.1 12.0 %collective-permute-start.22 = (f32[96,256]{1,0:T(8,128)S(1)}, f32[96,256]{1,0:T(8,128)S(1)}, u32[]{:S(2)}, u32[]{:S(2)}) collective-permute-start(f32[96,256]{1,0:T(8,128)S(1)} %add_add_fusion.rest_0_), channel_id=1, source_target_pairs={{0,12},{4,8},{8,4},{12,0},{1,13},{5,9},{9,5},{13,1},{2,14},{6,10},... | collective-permute-start | bytes 294920 | tf_op jit(solution)/shard_map/ppermute | solution.py:35
